TPU v7x, 512 devices: a whole 4x8x8 slice. The times are simulated.
512 devices in a mesh: dp: 2 (over z_lo), row: 8 (over x, core), col: 32 (over y, z_hi).
Axes of the slice: x: 4, y: 8, z: 8 (z_hi: 4, z_lo: 2; z = z_hi * 2 + z_lo), core: 2. Of those that a mesh axis runs over, the one named last changes fastest.
Arguments:
- features: bfloat16 [2, 64, 64, 16, 256], P('dp', 'col', 'row'), may hold values from -10.5 to 10.5
- w_qkv: bfloat16 [256, 768], replicated, may hold values from -0.375 to 0.375
- w_out: bfloat16 [256, 256], replicated, may hold values from -0.375 to 0.375
- cotangent: bfloat16 [2, 64, 64, 16, 256], P('dp', 'col', 'row'), may hold values from -6 to 6
Outputs:
- update: bfloat16 [2, 64, 64, 16, 256], P('dp', 'col', 'row')
- grad_in: bfloat16 [2, 64, 64, 16, 256], P('dp', 'col', 'row')
- grad_qkv: float32 [256, 768], replicated
- grad_out: float32 [256, 256], replicated
All inputs are finite; a program needn't handle non-finite values.
Results may differ from a plain program's by a relative error of at most 0.017.
The roundings to bfloat16 on the way count: a program that leaves them out, or rounds other values in their place, can miss the bound.
Values may be sent and summed in bfloat16 or wider, within the bound.
No kernel may reach another device: no remote copies, remote signals or barrier semaphores. Data moves between devices by JAX's collectives and lax.ppermute only.
A program may use at most 64 MiB of HBM per device.

v0:
```python
import math

import jax
import jax.numpy as jnp
from jax import lax
from jax.sharding import PartitionSpec as P

HEADS = 8


def split_heads(line_block):
    leading = line_block.shape[:3]
    model_width = line_block.shape[3] // 3
    parts = line_block.reshape(leading + (3, HEADS, model_width // HEADS))
    return (parts[:, :, :, 0], parts[:, :, :, 1], parts[:, :, :, 2], model_width)


def weights_of(queries, key_heads):
    score_scale = 1.0 / math.sqrt(queries.shape[-1])
    scores = (
        jnp.einsum("albhd,ambhd->abhlm", queries, key_heads, preferred_element_type=jnp.float32)
        * score_scale
    )
    return jax.nn.softmax(scores, axis=-1)


def attend(line_block):
    queries, key_heads, values, model_width = split_heads(line_block)
    rounded = weights_of(queries, key_heads).astype(jnp.bfloat16)
    mixed = jnp.einsum("abhlm,ambhd->albhd", rounded, values, preferred_element_type=jnp.float32)
    return mixed.reshape(line_block.shape[:3] + (model_width,)).astype(jnp.bfloat16)


def attend_back(line_block, upstream):
    queries, key_heads, values, model_width = split_heads(line_block)
    score_scale = 1.0 / math.sqrt(queries.shape[-1])
    weights_full = weights_of(queries, key_heads)
    rounded = weights_full.astype(jnp.bfloat16)
    upstream_heads = upstream.reshape(queries.shape)
    dprobs = jnp.einsum(
        "albhd,ambhd->abhlm", upstream_heads, values, preferred_element_type=jnp.float32
    )
    dvalues = jnp.einsum(
        "abhlm,albhd->ambhd", rounded, upstream_heads, preferred_element_type=jnp.float32
    )
    dscores = (
        weights_full
        * (dprobs - jnp.sum(dprobs * weights_full, axis=-1, keepdims=True))
        * score_scale
    )
    dround = dscores.astype(jnp.bfloat16)
    dqueries = jnp.einsum(
        "abhlm,ambhd->albhd", dround, key_heads, preferred_element_type=jnp.float32
    )
    dkeys = jnp.einsum("abhlm,albhd->ambhd", dround, queries, preferred_element_type=jnp.float32)
    stacked = jnp.stack([dqueries, dkeys, dvalues], axis=3)
    return stacked.reshape(line_block.shape[:3] + (3 * model_width,)).astype(jnp.bfloat16)


def project(rows_in, w_qkv):
    return jnp.dot(rows_in, w_qkv, preferred_element_type=jnp.float32).astype(jnp.bfloat16)


def input_grad(dproj_rows, w_qkv):
    return jnp.einsum("tk,ck->tc", dproj_rows, w_qkv, preferred_element_type=jnp.float32).astype(
        jnp.bfloat16
    )


def widened(rounded_term):
    return lax.optimization_barrier(rounded_term).astype(jnp.float32)


def weight_term(rows_in, dproj_rows):
    return jnp.einsum("tc,tk->ck", rows_in, dproj_rows, preferred_element_type=jnp.float32)


def body(features, w_qkv, w_out, cotangent):
    local_shape = features.shape
    y_local, x_local, z_local, model_width = local_shape[1:]
    triple = 3 * model_width
    col_count = lax.axis_size("col")
    row_count = lax.axis_size("row")
    y_full = y_local * col_count
    x_full = x_local * row_count
    y_batch = x_local * z_local // col_count
    feat_rows = features.reshape(-1, model_width)
    proj_local = project(feat_rows, w_qkv)
    proj_z = proj_local.reshape(y_local * x_local, z_local, 1, triple)
    out_z = attend(proj_z)
    proj_y = lax.all_to_all(
        proj_local.reshape(y_local, x_local * z_local, triple),
        "col",
        split_axis=1,
        concat_axis=0,
        tiled=True,
    )
    proj_x = lax.all_to_all(
        proj_local.reshape(y_local, x_local, z_local, triple),
        "row",
        split_axis=2,
        concat_axis=1,
        tiled=True,
    )
    proj_y = proj_y.reshape(1, y_full, y_batch, triple)
    out_y = lax.all_to_all(
        attend(proj_y).reshape(y_full, y_batch, model_width),
        "col",
        split_axis=0,
        concat_axis=1,
        tiled=True,
    )
    out_x = lax.all_to_all(attend(proj_x), "row", split_axis=1, concat_axis=2, tiled=True)
    mix = (
        out_z.reshape(-1, model_width).astype(jnp.float32)
        + out_y.reshape(-1, model_width).astype(jnp.float32)
        + out_x.reshape(-1, model_width).astype(jnp.float32)
    ).astype(jnp.bfloat16)
    update = (
        jnp.dot(mix, w_out, preferred_element_type=jnp.float32)
        .astype(jnp.bfloat16)
        .reshape(local_shape)
    )
    grad_rows = cotangent.reshape(-1, model_width)
    out_term = jnp.einsum("tc,td->cd", mix, grad_rows, preferred_element_type=jnp.float32)
    grad_mix = jnp.einsum("td,cd->tc", grad_rows, w_out, preferred_element_type=jnp.float32).astype(
        jnp.bfloat16
    )
    dproj_z = attend_back(proj_z, grad_mix.reshape(y_local * x_local, z_local, 1, model_width))
    grad_y = lax.all_to_all(
        grad_mix.reshape(y_local, x_local * z_local, model_width),
        "col",
        split_axis=1,
        concat_axis=0,
        tiled=True,
    )
    grad_x = lax.all_to_all(
        grad_mix.reshape(y_local, x_local, z_local, model_width),
        "row",
        split_axis=2,
        concat_axis=1,
        tiled=True,
    )
    dproj_y = attend_back(proj_y, grad_y.reshape(1, y_full, y_batch, model_width))
    dproj_x = attend_back(proj_x, grad_x)
    z_rows = dproj_z.reshape(-1, triple)
    input_total = widened(input_grad(z_rows, w_qkv))
    qkv_term = weight_term(feat_rows, z_rows)
    back_y = lax.all_to_all(
        dproj_y.reshape(y_full, y_batch, triple), "col", split_axis=0, concat_axis=1, tiled=True
    ).reshape(-1, triple)
    back_x = lax.all_to_all(dproj_x, "row", split_axis=1, concat_axis=2, tiled=True).reshape(
        -1, triple
    )
    input_total = (
        input_total + widened(input_grad(back_y, w_qkv)) + widened(input_grad(back_x, w_qkv))
    )
    qkv_term = qkv_term + weight_term(feat_rows, back_y) + weight_term(feat_rows, back_x)
    grad_in = input_total.astype(jnp.bfloat16).reshape(local_shape)
    token_total = lax.axis_size("dp") * y_full * x_full * z_local
    factor = 1.0 / math.sqrt(token_total)
    qkv_sum, out_sum = lax.psum((qkv_term, out_term), ("dp", "row", "col"))
    return (update, grad_in, qkv_sum * factor, out_sum * factor)


def solution(mesh):
    placed = (P("dp", "col", "row", None, None), P(), P(), P("dp", "col", "row", None, None))
    return jax.shard_map(
        body,
        mesh=mesh,
        in_specs=placed,
        out_specs=(P("dp", "col", "row", None, None), P("dp", "col", "row", None, None), P(), P()),
        check_vma=False,
    )
```

profile of v0, /device:TPU:1, one launch (start us, length us, event | category | flops | bytes accessed | tf_op | source)
XLA Modules:
  0.0 452.1 jit_solution(14585558989022820217)
XLA Ops:
  9.1 10.2 %all-to-all-start.6 = ((bf16[2,8,16,256]{3,1,0,2:T(8,128)(2,1)}), bf16[2,8,16,256]{3,1,0,2:T(8,128)(2,1)S(1)}, u32[]{:S(2)}, u32[]{:S(2)}) async-start(bf16[2,8,16,256]{3,1,0,2:T(8,128)(2,1)} %copy.155), calls=%async_computation.6 | async-start | bytes 262144 | tf_op jit(solution)/shard_map/all_to_all | solution.py:137
  21.5 1.5 fusion.114
  23.0 3.0 fusion.121
  27.1 4.8 %all-to-all-start.2 = ((bf16[2,8,16,768]{3,1,0,2:T(8,128)(2,1)}), bf16[2,8,16,768]{3,1,0,2:T(8,128)(2,1)S(1)}, u32[]{:S(2)}, u32[]{:S(2)}) async-start(bf16[2,8,16,768]{3,1,0,2:T(8,128)(2,1)} %copy.131), calls=%async_computation.2 | async-start | bytes 786432 | tf_op jit(solution)/shard_map/all_to_all | solution.py:98
  31.9 2.4 convolution_bitcast_fusion
  35.2 1.4 fusion.56
  37.8 2.2 all-to-all-done.2
  40.0 11.3 %all-to-all-start.4 = ((bf16[2,128,256]{2,0,1:T(2,128)(2,1)}), bf16[2,128,256]{2,0,1:T(2,128)(2,1)S(1)}, u32[]{:S(2)}, u32[]{:S(2)}) async-start(bf16[2,128,256]{2,0,1:T(2,128)(2,1)} %copy.145), calls=%async_computation.4 | async-start | bytes 262144 | tf_op jit(solution)/shard_map/all_to_all | solution.py:130
  55.6 1.5 fusion.116
  58.7 2.0 fusion.31
  60.6 2.0 fusion.32
  63.4 1.6 fusion.33
  65.1 4.4 all-to-all-start.3
  71.0 3.8 all-to-all-done.3
  74.8 4.2 all-to-all-start.7
  79.1 3.2 convolution_bitcast_fusion.2
  82.2 3.0 convolution_bitcast_fusion.1
  85.2 1.7 maximum_convert_fusion
  89.6 12.0 %all-to-all-start = ((bf16[2,128,768]{2,0,1:T(2,128)(2,1)}), bf16[2,128,768]{2,0,1:T(2,128)(2,1)S(1)}, u32[]{:S(2)}, u32[]{:S(2)}) async-start(bf16[2,128,768]{2,0,1:T(2,128)(2,1)} %copy.123), calls=%async_computation | async-start | bytes 786432 | tf_op jit(solution)/shard_map/all_to_all | solution.py:91
  108.4 8.1 %all-to-all-done = bf16[2,128,768]{2,0,1:T(2,128)(2,1)S(1)} async-done(((bf16[2,128,768]{2,0,1:T(2,128)(2,1)}), bf16[2,128,768]{2,0,1:T(2,128)(2,1)S(1)}, u32[]{:S(2)}, u32[]{:S(2)}) %all-to-all-start) | async-done | bytes 393248 | tf_op jit(solution)/shard_map/all_to_all | solution.py:91
  119.0 1.6 copy.189
  120.6 1.6 copy.190
  122.9 1.5 fusion.122
  127.8 2.7 fusion.28
  131.3 6.5 %all-to-all-start.1 = ((bf16[64,4,256]{2,1,0:T(4,128)(2,1)}), bf16[64,4,256]{2,1,0:T(4,128)(2,1)S(1)}, u32[]{:S(2)}, u32[]{:S(2)}) async-start(bf16[64,4,256]{2,1,0:T(4,128)(2,1)} %copy.129), calls=%async_computation.1 | async-start | bytes 262144 | tf_op jit(solution)/shard_map/all_to_all | solution.py:106
  137.7 2.8 fusion.29
  142.9 6.3 %all-to-all-done.1 = bf16[64,4,256]{2,1,0:T(4,128)(2,1)S(1)} async-done(((bf16[64,4,256]{2,1,0:T(4,128)(2,1)}), bf16[64,4,256]{2,1,0:T(4,128)(2,1)S(1)}, u32[]{:S(2)}, u32[]{:S(2)}) %all-to-all-start.1) | async-done | bytes 131104 | tf_op jit(solution)/shard_map/all_to_all | solution.py:106
  149.1 5.4 %all-to-all-start.5 = ((bf16[64,4,768]{2,1,0:T(4,128)(2,1)}), bf16[64,4,768]{2,1,0:T(4,128)(2,1)S(1)}, u32[]{:S(2)}, u32[]{:S(2)}) async-start(bf16[64,4,768]{2,1,0:T(4,128)(2,1)} %copy.153), calls=%async_computation.5 | async-start | bytes 786432 | tf_op jit(solution)/shard_map/all_to_all | solution.py:149
  156.7 3.8 fusion.34
  161.7 1.6 copy.122
  165.3 2.9 all-to-all-done.5
  171.9 270.2 %all-reduce.3.cloned.1.call-done = (f32[256,768]{0,1:T(8,128)}, f32[256,256]{1,0:T(8,128)}) async-done(((f32[256,768]{0,1:T(8,128)}, f32[256,256]{1,0:T(8,128)}), (f32[256,768]{0,1:T(8,128)}, f32[256,256]{1,0:T(8,128)})) %all-reduce.3.cloned.1.call-update) | async-done | bytes 1048592 | tf_op jit(solution)/shard_map/psum | solution.py:162
  (137 shorter events, 46.3 us)
Async XLA Ops:
  7.2 12.1 %copy-start = (bf16[256,768]{1,0:T(8,128)(2,1)S(1)}, bf16[256,768]{1,0:T(8,128)(2,1)}, u32[]{:S(2)}) copy-start(bf16[256,768]{1,0:T(8,128)(2,1)} %param.5) | copy-start | bytes 1179652
  9.1 18.0 %all-to-all-start.6 = ((bf16[2,8,16,256]{3,1,0,2:T(8,128)(2,1)}), bf16[2,8,16,256]{3,1,0,2:T(8,128)(2,1)S(1)}, u32[]{:S(2)}, u32[]{:S(2)}) async-start(bf16[2,8,16,256]{3,1,0,2:T(8,128)(2,1)} %copy.155), calls=%async_computation.6 | async-start | bytes 262144 | tf_op jit(solution)/shard_map/all_to_all | solution.py:137
  23.0 12.2 %copy-start.4 = (bf16[16,16,1,1,8,32]{5,4,3,1,0,2:T(8,128)(2,1)}, bf16[16,16,1,1,8,32]{5,4,3,1,0,2:T(8,128)(2,1)S(1)}, u32[]{:S(2)}) copy-start(bf16[16,16,1,1,8,32]{5,4,3,1,0,2:T(8,128)(2,1)S(1)} %get-tuple-element.27) | copy-start | bytes 393220
  26.0 8.4 %copy-start.27 = (f32[16,8,16]{2,1,0:T(8,128)}, f32[16,8,16]{2,1,0:T(8,128)S(1)}, u32[]{:S(2)}) copy-start(f32[16,8,16]{2,1,0:T(8,128)S(1)} %get-tuple-element.33) | copy-start | bytes 24580
  27.1 12.9 %all-to-all-start.2 = ((bf16[2,8,16,768]{3,1,0,2:T(8,128)(2,1)}), bf16[2,8,16,768]{3,1,0,2:T(8,128)(2,1)S(1)}, u32[]{:S(2)}, u32[]{:S(2)}) async-start(bf16[2,8,16,768]{3,1,0,2:T(8,128)(2,1)} %copy.131), calls=%async_computation.2 | async-start | bytes 786432 | tf_op jit(solution)/shard_map/all_to_all | solution.py:98
  40.0 25.0 %all-to-all-start.4 = ((bf16[2,128,256]{2,0,1:T(2,128)(2,1)}), bf16[2,128,256]{2,0,1:T(2,128)(2,1)S(1)}, u32[]{:S(2)}, u32[]{:S(2)}) async-start(bf16[2,128,256]{2,0,1:T(2,128)(2,1)} %copy.145), calls=%async_computation.4 | async-start | bytes 262144 | tf_op jit(solution)/shard_map/all_to_all | solution.py:130
  54.9 2.2 copy-start.8
  65.1 4.8 %copy-start.17 = (bf16[2,128,256]{2,0,1:T(2,128)(2,1)}, bf16[2,128,256]{2,0,1:T(2,128)(2,1)S(1)}, u32[]{:S(2)}) copy-start(bf16[2,128,256]{2,0,1:T(2,128)(2,1)S(1)} %all-to-all-done.4) | copy-start | bytes 393220
  65.1 9.7 %all-to-all-start.3 = ((bf16[2,64,2,256]{3,2,0,1:T(2,128)(2,1)}), bf16[2,64,2,256]{3,2,0,1:T(2,128)(2,1)S(1)}, u32[]{:S(2)}, u32[]{:S(2)}) async-start(bf16[2,64,2,256]{3,2,0,1:T(2,128)(2,1)} %copy.138), calls=%async_computation.3 | async-start | bytes 262144 | tf_op jit(solution)/shard_map/all_to_all | solution.py:113
  69.7 9.3 %copy-start.6 = (f32[16,8,16,16]{2,3,1,0:T(8,128)S(1)}, f32[16,8,16,16]{2,3,1,0:T(8,128)}, u32[]{:S(2)}) copy-start(f32[16,8,16,16]{2,3,1,0:T(8,128)} %fusion.56) | copy-start | bytes 393220
  69.7 9.3 %copy-start.28 = (f32[16,8,16]{2,1,0:T(8,128)S(1)}, f32[16,8,16]{2,1,0:T(8,128)}, u32[]{:S(2)}) copy-start(f32[16,8,16]{2,1,0:T(8,128)} %copy-done.27) | copy-start | bytes 24580
  74.8 7.4 %copy-start.12 = (bf16[2,64,2,256]{3,2,0,1:T(2,128)(2,1)}, bf16[2,64,2,256]{3,2,0,1:T(2,128)(2,1)S(1)}, u32[]{:S(2)}) copy-start(bf16[2,64,2,256]{3,2,0,1:T(2,128)(2,1)S(1)} %all-to-all-done.3) | copy-start | bytes 393220
  74.8 14.7 %all-to-all-start.7 = ((bf16[2,64,2,768]{3,2,0,1:T(2,128)(2,1)}), bf16[2,64,2,768]{3,2,0,1:T(2,128)(2,1)S(1)}, u32[]{:S(2)}, u32[]{:S(2)}) async-start(bf16[2,64,2,768]{3,2,0,1:T(2,128)(2,1)} %copy.164), calls=%async_computation.7 | async-start | bytes 786432 | tf_op jit(solution)/shard_map/all_to_all | solution.py:152
  79.0 3.2 copy-start.20
  88.4 14.2 %copy-start.1 = (bf16[1,2,8,16,256]{4,3,2,1,0:T(8,128)(2,1)S(1)}, bf16[1,2,8,16,256]{4,3,2,1,0:T(8,128)(2,1)}, u32[]{:S(2)}) copy-start(bf16[1,2,8,16,256]{4,3,2,1,0:T(8,128)(2,1)} %param.4) | copy-start | bytes 393220
  89.6 13.3 %copy-start.18 = (bf16[2,128,256]{2,0,1:T(2,128)(2,1)S(1)}, bf16[2,128,256]{2,0,1:T(2,128)(2,1)}, u32[]{:S(2)}) copy-start(bf16[2,128,256]{2,0,1:T(2,128)(2,1)} %copy-done.17) | copy-start | bytes 393220
  89.6 27.0 %all-to-all-start = ((bf16[2,128,768]{2,0,1:T(2,128)(2,1)}), bf16[2,128,768]{2,0,1:T(2,128)(2,1)S(1)}, u32[]{:S(2)}, u32[]{:S(2)}) async-start(bf16[2,128,768]{2,0,1:T(2,128)(2,1)} %copy.123), calls=%async_computation | async-start | bytes 786432 | tf_op jit(solution)/shard_map/all_to_all | solution.py:91
  102.5 1.9 copy-start.13
  119.0 3.3 copy-start.3
  120.6 3.8 copy-start.7
  127.8 2.7 copy-start.24
  131.3 17.9 %all-to-all-start.1 = ((bf16[64,4,256]{2,1,0:T(4,128)(2,1)}), bf16[64,4,256]{2,1,0:T(4,128)(2,1)S(1)}, u32[]{:S(2)}, u32[]{:S(2)}) async-start(bf16[64,4,256]{2,1,0:T(4,128)(2,1)} %copy.129), calls=%async_computation.1 | async-start | bytes 262144 | tf_op jit(solution)/shard_map/all_to_all | solution.py:106
  137.7 2.8 copy-start.26
  149.1 19.1 %all-to-all-start.5 = ((bf16[64,4,768]{2,1,0:T(4,128)(2,1)}), bf16[64,4,768]{2,1,0:T(4,128)(2,1)S(1)}, u32[]{:S(2)}, u32[]{:S(2)}) async-start(bf16[64,4,768]{2,1,0:T(4,128)(2,1)} %copy.153), calls=%async_computation.5 | async-start | bytes 786432 | tf_op jit(solution)/shard_map/all_to_all | solution.py:149
  154.5 2.2 copy-start.5
  154.5 2.2 copy-start.29
  154.5 287.6 %all-reduce.3.cloned.1.call-start = ((), (), s32[]{:S(2)}) async-start(), calls=%async_computation.8 | async-start | bytes 2097152 | tf_op jit(solution)/shard_map/psum | solution.py:162
  161.7 2.6 copy-start.14
  161.7 2.6 copy-start.19
  163.3 5.1 %copy-start.2 = (bf16[1,2,8,16,256]{4,3,2,1,0:T(8,128)(2,1)S(1)}, bf16[1,2,8,16,256]{4,3,2,1,0:T(8,128)(2,1)}, u32[]{:S(2)}) copy-start(bf16[1,2,8,16,256]{4,3,2,1,0:T(8,128)(2,1)} %param.4) | copy-start | bytes 393220
  168.8 1.3 copy-start.9
  442.2 2.4 copy-start.25
  (9 other events, 10.4 us)
Sparse Core Ops, SparseCore 0:
  170.1 271.9 all-reduce.2
where the time goes:
time: 454 us; the launch traced here: 452 us
  waiting for transfers between devices  294 us (65%)
  starting transfers between devices  58.8 us (13%)
  matrix products  42.1 us (9%)
  local copies, waits for them, and re-layouts  37.2 us (8%)
  between operations  14.6 us (3%)
  other arithmetic  5.87 us (1%)
    psum x1, waiting for transfers between devices, body(): qkv_sum, out_sum = lax.psum((qkv_term, out_term), ('dp', 'row', 'col'))  270 us
    all_to_all x1, starting transfers between devices, body(): lax.all_to_all(proj_local.reshape(y_local, x_local * z_local, triple), 'c...  12 us
    all_to_all x1, starting transfers between devices, body(): lax.all_to_all(grad_mix.reshape(y_local, x_local * z_local, model_width),...  11.3 us
    all_to_all x1, starting transfers between devices, body(): lax.all_to_all(grad_mix.reshape(y_local, x_local, z_local, model_width),...  10.2 us
  transfers between devices with their start and end apart: 9, of which 6 were waited for; matrix products, arithmetic and copies ran while one was open for 14% of the time, Pallas kernels for 0%

commit v1 on v0

v1 whole, which is shorter than its diff:
```python
import functools
import math

import jax
import jax.numpy as jnp
from jax import lax
from jax.experimental import pallas as pl
from jax.experimental.pallas import tpu as pltpu
from jax.sharding import PartitionSpec as P

HEADS = 8
DEPTH = 32
C = 256
T = 256
PATCHES = 2
LINES = 4
NEG = -1e30

BF = jnp.bfloat16
F32 = jnp.float32


def nn(a, b):
    return lax.dot_general(a, b, (((1,), (0,)), ((), ())), preferred_element_type=F32)


def nt(a, b):
    return lax.dot_general(a, b, (((1,), (1,)), ((), ())), preferred_element_type=F32)


def iota(axis, shape=(T, T)):
    return lax.broadcasted_iota(jnp.int32, shape, axis)


def y_source(r):
    return ((r // LINES) % 2) * 128 + (r // 8) * LINES + r % LINES


def x_source(r):
    peer = r // 32
    return (peer // 4) * 128 + (r % 8) * 16 + (peer % 4) * LINES + (r // 8) % LINES


def z_line(r):
    return r // 16


def y_line(r):
    return r % LINES


def x_line(r):
    return (r // 8) % LINES


def onehot(hit):
    return jnp.where(hit, 1.0, 0.0).astype(BF)


def pack_body(feat, cot, send_x, send_y):
    for source, out in ((x_source, send_x), (y_source, send_y)):
        pick = onehot(source(iota(0)) == iota(1))
        out[:, :C] = nn(pick, feat[...]).astype(BF)
        out[:, C:] = nn(pick, cot[...]).astype(BF)


def axis_math(line, feat, cot, w_qkv, w_qkv_t, w_out):
    scale = 1.0 / math.sqrt(DEPTH)
    eye = onehot(iota(0) == iota(1))
    feat_t = nt(eye, feat).astype(BF)
    cot_t = nt(eye, cot).astype(BF)
    proj = nn(feat, w_qkv[...]).astype(BF)
    proj_t = nn(w_qkv_t[...], feat_t).astype(BF)
    gmix = nt(cot, w_out[...]).astype(BF)
    gmix_t = nn(w_out[...], cot_t).astype(BF)
    q, k, v = proj[:, :C], proj[:, C : 2 * C], proj[:, 2 * C :]
    q_t, k_t, v_t = proj_t[:C], proj_t[C : 2 * C], proj_t[2 * C :]
    bias = jnp.where(line(iota(0)) == line(iota(1)), 0.0, NEG)
    head_of_row = iota(0) // DEPTH
    head_of_lane = iota(1) // DEPTH
    zero = jnp.zeros((T, C), BF)
    out_t = []
    dq_t = []
    dk = jnp.zeros((T, C), F32)
    dv = jnp.zeros((T, C), F32)
    for h in range(HEADS):
        rows = slice(h * DEPTH, (h + 1) * DEPTH)
        on_row = head_of_row == h
        on_lane = head_of_lane == h
        scores = nn(k, jnp.where(on_row, q_t, zero)) + bias
        top = jnp.max(scores, axis=0, keepdims=True)
        e = jnp.exp((scores - top) * scale)
        probs = e * (1.0 / jnp.sum(e, axis=0, keepdims=True))
        rounded = probs.astype(BF)
        out_t.append(nn(v_t[rows], rounded))
        dv += nn(rounded, jnp.where(on_lane, gmix, zero))
        dprobs = nn(v, jnp.where(on_row, gmix_t, zero))
        mean = jnp.sum(dprobs * probs, axis=0, keepdims=True)
        dround = (probs * (dprobs - mean) * scale).astype(BF)
        dq_t.append(nn(k_t[rows], dround))
        dk += nn(dround, jnp.where(on_lane, q, zero))
    out_t = jnp.concatenate(out_t, axis=0).astype(BF)
    dq_t = jnp.concatenate(dq_t, axis=0).astype(BF)
    out = nt(eye, out_t).astype(BF)
    dq = nt(eye, dq_t).astype(BF)
    dk = dk.astype(BF)
    dv = dv.astype(BF)
    dfeat = (
        nn(dq, w_qkv_t[:C]) + nn(dk, w_qkv_t[C : 2 * C]) + nn(dv, w_qkv_t[2 * C :])
    ).astype(BF)
    return out, dfeat, (nn(feat_t, dq), nn(feat_t, dk), nn(feat_t, dv), nn(out_t, cot))


def z_body(feat, cot, w_qkv, w_qkv_t, w_out, back, grad):
    back[:, :C], back[:, C:], terms = axis_math(z_line, feat[...], cot[...], w_qkv, w_qkv_t, w_out)
    for at, term in enumerate(terms):
        grad[:, at * C : (at + 1) * C] = term


def x_body(got, w_qkv, w_qkv_t, w_out, grad_so_far, back, grad):
    back[:, :C], back[:, C:], terms = axis_math(
        x_line, got[:, :C], got[:, C:], w_qkv, w_qkv_t, w_out
    )
    for at, term in enumerate(terms):
        cols = slice(at * C, (at + 1) * C)
        grad[:, cols] = grad_so_far[:, cols] + term


def y_body(got, w_qkv, w_qkv_t, w_out, grad_so_far, back_x, back, send_row):
    back[:, :C], back[:, C:], terms = axis_math(
        y_line, got[:, :C], got[:, C:], w_qkv, w_qkv_t, w_out
    )
    send_row[:, : 2 * C] = back_x[...]
    for at, term in enumerate(terms):
        cols = slice(at * C, (at + 1) * C)
        send_row[:, 2 * C + at * C : 3 * C + at * C] = (grad_so_far[:, cols] + term).astype(BF)


def row_sum_body(got_row, back_y, send_col):
    send_col[:, : 2 * C] = back_y[...]
    total = jnp.zeros((32, 4 * C), F32)
    for peer in range(8):
        total += got_row[peer * 32 : (peer + 1) * 32, 2 * C :].astype(F32)
    tiles = jnp.concatenate([total[:, j * 128 : (j + 1) * 128] for j in range(8)], axis=0)
    r = iota(0)
    pick = onehot(iota(1) == (r % 8) * 32 + r // 8)
    send_col[:, 2 * C :] = nn(pick, tiles.astype(BF)).astype(BF)


def col_sum_body(got_col, send):
    total = jnp.zeros((8, 128), F32)
    for peer in range(32):
        total += got_col[peer * 8 : (peer + 1) * 8, 2 * C :].astype(F32)
    send[...] = jnp.concatenate([total] * 64, axis=0).astype(BF)


def dp_sum_body(factor, got, send):
    total = ((got[:256].astype(F32) + got[256:].astype(F32)) * factor).astype(BF)
    r = iota(0)
    pick = onehot(iota(1) == (r % 32) * 8 + r // 32)
    tiles = nn(pick, total)
    rows = jnp.concatenate([tiles[j * 32 : (j + 1) * 32] for j in range(8)], axis=1).astype(BF)
    for peer in range(8):
        send[peer * 32 : (peer + 1) * 32] = rows


def final_body(back_z, back_y, back_x, w_out, update, grad_in):
    put_y = onehot(iota(0) == y_source(iota(1)))
    put_x = onehot(iota(0) == x_source(iota(1)))
    total = (
        back_z[...].astype(F32) + nn(put_y, back_y[:, : 2 * C]) + nn(put_x, back_x[:, : 2 * C])
    ).astype(BF)
    update[...] = nn(total[:, :C], w_out[...]).astype(BF)
    grad_in[...] = total[:, C:]


def call(body, outs, flops, *args):
    vmem = pl.BlockSpec(memory_space=pltpu.VMEM)
    return pl.pallas_call(
        body,
        out_shape=outs,
        in_specs=[vmem] * len(args),
        out_specs=[vmem] * len(outs),
        compiler_params=pltpu.CompilerParams(vmem_limit_bytes=40 * 2**20),
        cost_estimate=pl.CostEstimate(flops=flops, bytes_accessed=2**20, transcendentals=2**19),
    )(*args)


def shape(rows, cols, dtype):
    return jax.ShapeDtypeStruct((rows, cols), dtype)


def exchange(rows, axis):
    return lax.all_to_all(rows, axis, split_axis=0, concat_axis=0, tiled=True)


def body(features, w_qkv, w_out, cotangent):
    local_shape = features.shape
    feat = features.reshape(T, C)
    cot = cotangent.reshape(T, C)
    weights = (w_qkv, w_qkv.T, w_out)
    cube = 2 * T * T * C
    back_shape = shape(T, 2 * C, BF)
    grad_shape = shape(C, 4 * C, F32)
    send_x, send_y = call(pack_body, [back_shape] * 2, cube * 4, feat, cot)
    got_x = exchange(send_x, "row")
    back_z, grad = call(z_body, [back_shape, grad_shape], cube * 70, feat, cot, *weights)
    got_y = exchange(send_y, "col")
    back_x, grad = call(x_body, [back_shape, grad_shape], cube * 70, got_x, *weights, grad)
    back_y, send_row = call(
        y_body, [back_shape, shape(T, 6 * C, BF)], cube * 70, got_y, *weights, grad, back_x
    )
    got_row = exchange(send_row, "row")
    (send_col,) = call(row_sum_body, [shape(T, 2 * C + 128, BF)], cube, got_row, back_y)
    got_col = exchange(send_col, "col")
    (send_rest,) = call(col_sum_body, [shape(512, 128, BF)], 2**20, got_col)
    got_rest = exchange(send_rest, ("dp", "col"))
    update, grad_in = call(
        final_body, [shape(T, C, BF)] * 2, cube * 6, back_z, got_col, got_row, w_out
    )
    factor = 1.0 / math.sqrt(PATCHES * 64 * 64 * 16)
    (send_last,) = call(
        functools.partial(dp_sum_body, factor), [shape(C, 4 * C, BF)], cube, got_rest
    )
    whole = exchange(send_last, "row")
    return (
        update.reshape(local_shape),
        grad_in.reshape(local_shape),
        whole[:, : 3 * C].astype(F32),
        whole[:, 3 * C :].astype(F32),
    )


def solution(mesh):
    placed = (P("dp", "col", "row", None, None), P(), P(), P("dp", "col", "row", None, None))
    return jax.shard_map(
        body,
        mesh=mesh,
        in_specs=placed,
        out_specs=(P("dp", "col", "row", None, None), P("dp", "col", "row", None, None), P(), P()),
        check_vma=False,
    )
```

time: 454 us -> 128 us (0.28)
  waiting for transfers between devices: 294 us -> 8.43 us
  blocking collectives: 0 us -> 74.5 us
  matrix products: 42.1 us -> 0 us
  starting transfers between devices: 58.8 us -> 18.5 us
  local copies, waits for them, and re-layouts: 37.2 us -> 2.82 us
  Pallas kernels: 0 us -> 20.5 us
  between operations: 14.6 us -> 0.72 us
    psum x1 -> x0, waiting for transfers between devices: 270 us -> none  [body(): qkv_sum, out_sum = lax.psum((qkv_term, out_term), ('dp', 'row', 'col'))]
    all_to_all x0 -> x4, blocking collectives: none -> 74.5 us  [exchange(): return lax.all_to_all(rows, axis, split_axis=0, concat_axis=0, tiled=True)]
    all_to_all x8 -> x2, starting transfers between devices: 58.8 us -> 18.5 us  [exchange(): return lax.all_to_all(rows, axis, split_axis=0, concat_axis=0, tiled=True)]
    dot_general x25 -> x0, matrix products: 36 us -> none  [the longest x3 7.85 us: attend_back(): jnp.einsum('abhlm,ambhd->albhd', dround, key_heads, preferred_element_typ...]
    pallas_call x0 -> x8, Pallas kernels: none -> 20.5 us  [call(): pl.pallas_call(body, out_shape=outs, in_specs=[vmem] * len(args), out_spe...]
    all_to_all x8 -> x2, waiting for transfers between devices: 23.4 us -> 8.43 us  [exchange(): return lax.all_to_all(rows, axis, split_axis=0, concat_axis=0, tiled=True)]
    convert_element_type x17 -> x0, local copies, waits for them, and re-layouts: 13.5 us -> none  [the longest x4 3.61 us: attend_back(): stacked.reshape(line_block.shape[:3] + (3 * model_width,))]
    unnamed x71 -> x13, local copies, waits for them, and re-layouts: 8.99 us -> 2.82 us
  transfers between devices with their start and end apart: 9 -> 2, of which waited for: 6 -> 1; matrix products, arithmetic and copies ran while one was open for 14% -> 0% of each run, Pallas kernels for 0% -> 10%
where the time goes in v1:
time: 128 us; the launch traced here: 127 us
  blocking collectives  74.5 us (58%)
  Pallas kernels  20.5 us (16%)
  starting transfers between devices  18.5 us (14%)
  waiting for transfers between devices  8.43 us (7%)
  local copies, waits for them, and re-layouts  2.82 us (2%)
  other arithmetic  1.65 us (1%)
    all_to_all x4, blocking collectives, exchange(): return lax.all_to_all(rows, axis, split_axis=0, concat_axis=0, tiled=True)  74.5 us
    pallas_call x8, Pallas kernels, call(): pl.pallas_call(body, out_shape=outs, in_specs=[vmem] * len(args), out_spe...  20.5 us
    all_to_all x2, starting transfers between devices, exchange(): return lax.all_to_all(rows, axis, split_axis=0, concat_axis=0, tiled=True)  18.5 us
    all_to_all x2, waiting for transfers between devices, exchange(): return lax.all_to_all(rows, axis, split_axis=0, concat_axis=0, tiled=True)  8.43 us
    unnamed x13, local copies, waits for them, and re-layouts  2.82 us
  transfers between devices with their start and end apart: 2, of which 1 were waited for; matrix products, arithmetic and copies ran while one was open for 0% of the time, Pallas kernels for 10%

profile of v1, /device:TPU:1, one launch (start us, length us, event | category | flops | bytes accessed | tf_op | source)
XLA Modules:
  0.0 127.1 jit_solution(17921116429381657287)
XLA Ops:
  0.6 0.0 copy-start.2
  0.6 0.9 copy-done.2
  1.5 0.0 copy-start.4
  1.5 0.9 copy-done.4
  2.4 1.0 shard_map.76
  3.5 15.8 %all_to_all.67 = bf16[8,32,512]{2,1,0:T(8,128)(2,1)S(1)} all-to-all(bf16[8,32,512]{2,1,0:T(8,128)(2,1)S(1)} %bitcast.28), channel_id=1, replica_groups=mesh['dp'=2,'row'=8,'col'=32] {'row'}, dimensions={0} | all-to-all | bytes 524288 | tf_op jit(solution)/shard_map/all_to_all | solution.py:194
  19.2 0.0 copy-start
  19.2 12.1 %all-to-all-start = ((bf16[32,8,512]{2,1,0:T(8,128)(2,1)}), bf16[32,8,512]{2,1,0:T(8,128)(2,1)S(1)}, u32[]{:S(2)}, u32[]{:S(2)}) async-start(bf16[32,8,512]{2,1,0:T(8,128)(2,1)} %bitcast.3), calls=%async_computation | async-start | bytes 524288 | tf_op jit(solution)/shard_map/all_to_all | solution.py:194
  31.4 0.0 copy-done
  31.4 0.0 copy-start.1
  31.4 0.0 copy-start.3
  31.4 0.0 copy-start.5
  31.4 0.2 copy.8
  31.6 0.7 copy-done.1
  32.3 0.1 copy-done.3
  32.3 0.1 copy-done.5
  32.4 5.7 %shard_map.75 = (bf16[256,512]{1,0:T(8,128)(2,1)S(1)}, f32[256,1024]{1,0:T(8,128)S(1)}) custom-call(bf16[256,256]{1,0:T(8,128)(2,1)S(1)} %bitcast.32, bf16[256,256]{1,0:T(8,128)(2,1)S(1)} %bitcast.34, bf16[256,768]{1,0:T(8,128)(2,1)S(1)} %copy-done, bf16[768,256]{1,0:T(8,128)(2,1)S(1)} %bitcast.23, bf16[256,256]{1,0:T(8,128)(2,1)S(1)} %copy-done.1), custom_call_target="tpu_custom_call" | custom-call | flops 2348810240 | bytes 1048576 | tf_op jit(solution)/shard_map/pallas_call | solution.py:179
  38.1 5.7 %shard_map.77 = (bf16[256,512]{1,0:T(8,128)(2,1)S(1)}, f32[256,1024]{1,0:T(8,128)S(1)}) custom-call(bf16[256,512]{1,0:T(8,128)(2,1)S(1)} %bitcast.27, bf16[256,768]{1,0:T(8,128)(2,1)S(1)} %copy-done, bf16[768,256]{1,0:T(8,128)(2,1)S(1)} %bitcast.24, bf16[256,256]{1,0:T(8,128)(2,1)S(1)} %copy-done.1, f32[256,1024]{1,0:T(8,128)S(1)} %get-tuple-element.17.grad_so_far), custom_call_target="tpu_custom_call" | custom-call | flops 2348810240 | bytes 1048576 | tf_op jit(solution)/shard_map/pallas_call | solution.py:179
  43.8 0.0 all-to-all-done
  43.8 5.8 %shard_map.78 = (bf16[256,512]{1,0:T(8,128)(2,1)S(1)}, bf16[256,1536]{1,0:T(8,128)(2,1)S(1)}) custom-call(bf16[256,512]{1,0:T(8,128)(2,1)S(1)} %bitcast.26, bf16[256,768]{1,0:T(8,128)(2,1)S(1)} %copy-done, bf16[768,256]{1,0:T(8,128)(2,1)S(1)} %bitcast.25, bf16[256,256]{1,0:T(8,128)(2,1)S(1)} %copy-done.1, f32[256,1024]{1,0:T(8,128)S(1)} %get-tuple-element.18.grad_so_far, ...), custom_call_target="tpu_custom_call" | custom-call | flops 2348810240 | bytes 1048576 | tf_op jit(solution)/shard_map/pallas_call | solution.py:179
  49.6 17.1 %all_to_all.68 = bf16[8,32,1536]{2,1,0:T(8,128)(2,1)S(1)} all-to-all(bf16[8,32,1536]{2,1,0:T(8,128)(2,1)S(1)} %bitcast.22), channel_id=1, replica_groups=mesh['dp'=2,'row'=8,'col'=32] {'row'}, dimensions={0} | all-to-all | bytes 1572864 | tf_op jit(solution)/shard_map/all_to_all | solution.py:194
  66.6 0.2 shard_map.79
  66.9 23.7 %all_to_all.69 = bf16[32,8,640]{2,1,0:T(8,128)(2,1)S(1)} all-to-all(bf16[32,8,640]{2,1,0:T(8,128)(2,1)S(1)} %bitcast.21), channel_id=1, replica_groups=mesh['dp'=2,'row'=8,'col'=32] {'col'}, dimensions={0} | all-to-all | bytes 655360 | tf_op jit(solution)/shard_map/all_to_all | solution.py:194
  90.6 18.0 %all_to_all.70 = bf16[64,8,128]{2,1,0:T(8,128)(2,1)S(1)} all-to-all(bf16[64,8,128]{2,1,0:T(8,128)(2,1)S(1)} %bitcast.30), channel_id=1, replica_groups=mesh['dp'=2,'row'=8,'col'=32] {'dp','col'}, dimensions={0} | all-to-all | bytes 262144 | tf_op jit(solution)/shard_map/all_to_all | solution.py:194
  108.6 1.0 shard_map.82
  109.6 6.4 %all-to-all-start.5 = ((bf16[8,32,1024]{2,1,0:T(8,128)(2,1)}), bf16[8,32,1024]{2,1,0:T(8,128)(2,1)S(1)}, u32[]{:S(2)}, u32[]{:S(2)}) async-start(bf16[8,32,1024]{2,1,0:T(8,128)(2,1)} %bitcast.15), calls=%async_computation.5 | async-start | bytes 1048576 | tf_op jit(solution)/shard_map/all_to_all | solution.py:194
  116.0 1.1 shard_map.80
  117.0 8.4 %all-to-all-done.5 = bf16[8,32,1024]{2,1,0:T(8,128)(2,1)S(1)} async-done(((bf16[8,32,1024]{2,1,0:T(8,128)(2,1)}), bf16[8,32,1024]{2,1,0:T(8,128)(2,1)S(1)}, u32[]{:S(2)}, u32[]{:S(2)}) %all-to-all-start.5) | async-done | bytes 524320 | tf_op jit(solution)/shard_map/all_to_all | solution.py:194
  125.5 0.7 slice_convert_fusion.1
  126.2 0.9 slice_convert_fusion
  (1 shorter events, 0.0 us)
Async XLA Ops:
  0.6 0.9 copy-start.2
  1.5 0.9 copy-start.4
  19.2 12.1 %copy-start = (bf16[256,768]{1,0:T(8,128)(2,1)S(1)}, bf16[256,768]{1,0:T(8,128)(2,1)}, u32[]{:S(2)}) copy-start(bf16[256,768]{1,0:T(8,128)(2,1)} %w_qkv.5) | copy-start | bytes 1179652
  19.2 24.5 %all-to-all-start = ((bf16[32,8,512]{2,1,0:T(8,128)(2,1)}), bf16[32,8,512]{2,1,0:T(8,128)(2,1)S(1)}, u32[]{:S(2)}, u32[]{:S(2)}) async-start(bf16[32,8,512]{2,1,0:T(8,128)(2,1)} %bitcast.3), calls=%async_computation | async-start | bytes 524288 | tf_op jit(solution)/shard_map/all_to_all | solution.py:194
  31.4 0.9 copy-start.1
  31.4 1.0 copy-start.3
  31.4 1.0 copy-start.5
  109.6 15.9 %all-to-all-start.5 = ((bf16[8,32,1024]{2,1,0:T(8,128)(2,1)}), bf16[8,32,1024]{2,1,0:T(8,128)(2,1)S(1)}, u32[]{:S(2)}, u32[]{:S(2)}) async-start(bf16[8,32,1024]{2,1,0:T(8,128)(2,1)} %bitcast.15), calls=%async_computation.5 | async-start | bytes 1048576 | tf_op jit(solution)/shard_map/all_to_all | solution.py:194

commit v2 on v1

--- a/solution.py
+++ b/solution.py
@@ -13,6 +13,9 @@
 C = 256
 T = 256
 PATCHES = 2
+Z = 16
+HALF = 128
+QUAD = 4
 LINES = 4
 NEG = -1e30
 
@@ -41,32 +44,54 @@
     return (peer // 4) * 128 + (r % 8) * 16 + (peer % 4) * LINES + (r // 8) % LINES
 
 
+def y_sorted(r):
+    return (r % 64) * LINES + r // 64
+
+
+def x_sorted(r):
+    return (r % 64) // 8 * 32 + r // 64 * 8 + r % 8
+
+
 def z_line(r):
-    return r // 16
-
-
-def y_line(r):
-    return r % LINES
-
-
-def x_line(r):
-    return (r // 8) % LINES
+    return r // Z
+
+
+def long_line(r):
+    return r // 64
 
 
 def onehot(hit):
     return jnp.where(hit, 1.0, 0.0).astype(BF)
 
 
-def pack_body(feat, cot, send_x, send_y):
-    for source, out in ((x_source, send_x), (y_source, send_y)):
-        pick = onehot(source(iota(0)) == iota(1))
-        out[:, :C] = nn(pick, feat[...]).astype(BF)
-        out[:, C:] = nn(pick, cot[...]).astype(BF)
-
-
-def axis_math(line, feat, cot, w_qkv, w_qkv_t, w_out):
+def send(source, feat, cot, out):
+    pick = onehot(source(iota(0)) == iota(1))
+    out[:, :C] = nn(pick, feat).astype(BF)
+    out[:, C:] = nn(pick, cot).astype(BF)
+
+
+def pack_body(feat_hbm, cot_hbm, send_x, feat, cot, sem):
+    copies = [
+        pltpu.make_async_copy(feat_hbm, feat, sem.at[0]),
+        pltpu.make_async_copy(cot_hbm, cot, sem.at[1]),
+    ]
+    for copy in copies:
+        copy.start()
+    for copy in copies:
+        copy.wait()
+    send(x_source, feat[...], cot[...], send_x)
+
+
+def axis_math(source, line, feat, cot, w_qkv, w_qkv_t, w_out):
     scale = 1.0 / math.sqrt(DEPTH)
     eye = onehot(iota(0) == iota(1))
+    if source is None:
+        unsort = eye
+    else:
+        sort = onehot(source(iota(0)) == iota(1))
+        unsort = onehot(iota(0) == source(iota(1)))
+        feat = nn(sort, feat).astype(BF)
+        cot = nn(sort, cot).astype(BF)
     feat_t = nt(eye, feat).astype(BF)
     cot_t = nt(eye, cot).astype(BF)
     proj = nn(feat, w_qkv[...]).astype(BF)
@@ -75,51 +100,85 @@
     gmix_t = nn(w_out[...], cot_t).astype(BF)
     q, k, v = proj[:, :C], proj[:, C : 2 * C], proj[:, 2 * C :]
     q_t, k_t, v_t = proj_t[:C], proj_t[C : 2 * C], proj_t[2 * C :]
-    bias = jnp.where(line(iota(0)) == line(iota(1)), 0.0, NEG)
-    head_of_row = iota(0) // DEPTH
-    head_of_lane = iota(1) // DEPTH
-    zero = jnp.zeros((T, C), BF)
-    out_t = []
-    dq_t = []
-    dk = jnp.zeros((T, C), F32)
-    dv = jnp.zeros((T, C), F32)
-    for h in range(HEADS):
-        rows = slice(h * DEPTH, (h + 1) * DEPTH)
-        on_row = head_of_row == h
-        on_lane = head_of_lane == h
-        scores = nn(k, jnp.where(on_row, q_t, zero)) + bias
-        top = jnp.max(scores, axis=0, keepdims=True)
-        e = jnp.exp((scores - top) * scale)
-        probs = e * (1.0 / jnp.sum(e, axis=0, keepdims=True))
-        rounded = probs.astype(BF)
-        out_t.append(nn(v_t[rows], rounded))
-        dv += nn(rounded, jnp.where(on_lane, gmix, zero))
-        dprobs = nn(v, jnp.where(on_row, gmix_t, zero))
-        mean = jnp.sum(dprobs * probs, axis=0, keepdims=True)
-        dround = (probs * (dprobs - mean) * scale).astype(BF)
-        dq_t.append(nn(k_t[rows], dround))
-        dk += nn(dround, jnp.where(on_lane, q, zero))
-    out_t = jnp.concatenate(out_t, axis=0).astype(BF)
-    dq_t = jnp.concatenate(dq_t, axis=0).astype(BF)
-    out = nt(eye, out_t).astype(BF)
+    wide = (HALF, QUAD * HALF)
+    bias = jnp.where(line(iota(0, wide)) == line(iota(1, wide) % HALF), 0.0, NEG)
+    head_of_lane = iota(1, (HALF, HALF)) // DEPTH
+    blank = jnp.zeros((HALF, HALF), BF)
+    strip = jnp.zeros((DEPTH, HALF), BF)
+
+    def spread(a_t):
+        return jnp.concatenate(
+            [
+                jnp.concatenate(
+                    [a_t[i * DEPTH : (i + 1) * DEPTH] if i == j else strip for i in range(QUAD)],
+                    axis=0,
+                )
+                for j in range(QUAD)
+            ],
+            axis=1,
+        )
+
+    def stack(a):
+        return jnp.concatenate(
+            [jnp.where(head_of_lane == j, a, blank) for j in range(QUAD)], axis=0
+        )
+
+    def per_head(a_t, m):
+        return jnp.concatenate(
+            [
+                nn(a_t[j * DEPTH : (j + 1) * DEPTH], m[:, j * HALF : (j + 1) * HALF])
+                for j in range(QUAD)
+            ],
+            axis=0,
+        )
+
+    parts = []
+    for half in range(2):
+        toks = slice(half * HALF, (half + 1) * HALF)
+        for quad in range(2):
+            chans = slice(quad * HALF, (quad + 1) * HALF)
+            scores = nn(k[toks, chans], spread(q_t[chans, toks])) + bias
+            top = jnp.max(scores, axis=0, keepdims=True)
+            e = jnp.exp((scores - top) * scale)
+            probs = e * (1.0 / jnp.sum(e, axis=0, keepdims=True))
+            rounded = probs.astype(BF)
+            out_t = per_head(v_t[chans, toks], rounded)
+            dv = nn(rounded, stack(gmix[toks, chans]))
+            dprobs = nn(v[toks, chans], spread(gmix_t[chans, toks]))
+            mean = jnp.sum(dprobs * probs, axis=0, keepdims=True)
+            dround = (probs * (dprobs - mean) * scale).astype(BF)
+            dq_t = per_head(k_t[chans, toks], dround)
+            dk = nn(dround, stack(q[toks, chans]))
+            parts.append([m.astype(BF) for m in (out_t, dq_t, dk, dv)])
+
+    def whole(at, transposed):
+        p = [[parts[2 * half + quad][at] for quad in range(2)] for half in range(2)]
+        if transposed:
+            p = [[p[j][i] for j in range(2)] for i in range(2)]
+        return jnp.concatenate([jnp.concatenate(r, axis=1) for r in p], axis=0)
+
+    out_t, dq_t = whole(0, True), whole(1, True)
+    dk, dv = whole(2, False), whole(3, False)
+    out = nt(unsort, out_t).astype(BF)
     dq = nt(eye, dq_t).astype(BF)
-    dk = dk.astype(BF)
-    dv = dv.astype(BF)
     dfeat = (
         nn(dq, w_qkv_t[:C]) + nn(dk, w_qkv_t[C : 2 * C]) + nn(dv, w_qkv_t[2 * C :])
     ).astype(BF)
+    if source is not None:
+        dfeat = nn(unsort, dfeat).astype(BF)
     return out, dfeat, (nn(feat_t, dq), nn(feat_t, dk), nn(feat_t, dv), nn(out_t, cot))
 
 
-def z_body(feat, cot, w_qkv, w_qkv_t, w_out, back, grad):
-    back[:, :C], back[:, C:], terms = axis_math(z_line, feat[...], cot[...], w_qkv, w_qkv_t, w_out)
+def z_body(feat, cot, w_qkv, w_qkv_t, w_out, back, grad, send_y):
+    send(y_source, feat[...], cot[...], send_y)
+    back[:, :C], back[:, C:], terms = axis_math(None, z_line, feat[...], cot[...], w_qkv, w_qkv_t, w_out)
     for at, term in enumerate(terms):
         grad[:, at * C : (at + 1) * C] = term
 
 
 def x_body(got, w_qkv, w_qkv_t, w_out, grad_so_far, back, grad):
     back[:, :C], back[:, C:], terms = axis_math(
-        x_line, got[:, :C], got[:, C:], w_qkv, w_qkv_t, w_out
+        x_sorted, long_line, got[:, :C], got[:, C:], w_qkv, w_qkv_t, w_out
     )
     for at, term in enumerate(terms):
         cols = slice(at * C, (at + 1) * C)
@@ -128,7 +187,7 @@
 
 def y_body(got, w_qkv, w_qkv_t, w_out, grad_so_far, back_x, back, send_row):
     back[:, :C], back[:, C:], terms = axis_math(
-        y_line, got[:, :C], got[:, C:], w_qkv, w_qkv_t, w_out
+        y_sorted, long_line, got[:, :C], got[:, C:], w_qkv, w_qkv_t, w_out
     )
     send_row[:, : 2 * C] = back_x[...]
     for at, term in enumerate(terms):
@@ -174,14 +233,20 @@
     grad_in[...] = total[:, C:]
 
 
-def call(body, outs, flops, *args):
+def unpack_body(got, grad_qkv, grad_out):
+    grad_qkv[...] = got[:, : 3 * C].astype(F32)
+    grad_out[...] = got[:, 3 * C :].astype(F32)
+
+
+def call(body, outs, flops, *args, space=pltpu.VMEM, scratch=(), grant=40 * 2**20):
     vmem = pl.BlockSpec(memory_space=pltpu.VMEM)
     return pl.pallas_call(
         body,
         out_shape=outs,
-        in_specs=[vmem] * len(args),
+        in_specs=[pl.BlockSpec(memory_space=space)] * len(args),
+        scratch_shapes=scratch,
         out_specs=[vmem] * len(outs),
-        compiler_params=pltpu.CompilerParams(vmem_limit_bytes=40 * 2**20),
+        compiler_params=pltpu.CompilerParams(vmem_limit_bytes=grant),
         cost_estimate=pl.CostEstimate(flops=flops, bytes_accessed=2**20, transcendentals=2**19),
     )(*args)
 
@@ -202,9 +267,20 @@
     cube = 2 * T * T * C
     back_shape = shape(T, 2 * C, BF)
     grad_shape = shape(C, 4 * C, F32)
-    send_x, send_y = call(pack_body, [back_shape] * 2, cube * 4, feat, cot)
+    (send_x,) = call(
+        pack_body,
+        [back_shape],
+        cube * 2,
+        feat,
+        cot,
+        space=pltpu.HBM,
+        scratch=[pltpu.VMEM((T, C), BF), pltpu.VMEM((T, C), BF), pltpu.SemaphoreType.DMA((2,))],
+        grant=None,
+    )
     got_x = exchange(send_x, "row")
-    back_z, grad = call(z_body, [back_shape, grad_shape], cube * 70, feat, cot, *weights)
+    back_z, grad, send_y = call(
+        z_body, [back_shape, grad_shape, back_shape], cube * 70, feat, cot, *weights
+    )
     got_y = exchange(send_y, "col")
     back_x, grad = call(x_body, [back_shape, grad_shape], cube * 70, got_x, *weights, grad)
     back_y, send_row = call(
@@ -223,12 +299,10 @@
         functools.partial(dp_sum_body, factor), [shape(C, 4 * C, BF)], cube, got_rest
     )
     whole = exchange(send_last, "row")
-    return (
-        update.reshape(local_shape),
-        grad_in.reshape(local_shape),
-        whole[:, : 3 * C].astype(F32),
-        whole[:, 3 * C :].astype(F32),
-    )
+    grad_qkv, grad_out = call(
+        unpack_body, [shape(C, 3 * C, F32), shape(C, C, F32)], 2**20, whole
+    )
+    return (update.reshape(local_shape), grad_in.reshape(local_shape), grad_qkv, grad_out)
 
 
 def solution(mesh):

time: 128 us -> 119 us (0.930)
  blocking collectives: 74.5 us -> 53.7 us
  starting transfers between devices: 18.5 us -> 28.3 us
  waiting for transfers between devices: 8.43 us -> 16.3 us
  Pallas kernels: 20.5 us -> 15.9 us
  other arithmetic: 1.65 us -> 0 us
    all_to_all x4 -> x3, blocking collectives: 74.5 us -> 53.7 us  [exchange(): return lax.all_to_all(rows, axis, split_axis=0, concat_axis=0, tiled=True)]
    all_to_all x2 -> x3, starting transfers between devices: 18.5 us -> 28.3 us  [exchange(): return lax.all_to_all(rows, axis, split_axis=0, concat_axis=0, tiled=True)]
    all_to_all x2 -> x3, waiting for transfers between devices: 8.43 us -> 16.3 us  [exchange(): return lax.all_to_all(rows, axis, split_axis=0, concat_axis=0, tiled=True)]
    pallas_call x8 -> x9, Pallas kernels: 20.5 us -> 15.9 us  [call(): pl.pallas_call(body, out_shape=outs, in_specs=[pl.BlockSpec(memory_space=...]
    convert_element_type x2 -> x0, other arithmetic: 1.65 us -> none  [the longest x1 0.93 us: body(): whole[:, :3 * C].astype(F32)]
  transfers between devices with their start and end apart: 2 -> 3, of which waited for: 1 -> 3; matrix products, arithmetic and copies ran while one was open for 0% -> 0% of each run, Pallas kernels for 10% -> 7%
where the time goes in v2:
time: 119 us; the launch traced here: 118 us
  blocking collectives  53.7 us (45%)
  starting transfers between devices  28.3 us (24%)
  waiting for transfers between devices  16.3 us (14%)
  Pallas kernels  15.9 us (13%)
  local copies, waits for them, and re-layouts  3.21 us (3%)
    all_to_all x3, blocking collectives, exchange(): return lax.all_to_all(rows, axis, split_axis=0, concat_axis=0, tiled=True)  53.7 us
    all_to_all x3, starting transfers between devices, exchange(): return lax.all_to_all(rows, axis, split_axis=0, concat_axis=0, tiled=True)  28.3 us
    all_to_all x3, waiting for transfers between devices, exchange(): return lax.all_to_all(rows, axis, split_axis=0, concat_axis=0, tiled=True)  16.3 us
    pallas_call x9, Pallas kernels, call(): pl.pallas_call(body, out_shape=outs, in_specs=[pl.BlockSpec(memory_space=...  15.9 us
    unnamed x13, local copies, waits for them, and re-layouts  3.21 us
  transfers between devices with their start and end apart: 3, of which 3 were waited for; matrix products, arithmetic and copies ran while one was open for 0% of the time, Pallas kernels for 7%

profile of v2, /device:TPU:1, one launch (start us, length us, event | category | flops | bytes accessed | tf_op | source)
XLA Modules:
  0.0 118.1 jit_solution(9696781027392063128)
XLA Ops:
  0.6 1.9 %shard_map.76 = bf16[256,512]{1,0:T(8,128)(2,1)} custom-call(bf16[256,256]{1,0:T(8,128)(2,1)} %bitcast.31, bf16[256,256]{1,0:T(8,128)(2,1)} %bitcast.33), custom_call_target="tpu_custom_call" | custom-call | flops 67108864 | bytes 1048576 | tf_op jit(solution)/shard_map/pallas_call | solution.py:243
  2.6 0.0 copy-start
  2.6 10.3 %all-to-all-start.1 = ((bf16[8,32,512]{2,1,0:T(8,128)(2,1)}), bf16[8,32,512]{2,1,0:T(8,128)(2,1)S(1)}, u32[]{:S(2)}, u32[]{:S(2)}) async-start(bf16[8,32,512]{2,1,0:T(8,128)(2,1)} %bitcast.35), calls=%async_computation.1 | async-start | bytes 524288 | tf_op jit(solution)/shard_map/all_to_all | solution.py:259
  12.9 0.0 copy-done
  12.9 0.0 copy-start.1
  12.9 0.0 copy-start.2
  12.9 0.0 copy-start.3
  12.9 0.2 copy.8
  13.1 0.7 copy-done.1
  13.8 0.1 copy-done.2
  13.9 0.1 copy-done.3
  13.9 3.3 %shard_map.75 = (bf16[256,512]{1,0:T(8,128)(2,1)S(1)}, f32[256,1024]{1,0:T(8,128)S(1)}, bf16[256,512]{1,0:T(8,128)(2,1)}) custom-call(bf16[256,256]{1,0:T(8,128)(2,1)S(1)} %bitcast.32, bf16[256,256]{1,0:T(8,128)(2,1)S(1)} %bitcast.34, bf16[256,768]{1,0:T(8,128)(2,1)S(1)} %copy-done, bf16[768,256]{1,0:T(8,128)(2,1)S(1)} %bitcast.24, ...), custom_call_target="tpu_custom_call" | custom-call | flops 2348810240 | bytes 1048576 | tf_op jit(solution)/shard_map/pallas_call | solution.py:243
  17.2 0.0 copy-start.4
  17.2 1.0 copy-done.4
  18.2 1.2 %all-to-all-done.1 = bf16[8,32,512]{2,1,0:T(8,128)(2,1)S(1)} async-done(((bf16[8,32,512]{2,1,0:T(8,128)(2,1)}), bf16[8,32,512]{2,1,0:T(8,128)(2,1)S(1)}, u32[]{:S(2)}, u32[]{:S(2)}) %all-to-all-start.1) | async-done | bytes 262176 | tf_op jit(solution)/shard_map/all_to_all | solution.py:259
  19.4 11.3 %all-to-all-start = ((bf16[32,8,512]{2,1,0:T(8,128)(2,1)}), bf16[32,8,512]{2,1,0:T(8,128)(2,1)S(1)}, u32[]{:S(2)}, u32[]{:S(2)}) async-start(bf16[32,8,512]{2,1,0:T(8,128)(2,1)} %bitcast.3), calls=%async_computation | async-start | bytes 524288 | tf_op jit(solution)/shard_map/all_to_all | solution.py:259
  30.7 0.0 copy-start.5
  30.7 1.2 %copy-done.5 = f32[256,1024]{1,0:T(8,128)S(1)} copy-done((f32[256,1024]{1,0:T(8,128)S(1)}, f32[256,1024]{1,0:T(8,128)}, u32[]{:S(2)}) %copy-start.5) | copy-done | bytes 1048600
  31.9 3.7 %shard_map.77 = (bf16[256,512]{1,0:T(8,128)(2,1)S(1)}, f32[256,1024]{1,0:T(8,128)S(1)}) custom-call(bf16[256,512]{1,0:T(8,128)(2,1)S(1)} %bitcast.27, bf16[256,768]{1,0:T(8,128)(2,1)S(1)} %copy-done, bf16[768,256]{1,0:T(8,128)(2,1)S(1)} %bitcast.25, bf16[256,256]{1,0:T(8,128)(2,1)S(1)} %copy-done.1, f32[256,1024]{1,0:T(8,128)S(1)} %copy-done.5), custom_call_target="tpu_custom_call" | custom-call | flops 2348810240 | bytes 1048576 | tf_op jit(solution)/shard_map/pallas_call | solution.py:243
  35.6 6.6 %all-to-all-done = bf16[32,8,512]{2,1,0:T(8,128)(2,1)S(1)} async-done(((bf16[32,8,512]{2,1,0:T(8,128)(2,1)}), bf16[32,8,512]{2,1,0:T(8,128)(2,1)S(1)}, u32[]{:S(2)}, u32[]{:S(2)}) %all-to-all-start) | async-done | bytes 262176 | tf_op jit(solution)/shard_map/all_to_all | solution.py:259
  42.2 3.7 %shard_map.78 = (bf16[256,512]{1,0:T(8,128)(2,1)S(1)}, bf16[256,1536]{1,0:T(8,128)(2,1)S(1)}) custom-call(bf16[256,512]{1,0:T(8,128)(2,1)S(1)} %bitcast.28, bf16[256,768]{1,0:T(8,128)(2,1)S(1)} %copy-done, bf16[768,256]{1,0:T(8,128)(2,1)S(1)} %bitcast.26, bf16[256,256]{1,0:T(8,128)(2,1)S(1)} %copy-done.1, f32[256,1024]{1,0:T(8,128)S(1)} %get-tuple-element.18.grad_so_far, ...), custom_call_target="tpu_custom_call" | custom-call | flops 2348810240 | bytes 1048576 | tf_op jit(solution)/shard_map/pallas_call | solution.py:243
  45.9 18.5 %all_to_all.66 = bf16[8,32,1536]{2,1,0:T(8,128)(2,1)S(1)} all-to-all(bf16[8,32,1536]{2,1,0:T(8,128)(2,1)S(1)} %bitcast.22), channel_id=1, replica_groups=mesh['dp'=2,'row'=8,'col'=32] {'row'}, dimensions={0} | all-to-all | bytes 1572864 | tf_op jit(solution)/shard_map/all_to_all | solution.py:259
  64.4 0.2 shard_map.79
  64.7 17.5 %all_to_all.67 = bf16[32,8,640]{2,1,0:T(8,128)(2,1)S(1)} all-to-all(bf16[32,8,640]{2,1,0:T(8,128)(2,1)S(1)} %bitcast.21), channel_id=1, replica_groups=mesh['dp'=2,'row'=8,'col'=32] {'col'}, dimensions={0} | all-to-all | bytes 655360 | tf_op jit(solution)/shard_map/all_to_all | solution.py:259
  82.2 17.7 %all_to_all.68 = bf16[64,8,128]{2,1,0:T(8,128)(2,1)S(1)} all-to-all(bf16[64,8,128]{2,1,0:T(8,128)(2,1)S(1)} %bitcast.30), channel_id=1, replica_groups=mesh['dp'=2,'row'=8,'col'=32] {'dp','col'}, dimensions={0} | all-to-all | bytes 262144 | tf_op jit(solution)/shard_map/all_to_all | solution.py:259
  99.9 1.0 shard_map.82
  100.9 6.7 %all-to-all-start.5 = ((bf16[8,32,1024]{2,1,0:T(8,128)(2,1)}), bf16[8,32,1024]{2,1,0:T(8,128)(2,1)S(1)}, u32[]{:S(2)}, u32[]{:S(2)}) async-start(bf16[8,32,1024]{2,1,0:T(8,128)(2,1)} %bitcast.15), calls=%async_computation.5 | async-start | bytes 1048576 | tf_op jit(solution)/shard_map/all_to_all | solution.py:259
  107.5 1.1 shard_map.80
  108.6 8.4 %all-to-all-done.5 = bf16[8,32,1024]{2,1,0:T(8,128)(2,1)S(1)} async-done(((bf16[8,32,1024]{2,1,0:T(8,128)(2,1)}), bf16[8,32,1024]{2,1,0:T(8,128)(2,1)S(1)}, u32[]{:S(2)}, u32[]{:S(2)}) %all-to-all-start.5) | async-done | bytes 524320 | tf_op jit(solution)/shard_map/all_to_all | solution.py:259
  117.0 1.0 shard_map.83
  (1 shorter events, 0.0 us)
Async XLA Ops:
  2.6 10.4 %copy-start = (bf16[256,768]{1,0:T(8,128)(2,1)S(1)}, bf16[256,768]{1,0:T(8,128)(2,1)}, u32[]{:S(2)}) copy-start(bf16[256,768]{1,0:T(8,128)(2,1)} %w_qkv.5) | copy-start | bytes 1179652
  2.6 16.9 %all-to-all-start.1 = ((bf16[8,32,512]{2,1,0:T(8,128)(2,1)}), bf16[8,32,512]{2,1,0:T(8,128)(2,1)S(1)}, u32[]{:S(2)}, u32[]{:S(2)}) async-start(bf16[8,32,512]{2,1,0:T(8,128)(2,1)} %bitcast.35), calls=%async_computation.1 | async-start | bytes 524288 | tf_op jit(solution)/shard_map/all_to_all | solution.py:259
  12.9 0.9 copy-start.1
  12.9 1.0 copy-start.2
  12.9 1.0 copy-start.3
  17.2 1.0 copy-start.4
  19.4 22.8 %all-to-all-start = ((bf16[32,8,512]{2,1,0:T(8,128)(2,1)}), bf16[32,8,512]{2,1,0:T(8,128)(2,1)S(1)}, u32[]{:S(2)}, u32[]{:S(2)}) async-start(bf16[32,8,512]{2,1,0:T(8,128)(2,1)} %bitcast.3), calls=%async_computation | async-start | bytes 524288 | tf_op jit(solution)/shard_map/all_to_all | solution.py:259
  30.7 1.2 %copy-start.5 = (f32[256,1024]{1,0:T(8,128)S(1)}, f32[256,1024]{1,0:T(8,128)}, u32[]{:S(2)}) copy-start(f32[256,1024]{1,0:T(8,128)} %copy-done.4) | copy-start | bytes 3145732
  100.9 16.2 %all-to-all-start.5 = ((bf16[8,32,1024]{2,1,0:T(8,128)(2,1)}), bf16[8,32,1024]{2,1,0:T(8,128)(2,1)S(1)}, u32[]{:S(2)}, u32[]{:S(2)}) async-start(bf16[8,32,1024]{2,1,0:T(8,128)(2,1)} %bitcast.15), calls=%async_computation.5 | async-start | bytes 1048576 | tf_op jit(solution)/shard_map/all_to_all | solution.py:259

commit v3 on v2

--- a/solution.py
+++ b/solution.py
@@ -40,8 +40,8 @@
 
 
 def x_source(r):
-    peer = r // 32
-    return (peer // 4) * 128 + (r % 8) * 16 + (peer % 4) * LINES + (r // 8) % LINES
+    peer = r // 16
+    return (peer // 8) * 128 + (r % 8) * 16 + (peer % 8) * 2 + (r // 8) % 2
 
 
 def y_sorted(r):
@@ -49,7 +49,7 @@
 
 
 def x_sorted(r):
-    return (r % 64) // 8 * 32 + r // 64 * 8 + r % 8
+    return r // 128 * 128 + (r % 64) // 8 * 16 + (r // 64) % 2 * 8 + r % 8
 
 
 def z_line(r):
@@ -132,24 +132,27 @@
             axis=0,
         )
 
+    blocks = [
+        (slice(half * HALF, (half + 1) * HALF), slice(quad * HALF, (quad + 1) * HALF))
+        for half in range(2)
+        for quad in range(2)
+    ]
+    all_scores = [nn(k[t, c], spread(q_t[c, t])) + bias for t, c in blocks]
+    all_dprobs = [nn(v[t, c], spread(gmix_t[c, t])) for t, c in blocks]
+    soft = []
+    for scores, dprobs in zip(all_scores, all_dprobs):
+        top = jnp.max(scores, axis=0, keepdims=True)
+        e = jnp.exp((scores - top) * scale)
+        probs = e * (1.0 / jnp.sum(e, axis=0, keepdims=True))
+        mean = jnp.sum(dprobs * probs, axis=0, keepdims=True)
+        soft.append((probs.astype(BF), (probs * (dprobs - mean) * scale).astype(BF)))
     parts = []
-    for half in range(2):
-        toks = slice(half * HALF, (half + 1) * HALF)
-        for quad in range(2):
-            chans = slice(quad * HALF, (quad + 1) * HALF)
-            scores = nn(k[toks, chans], spread(q_t[chans, toks])) + bias
-            top = jnp.max(scores, axis=0, keepdims=True)
-            e = jnp.exp((scores - top) * scale)
-            probs = e * (1.0 / jnp.sum(e, axis=0, keepdims=True))
-            rounded = probs.astype(BF)
-            out_t = per_head(v_t[chans, toks], rounded)
-            dv = nn(rounded, stack(gmix[toks, chans]))
-            dprobs = nn(v[toks, chans], spread(gmix_t[chans, toks]))
-            mean = jnp.sum(dprobs * probs, axis=0, keepdims=True)
-            dround = (probs * (dprobs - mean) * scale).astype(BF)
-            dq_t = per_head(k_t[chans, toks], dround)
-            dk = nn(dround, stack(q[toks, chans]))
-            parts.append([m.astype(BF) for m in (out_t, dq_t, dk, dv)])
+    for (t, c), (rounded, dround) in zip(blocks, soft):
+        out_t = per_head(v_t[c, t], rounded)
+        dv = nn(rounded, stack(gmix[t, c]))
+        dq_t = per_head(k_t[c, t], dround)
+        dk = nn(dround, stack(q[t, c]))
+        parts.append([m.astype(BF) for m in (out_t, dq_t, dk, dv)])
 
     def whole(at, transposed):
         p = [[parts[2 * half + quad][at] for quad in range(2)] for half in range(2)]
@@ -173,7 +176,7 @@
     send(y_source, feat[...], cot[...], send_y)
     back[:, :C], back[:, C:], terms = axis_math(None, z_line, feat[...], cot[...], w_qkv, w_qkv_t, w_out)
     for at, term in enumerate(terms):
-        grad[:, at * C : (at + 1) * C] = term
+        grad[:, at * C : (at + 1) * C] = term.astype(BF)
 
 
 def x_body(got, w_qkv, w_qkv_t, w_out, grad_so_far, back, grad):
@@ -182,45 +185,46 @@
     )
     for at, term in enumerate(terms):
         cols = slice(at * C, (at + 1) * C)
-        grad[:, cols] = grad_so_far[:, cols] + term
-
-
-def y_body(got, w_qkv, w_qkv_t, w_out, grad_so_far, back_x, back, send_row):
+        grad[:, cols] = (grad_so_far[:, cols].astype(F32) + term).astype(BF)
+
+
+def core():
+    return lax.rem(lax.axis_index("row"), 2)
+
+
+def y_body(got, w_qkv, w_qkv_t, w_out, grad_so_far, back, keep, give, total):
     back[:, :C], back[:, C:], terms = axis_math(
         y_sorted, long_line, got[:, :C], got[:, C:], w_qkv, w_qkv_t, w_out
     )
-    send_row[:, : 2 * C] = back_x[...]
     for at, term in enumerate(terms):
         cols = slice(at * C, (at + 1) * C)
-        send_row[:, 2 * C + at * C : 3 * C + at * C] = (grad_so_far[:, cols] + term).astype(BF)
-
-
-def row_sum_body(got_row, back_y, send_col):
+        total[:, cols] = grad_so_far[:, cols].astype(F32) + term
+    mine = core()
+    keep[...] = total[pl.ds(pl.multiple_of(mine * 128, 128), 128)]
+    give[...] = total[pl.ds(pl.multiple_of((1 - mine) * 128, 128), 128)].astype(BF)
+
+
+def col_pack_body(back_y, keep, took, send_col):
     send_col[:, : 2 * C] = back_y[...]
-    total = jnp.zeros((32, 4 * C), F32)
+    half = (keep[...] + took[...].astype(F32)).astype(BF)
+    send_col[:128, 2 * C :] = half[:, : 2 * C]
+    send_col[128:, 2 * C :] = half[:, 2 * C :]
+
+
+def row_pack_body(got_col, back_x, send_row):
+    send_row[:, : 2 * C] = back_x[...]
+    block = jnp.sum(got_col[:, 2 * C :].astype(F32).reshape(32, 8, 2 * C), axis=0)
+    block = jnp.concatenate([block[:, :C], block[:, C:]], axis=0)
+    send_row[:, 2 * C :] = jnp.concatenate([block] * 16, axis=0).astype(BF)
+
+
+def last_pack_body(factor, got_row, send):
+    mine = core()
+    block = jnp.zeros((16, C), F32)
     for peer in range(8):
-        total += got_row[peer * 32 : (peer + 1) * 32, 2 * C :].astype(F32)
-    tiles = jnp.concatenate([total[:, j * 128 : (j + 1) * 128] for j in range(8)], axis=0)
-    r = iota(0)
-    pick = onehot(iota(1) == (r % 8) * 32 + r // 8)
-    send_col[:, 2 * C :] = nn(pick, tiles.astype(BF)).astype(BF)
-
-
-def col_sum_body(got_col, send):
-    total = jnp.zeros((8, 128), F32)
-    for peer in range(32):
-        total += got_col[peer * 8 : (peer + 1) * 8, 2 * C :].astype(F32)
-    send[...] = jnp.concatenate([total] * 64, axis=0).astype(BF)
-
-
-def dp_sum_body(factor, got, send):
-    total = ((got[:256].astype(F32) + got[256:].astype(F32)) * factor).astype(BF)
-    r = iota(0)
-    pick = onehot(iota(1) == (r % 32) * 8 + r // 32)
-    tiles = nn(pick, total)
-    rows = jnp.concatenate([tiles[j * 32 : (j + 1) * 32] for j in range(8)], axis=1).astype(BF)
-    for peer in range(8):
-        send[peer * 32 : (peer + 1) * 32] = rows
+        at = pl.multiple_of((2 * peer + mine) * 16, 16)
+        block += got_row[pl.ds(at, 16), 2 * C :].astype(F32)
+    send[...] = jnp.concatenate([block * factor] * 32, axis=0).astype(BF)
 
 
 def final_body(back_z, back_y, back_x, w_out, update, grad_in):
@@ -233,9 +237,16 @@
     grad_in[...] = total[:, C:]
 
 
-def unpack_body(got, grad_qkv, grad_out):
-    grad_qkv[...] = got[:, : 3 * C].astype(F32)
-    grad_out[...] = got[:, 3 * C :].astype(F32)
+def unpack_body(mine, other, grad_qkv, grad_out):
+    for src, half in ((mine, core()), (other, 1 - core())):
+        rows = pl.ds(pl.multiple_of(half * 128, 128), 128)
+        tiles = src[...].astype(F32).reshape(2, 16, 2, 8, C)
+        for at in range(4):
+            block = tiles[at // 2, :, at % 2].reshape(128, C)
+            if at < 3:
+                grad_qkv[rows, at * C : (at + 1) * C] = block
+            else:
+                grad_out[rows, :] = block
 
 
 def call(body, outs, flops, *args, space=pltpu.VMEM, scratch=(), grant=40 * 2**20):
@@ -259,6 +270,10 @@
     return lax.all_to_all(rows, axis, split_axis=0, concat_axis=0, tiled=True)
 
 
+def swap(rows):
+    return lax.ppermute(rows, "row", [(i, i ^ 1) for i in range(8)])
+
+
 def body(features, w_qkv, w_out, cotangent):
     local_shape = features.shape
     feat = features.reshape(T, C)
@@ -266,7 +281,7 @@
     weights = (w_qkv, w_qkv.T, w_out)
     cube = 2 * T * T * C
     back_shape = shape(T, 2 * C, BF)
-    grad_shape = shape(C, 4 * C, F32)
+    grad_shape = shape(C, 4 * C, BF)
     (send_x,) = call(
         pack_body,
         [back_shape],
@@ -277,30 +292,36 @@
         scratch=[pltpu.VMEM((T, C), BF), pltpu.VMEM((T, C), BF), pltpu.SemaphoreType.DMA((2,))],
         grant=None,
     )
-    got_x = exchange(send_x, "row")
+    got_x = exchange(send_x, ("dp", "row"))
     back_z, grad, send_y = call(
         z_body, [back_shape, grad_shape, back_shape], cube * 70, feat, cot, *weights
     )
     got_y = exchange(send_y, "col")
     back_x, grad = call(x_body, [back_shape, grad_shape], cube * 70, got_x, *weights, grad)
-    back_y, send_row = call(
-        y_body, [back_shape, shape(T, 6 * C, BF)], cube * 70, got_y, *weights, grad, back_x
-    )
-    got_row = exchange(send_row, "row")
-    (send_col,) = call(row_sum_body, [shape(T, 2 * C + 128, BF)], cube, got_row, back_y)
+    back_y, keep, give = call(
+        y_body,
+        [back_shape, shape(128, 4 * C, F32), shape(128, 4 * C, BF)],
+        cube * 70,
+        got_y,
+        *weights,
+        grad,
+        scratch=[pltpu.VMEM((C, 4 * C), F32)],
+    )
+    took = swap(give)
+    (send_col,) = call(col_pack_body, [shape(T, 4 * C, BF)], 2**20, back_y, keep, took)
     got_col = exchange(send_col, "col")
-    (send_rest,) = call(col_sum_body, [shape(512, 128, BF)], 2**20, got_col)
-    got_rest = exchange(send_rest, ("dp", "col"))
+    (send_row,) = call(row_pack_body, [shape(T, 3 * C, BF)], 2**20, got_col, back_x)
+    got_row = exchange(send_row, ("dp", "row"))
+    factor = 1.0 / math.sqrt(PATCHES * 64 * 64 * 16)
+    (send_last,) = call(
+        functools.partial(last_pack_body, factor), [shape(512, C, BF)], 2**20, got_row
+    )
+    mine = exchange(send_last, "col")
     update, grad_in = call(
         final_body, [shape(T, C, BF)] * 2, cube * 6, back_z, got_col, got_row, w_out
     )
-    factor = 1.0 / math.sqrt(PATCHES * 64 * 64 * 16)
-    (send_last,) = call(
-        functools.partial(dp_sum_body, factor), [shape(C, 4 * C, BF)], cube, got_rest
-    )
-    whole = exchange(send_last, "row")
     grad_qkv, grad_out = call(
-        unpack_body, [shape(C, 3 * C, F32), shape(C, C, F32)], 2**20, whole
+        unpack_body, [shape(C, 3 * C, F32), shape(C, C, F32)], 2**20, mine, swap(mine)
     )
     return (update.reshape(local_shape), grad_in.reshape(local_shape), grad_qkv, grad_out)
 

time: 119 us -> 113 us (0.950)
  starting transfers between devices: 28.3 us -> 32.7 us
  Pallas kernels: 15.9 us -> 11.9 us
  waiting for transfers between devices: 16.3 us -> 13.9 us
  local copies, waits for them, and re-layouts: 3.21 us -> 1.02 us
  blocking collectives: 53.7 us -> 52.1 us
    ppermute x0 -> x2, starting transfers between devices: none -> 10.2 us  [swap(): return lax.ppermute(rows, 'row', [(i, i ^ 1) for i in range(8)])]
    all_to_all x3 -> x2, starting transfers between devices: 28.3 us -> 22.5 us  [exchange(): return lax.all_to_all(rows, axis, split_axis=0, concat_axis=0, tiled=True)]
    pallas_call x9, Pallas kernels: 15.9 us -> 11.9 us  [call(): pl.pallas_call(body, out_shape=outs, in_specs=[pl.BlockSpec(memory_space=...]
    all_to_all x3 -> x2, waiting for transfers between devices: 16.3 us -> 12.7 us  [exchange(): return lax.all_to_all(rows, axis, split_axis=0, concat_axis=0, tiled=True)]
    unnamed x13 -> x9, local copies, waits for them, and re-layouts: 3.21 us -> 1.02 us
    all_to_all x3, blocking collectives: 53.7 us -> 52.1 us  [exchange(): return lax.all_to_all(rows, axis, split_axis=0, concat_axis=0, tiled=True)]
  transfers between devices with their start and end apart: 3 -> 4, of which waited for: 3 -> 3; matrix products, arithmetic and copies ran while one was open for 0% -> 0% of each run, Pallas kernels for 7% -> 5%
where the time goes in v3:
time: 113 us; the launch traced here: 112 us
  blocking collectives  52.1 us (46%)
  starting transfers between devices  32.7 us (29%)
  waiting for transfers between devices  13.9 us (12%)
  Pallas kernels  11.9 us (11%)
    all_to_all x3, blocking collectives, exchange(): return lax.all_to_all(rows, axis, split_axis=0, concat_axis=0, tiled=True)  52.1 us
    all_to_all x2, starting transfers between devices, exchange(): return lax.all_to_all(rows, axis, split_axis=0, concat_axis=0, tiled=True)  22.5 us
    all_to_all x2, waiting for transfers between devices, exchange(): return lax.all_to_all(rows, axis, split_axis=0, concat_axis=0, tiled=True)  12.7 us
    pallas_call x9, Pallas kernels, call(): pl.pallas_call(body, out_shape=outs, in_specs=[pl.BlockSpec(memory_space=...  11.9 us
    ppermute x2, starting transfers between devices, swap(): return lax.ppermute(rows, 'row', [(i, i ^ 1) for i in range(8)])  10.2 us
  transfers between devices with their start and end apart: 4, of which 3 were waited for; matrix products, arithmetic and copies ran while one was open for 0% of the time, Pallas kernels for 5%

profile of v3, /device:TPU:1, one launch (start us, length us, event | category | flops | bytes accessed | tf_op | source)
XLA Modules:
  0.0 112.4 jit_solution(5705062375962541911)
XLA Ops:
  0.6 1.9 %shard_map.76 = bf16[256,512]{1,0:T(8,128)(2,1)} custom-call(bf16[256,256]{1,0:T(8,128)(2,1)} %bitcast.29, bf16[256,256]{1,0:T(8,128)(2,1)} %bitcast.31), custom_call_target="tpu_custom_call" | custom-call | flops 67108864 | bytes 1048576 | tf_op jit(solution)/shard_map/pallas_call | solution.py:254
  2.6 0.0 copy-start
  2.6 10.3 %all-to-all-start.1 = ((bf16[16,16,512]{2,1,0:T(8,128)(2,1)}), bf16[16,16,512]{2,1,0:T(8,128)(2,1)S(1)}, u32[]{:S(2)}, u32[]{:S(2)}) async-start(bf16[16,16,512]{2,1,0:T(8,128)(2,1)} %bitcast.33), calls=%async_computation.1 | async-start | bytes 524288 | tf_op jit(solution)/shard_map/all_to_all | solution.py:270
  12.9 0.0 copy-done
  12.9 0.0 copy-start.1
  12.9 0.0 copy-start.2
  12.9 0.0 copy-start.3
  13.0 0.2 copy.8
  13.1 0.7 copy-done.1
  13.8 0.1 copy-done.2
  13.9 0.1 copy-done.3
  14.0 2.5 %shard_map.75 = (bf16[256,512]{1,0:T(8,128)(2,1)S(1)}, bf16[256,1024]{1,0:T(8,128)(2,1)S(1)}, bf16[256,512]{1,0:T(8,128)(2,1)}) custom-call(bf16[256,256]{1,0:T(8,128)(2,1)S(1)} %bitcast.30, bf16[256,256]{1,0:T(8,128)(2,1)S(1)} %bitcast.32, bf16[256,768]{1,0:T(8,128)(2,1)S(1)} %copy-done, bf16[768,256]{1,0:T(8,128)(2,1)S(1)} %bitcast.21, ...), custom_call_target="tpu_custom_call" | custom-call | flops 2348810240 | bytes 1048576 | tf_op jit(solution)/shard_map/pallas_call | solution.py:254
  16.5 3.7 %all-to-all-done.1 = bf16[16,16,512]{2,1,0:T(8,128)(2,1)S(1)} async-done(((bf16[16,16,512]{2,1,0:T(8,128)(2,1)}), bf16[16,16,512]{2,1,0:T(8,128)(2,1)S(1)}, u32[]{:S(2)}, u32[]{:S(2)}) %all-to-all-start.1) | async-done | bytes 262176 | tf_op jit(solution)/shard_map/all_to_all | solution.py:270
  20.2 12.1 %all-to-all-start = ((bf16[32,8,512]{2,1,0:T(8,128)(2,1)}), bf16[32,8,512]{2,1,0:T(8,128)(2,1)S(1)}, u32[]{:S(2)}, u32[]{:S(2)}) async-start(bf16[32,8,512]{2,1,0:T(8,128)(2,1)} %bitcast.3), calls=%async_computation | async-start | bytes 524288 | tf_op jit(solution)/shard_map/all_to_all | solution.py:270
  32.3 2.5 %shard_map.77 = (bf16[256,512]{1,0:T(8,128)(2,1)S(1)}, bf16[256,1024]{1,0:T(8,128)(2,1)S(1)}) custom-call(bf16[256,512]{1,0:T(8,128)(2,1)S(1)} %bitcast.24, bf16[256,768]{1,0:T(8,128)(2,1)S(1)} %copy-done, bf16[768,256]{1,0:T(8,128)(2,1)S(1)} %bitcast.22, bf16[256,256]{1,0:T(8,128)(2,1)S(1)} %copy-done.1, bf16[256,1024]{1,0:T(8,128)(2,1)S(1)} %get-tuple-element.18.grad_so_far), custom_call_target="tpu_custom_call" | custom-call | flops 2348810240 | bytes 1048576 | tf_op jit(solution)/shard_map/pallas_call | solution.py:254
  34.8 9.1 %all-to-all-done = bf16[32,8,512]{2,1,0:T(8,128)(2,1)S(1)} async-done(((bf16[32,8,512]{2,1,0:T(8,128)(2,1)}), bf16[32,8,512]{2,1,0:T(8,128)(2,1)S(1)}, u32[]{:S(2)}, u32[]{:S(2)}) %all-to-all-start) | async-done | bytes 262176 | tf_op jit(solution)/shard_map/all_to_all | solution.py:270
  43.9 2.6 %shard_map.78 = (bf16[256,512]{1,0:T(8,128)(2,1)S(1)}, f32[128,1024]{1,0:T(8,128)S(1)}, bf16[128,1024]{1,0:T(8,128)(2,1)S(1)}) custom-call(bf16[256,512]{1,0:T(8,128)(2,1)S(1)} %bitcast.25, bf16[256,768]{1,0:T(8,128)(2,1)S(1)} %copy-done, bf16[768,256]{1,0:T(8,128)(2,1)S(1)} %bitcast.23, bf16[256,256]{1,0:T(8,128)(2,1)S(1)} %copy-done.1, ...), custom_call_target="tpu_custom_call" | custom-call | flops 2348810240 | bytes 1048576 | tf_op jit(solution)/shard_map/pallas_call | solution.py:254
  46.6 5.1 %collective-permute-start = (bf16[128,1024]{1,0:T(8,128)(2,1)S(1)}, bf16[128,1024]{1,0:T(8,128)(2,1)S(1)}, u32[]{:S(2)}, u32[]{:S(2)}) collective-permute-start(bf16[128,1024]{1,0:T(8,128)(2,1)S(1)} %get-tuple-element.22), channel_id=1, source_target_pairs={{0,32},{32,0},{64,96},{96,64},{128,160},{160,128},{192,224},{224,1... | collective-permute-start | bytes 786440 | tf_op jit(solution)/shard_map/ppermute | solution.py:274
  51.6 1.1 %collective-permute-done.took = bf16[128,1024]{1,0:T(8,128)(2,1)S(1)} collective-permute-done((bf16[128,1024]{1,0:T(8,128)(2,1)S(1)}, bf16[128,1024]{1,0:T(8,128)(2,1)S(1)}, u32[]{:S(2)}, u32[]{:S(2)}) %collective-permute-start) | collective-permute-done | bytes 262176 | tf_op jit(solution)/shard_map/ppermute | solution.py:274
  52.8 0.1 shard_map.79
  52.8 21.9 %all_to_all.55 = bf16[32,8,1024]{2,1,0:T(8,128)(2,1)S(1)} all-to-all(bf16[32,8,1024]{2,1,0:T(8,128)(2,1)S(1)} %bitcast.17), channel_id=1, replica_groups=mesh['dp'=2,'row'=8,'col'=32] {'col'}, dimensions={0} | all-to-all | bytes 1048576 | tf_op jit(solution)/shard_map/all_to_all | solution.py:270
  74.8 0.1 shard_map.80
  74.8 13.4 %all_to_all.56 = bf16[16,16,768]{2,1,0:T(8,128)(2,1)S(1)} all-to-all(bf16[16,16,768]{2,1,0:T(8,128)(2,1)S(1)} %bitcast.20), channel_id=1, replica_groups=mesh['dp'=2,'row'=8,'col'=32] {'dp','row'}, dimensions={0} | all-to-all | bytes 786432 | tf_op jit(solution)/shard_map/all_to_all | solution.py:270
  88.3 16.8 %all_to_all.57 = bf16[32,16,256]{2,1,0:T(8,128)(2,1)S(1)} all-to-all(bf16[32,16,256]{2,1,0:T(8,128)(2,1)S(1)} %bitcast.28), channel_id=1, replica_groups=mesh['dp'=2,'row'=8,'col'=32] {'col'}, dimensions={0} | all-to-all | bytes 524288 | tf_op jit(solution)/shard_map/all_to_all | solution.py:270
  105.1 5.1 %collective-permute-start.1 = (bf16[512,256]{1,0:T(8,128)(2,1)S(1)}, bf16[512,256]{1,0:T(8,128)(2,1)S(1)}, u32[]{:S(2)}, u32[]{:S(2)}) collective-permute-start(bf16[512,256]{1,0:T(8,128)(2,1)S(1)} %bitcast.26), channel_id=1, source_target_pairs={{0,32},{32,0},{64,96},{96,64},{128,160},{160,128},{192,224},{224,1... | collective-permute-start | bytes 786440 | tf_op jit(solution)/shard_map/ppermute | solution.py:274
  110.2 1.1 shard_map.81
  111.3 0.0 collective-permute-done.1.other
  111.3 1.0 shard_map.83
  (1 shorter events, 0.0 us)
Async XLA Ops:
  2.6 10.4 %copy-start = (bf16[256,768]{1,0:T(8,128)(2,1)S(1)}, bf16[256,768]{1,0:T(8,128)(2,1)}, u32[]{:S(2)}) copy-start(bf16[256,768]{1,0:T(8,128)(2,1)} %w_qkv.5) | copy-start | bytes 1179652
  2.6 17.6 %all-to-all-start.1 = ((bf16[16,16,512]{2,1,0:T(8,128)(2,1)}), bf16[16,16,512]{2,1,0:T(8,128)(2,1)S(1)}, u32[]{:S(2)}, u32[]{:S(2)}) async-start(bf16[16,16,512]{2,1,0:T(8,128)(2,1)} %bitcast.33), calls=%async_computation.1 | async-start | bytes 524288 | tf_op jit(solution)/shard_map/all_to_all | solution.py:270
  12.9 0.9 copy-start.1
  12.9 1.0 copy-start.2
  12.9 1.0 copy-start.3
  20.2 23.8 %all-to-all-start = ((bf16[32,8,512]{2,1,0:T(8,128)(2,1)}), bf16[32,8,512]{2,1,0:T(8,128)(2,1)S(1)}, u32[]{:S(2)}, u32[]{:S(2)}) async-start(bf16[32,8,512]{2,1,0:T(8,128)(2,1)} %bitcast.3), calls=%async_computation | async-start | bytes 524288 | tf_op jit(solution)/shard_map/all_to_all | solution.py:270
  46.6 6.2 %collective-permute-start = (bf16[128,1024]{1,0:T(8,128)(2,1)S(1)}, bf16[128,1024]{1,0:T(8,128)(2,1)S(1)}, u32[]{:S(2)}, u32[]{:S(2)}) collective-permute-start(bf16[128,1024]{1,0:T(8,128)(2,1)S(1)} %get-tuple-element.22), channel_id=1, source_target_pairs={{0,32},{32,0},{64,96},{96,64},{128,160},{160,128},{192,224},{224,1... | collective-permute-start | bytes 786440 | tf_op jit(solution)/shard_map/ppermute | solution.py:274
  105.1 6.3 %collective-permute-start.1 = (bf16[512,256]{1,0:T(8,128)(2,1)S(1)}, bf16[512,256]{1,0:T(8,128)(2,1)S(1)}, u32[]{:S(2)}, u32[]{:S(2)}) collective-permute-start(bf16[512,256]{1,0:T(8,128)(2,1)S(1)} %bitcast.26), channel_id=1, source_target_pairs={{0,32},{32,0},{64,96},{96,64},{128,160},{160,128},{192,224},{224,1... | collective-permute-start | bytes 786440 | tf_op jit(solution)/shard_map/ppermute | solution.py:274

commit v4 on v3

--- a/solution.py
+++ b/solution.py
@@ -70,26 +70,32 @@
     out[:, C:] = nn(pick, cot).astype(BF)
 
 
-def pack_body(feat_hbm, cot_hbm, send_x, feat, cot, sem):
+def pack_body(feat_hbm, cot_hbm, send_x, feat, cot, sorted_rows, sem):
     copies = [
         pltpu.make_async_copy(feat_hbm, feat, sem.at[0]),
         pltpu.make_async_copy(cot_hbm, cot, sem.at[1]),
     ]
     for copy in copies:
         copy.start()
-    for copy in copies:
+    pick = onehot(x_source(iota(0)) == iota(1))
+    outs = []
+    for at, (copy, rows) in enumerate(zip(copies, (feat, cot))):
         copy.wait()
-    send(x_source, feat[...], cot[...], send_x)
+        cols = slice(at * C, (at + 1) * C)
+        sorted_rows[:, cols] = nn(pick, rows[...]).astype(BF)
+        outs.append(
+            pltpu.make_async_copy(sorted_rows.at[:, cols], send_x.at[:, cols], sem.at[2 + at])
+        )
+        outs[at].start()
+    for out in outs:
+        out.wait()
 
 
 def axis_math(source, line, feat, cot, w_qkv, w_qkv_t, w_out):
     scale = 1.0 / math.sqrt(DEPTH)
     eye = onehot(iota(0) == iota(1))
-    if source is None:
-        unsort = eye
-    else:
+    if source is not None:
         sort = onehot(source(iota(0)) == iota(1))
-        unsort = onehot(iota(0) == source(iota(1)))
         feat = nn(sort, feat).astype(BF)
         cot = nn(sort, cot).astype(BF)
     feat_t = nt(eye, feat).astype(BF)
@@ -162,27 +168,32 @@
 
     out_t, dq_t = whole(0, True), whole(1, True)
     dk, dv = whole(2, False), whole(3, False)
+    grads = (nt(feat_t, dq_t), nn(feat_t, dk), nn(feat_t, dv), nn(out_t, cot))
+    return (out_t, dq_t, dk, dv), grads
+
+
+def results(source, out_t, dq_t, dk, dv, w_qkv):
+    unsort = onehot(iota(0) == (iota(1) if source is None else source(iota(1))))
     out = nt(unsort, out_t).astype(BF)
-    dq = nt(eye, dq_t).astype(BF)
-    dfeat = (
-        nn(dq, w_qkv_t[:C]) + nn(dk, w_qkv_t[C : 2 * C]) + nn(dv, w_qkv_t[2 * C :])
+    dfeat_t = (
+        nn(w_qkv[:, :C], dq_t) + nt(w_qkv[:, C : 2 * C], dk) + nt(w_qkv[:, 2 * C :], dv)
     ).astype(BF)
-    if source is not None:
-        dfeat = nn(unsort, dfeat).astype(BF)
-    return out, dfeat, (nn(feat_t, dq), nn(feat_t, dk), nn(feat_t, dv), nn(out_t, cot))
+    return out, nt(unsort, dfeat_t).astype(BF)
 
 
 def z_body(feat, cot, w_qkv, w_qkv_t, w_out, back, grad, send_y):
     send(y_source, feat[...], cot[...], send_y)
-    back[:, :C], back[:, C:], terms = axis_math(None, z_line, feat[...], cot[...], w_qkv, w_qkv_t, w_out)
+    parts, terms = axis_math(None, z_line, feat[...], cot[...], w_qkv, w_qkv_t, w_out)
+    back[:, :C], back[:, C:] = results(None, *parts, w_qkv)
     for at, term in enumerate(terms):
         grad[:, at * C : (at + 1) * C] = term.astype(BF)
 
 
 def x_body(got, w_qkv, w_qkv_t, w_out, grad_so_far, back, grad):
-    back[:, :C], back[:, C:], terms = axis_math(
+    parts, terms = axis_math(
         x_sorted, long_line, got[:, :C], got[:, C:], w_qkv, w_qkv_t, w_out
     )
+    back[:, :C], back[:, C:] = results(x_sorted, *parts, w_qkv)
     for at, term in enumerate(terms):
         cols = slice(at * C, (at + 1) * C)
         grad[:, cols] = (grad_so_far[:, cols].astype(F32) + term).astype(BF)
@@ -192,16 +203,24 @@
     return lax.rem(lax.axis_index("row"), 2)
 
 
-def y_body(got, w_qkv, w_qkv_t, w_out, grad_so_far, back, keep, give, total):
-    back[:, :C], back[:, C:], terms = axis_math(
+def y_body(got, w_qkv, w_qkv_t, w_out, grad_so_far, out_t, dq_t, dk, dv, keep, give, total):
+    parts, terms = axis_math(
         y_sorted, long_line, got[:, :C], got[:, C:], w_qkv, w_qkv_t, w_out
     )
+    for ref, part in zip((out_t, dq_t, dk, dv), parts):
+        ref[...] = part
     for at, term in enumerate(terms):
         cols = slice(at * C, (at + 1) * C)
         total[:, cols] = grad_so_far[:, cols].astype(F32) + term
     mine = core()
     keep[...] = total[pl.ds(pl.multiple_of(mine * 128, 128), 128)]
     give[...] = total[pl.ds(pl.multiple_of((1 - mine) * 128, 128), 128)].astype(BF)
+
+
+def y_back_body(out_t, dq_t, dk, dv, w_qkv, back):
+    back[:, :C], back[:, C:] = results(
+        y_sorted, out_t[...], dq_t[...], dk[...], dv[...], w_qkv
+    )
 
 
 def col_pack_body(back_y, keep, took, send_col):
@@ -250,13 +269,12 @@
 
 
 def call(body, outs, flops, *args, space=pltpu.VMEM, scratch=(), grant=40 * 2**20):
-    vmem = pl.BlockSpec(memory_space=pltpu.VMEM)
     return pl.pallas_call(
         body,
         out_shape=outs,
         in_specs=[pl.BlockSpec(memory_space=space)] * len(args),
         scratch_shapes=scratch,
-        out_specs=[vmem] * len(outs),
+        out_specs=[pl.BlockSpec(memory_space=space)] * len(outs),
         compiler_params=pltpu.CompilerParams(vmem_limit_bytes=grant),
         cost_estimate=pl.CostEstimate(flops=flops, bytes_accessed=2**20, transcendentals=2**19),
     )(*args)
@@ -289,7 +307,12 @@
         feat,
         cot,
         space=pltpu.HBM,
-        scratch=[pltpu.VMEM((T, C), BF), pltpu.VMEM((T, C), BF), pltpu.SemaphoreType.DMA((2,))],
+        scratch=[
+            pltpu.VMEM((T, C), BF),
+            pltpu.VMEM((T, C), BF),
+            pltpu.VMEM((T, 2 * C), BF),
+            pltpu.SemaphoreType.DMA((4,)),
+        ],
         grant=None,
     )
     got_x = exchange(send_x, ("dp", "row"))
@@ -298,9 +321,9 @@
     )
     got_y = exchange(send_y, "col")
     back_x, grad = call(x_body, [back_shape, grad_shape], cube * 70, got_x, *weights, grad)
-    back_y, keep, give = call(
+    *parts, keep, give = call(
         y_body,
-        [back_shape, shape(128, 4 * C, F32), shape(128, 4 * C, BF)],
+        [shape(T, C, BF)] * 4 + [shape(128, 4 * C, F32), shape(128, 4 * C, BF)],
         cube * 70,
         got_y,
         *weights,
@@ -308,6 +331,7 @@
         scratch=[pltpu.VMEM((C, 4 * C), F32)],
     )
     took = swap(give)
+    (back_y,) = call(y_back_body, [back_shape], cube * 6, *parts, w_qkv)
     (send_col,) = call(col_pack_body, [shape(T, 4 * C, BF)], 2**20, back_y, keep, took)
     got_col = exchange(send_col, "col")
     (send_row,) = call(row_pack_body, [shape(T, 3 * C, BF)], 2**20, got_col, back_x)

time: 113 us -> 113 us (level)
    pallas_call x9 -> x10, Pallas kernels: 11.9 us -> 11.8 us  [call(): pl.pallas_call(body, out_shape=outs, in_specs=[pl.BlockSpec(memory_space=...]
  transfers between devices with their start and end apart: 4 -> 4, of which waited for: 3 -> 4; matrix products, arithmetic and copies ran while one was open for 0% -> 0% of each run, Pallas kernels for 5% -> 6%
where the time goes in v4:
time: 113 us; the launch traced here: 112 us
  blocking collectives  52.2 us (46%)
  starting transfers between devices  32.6 us (29%)
  waiting for transfers between devices  13.7 us (12%)
  Pallas kernels  11.8 us (10%)
    all_to_all x3, blocking collectives, exchange(): return lax.all_to_all(rows, axis, split_axis=0, concat_axis=0, tiled=True)  52.2 us
    all_to_all x2, starting transfers between devices, exchange(): return lax.all_to_all(rows, axis, split_axis=0, concat_axis=0, tiled=True)  22.5 us
    all_to_all x2, waiting for transfers between devices, exchange(): return lax.all_to_all(rows, axis, split_axis=0, concat_axis=0, tiled=True)  13.1 us
    pallas_call x10, Pallas kernels, call(): pl.pallas_call(body, out_shape=outs, in_specs=[pl.BlockSpec(memory_space=...  11.8 us
    ppermute x2, starting transfers between devices, swap(): return lax.ppermute(rows, 'row', [(i, i ^ 1) for i in range(8)])  10.2 us
  transfers between devices with their start and end apart: 4, of which 4 were waited for; matrix products, arithmetic and copies ran while one was open for 0% of the time, Pallas kernels for 6%

profile of v4, /device:TPU:1, one launch (start us, length us, event | category | flops | bytes accessed | tf_op | source)
XLA Modules:
  0.0 112.1 jit_solution(7028634004985903636)
XLA Ops:
  0.6 2.0 %shard_map.76 = bf16[256,512]{1,0:T(8,128)(2,1)} custom-call(bf16[256,256]{1,0:T(8,128)(2,1)} %bitcast.29, bf16[256,256]{1,0:T(8,128)(2,1)} %bitcast.31), custom_call_target="tpu_custom_call" | custom-call | flops 67108864 | bytes 1048576 | tf_op jit(solution)/shard_map/pallas_call | solution.py:272
  2.7 0.0 copy-start
  2.7 10.3 %all-to-all-start.1 = ((bf16[16,16,512]{2,1,0:T(8,128)(2,1)}), bf16[16,16,512]{2,1,0:T(8,128)(2,1)S(1)}, u32[]{:S(2)}, u32[]{:S(2)}) async-start(bf16[16,16,512]{2,1,0:T(8,128)(2,1)} %bitcast.33), calls=%async_computation.1 | async-start | bytes 524288 | tf_op jit(solution)/shard_map/all_to_all | solution.py:288
  13.0 0.0 copy-done
  13.0 0.0 copy-start.1
  13.0 0.0 copy-start.2
  13.1 0.0 copy-start.3
  13.1 0.2 copy.8
  13.2 0.7 copy-done.1
  13.9 0.1 copy-done.2
  14.0 0.1 copy-done.3
  14.1 2.3 %shard_map.75 = (bf16[256,512]{1,0:T(8,128)(2,1)S(1)}, bf16[256,1024]{1,0:T(8,128)(2,1)S(1)}, bf16[256,512]{1,0:T(8,128)(2,1)}) custom-call(bf16[256,256]{1,0:T(8,128)(2,1)S(1)} %bitcast.30, bf16[256,256]{1,0:T(8,128)(2,1)S(1)} %bitcast.32, bf16[256,768]{1,0:T(8,128)(2,1)S(1)} %copy-done, bf16[768,256]{1,0:T(8,128)(2,1)S(1)} %bitcast.21, ...), custom_call_target="tpu_custom_call" | custom-call | flops 2348810240 | bytes 1048576 | tf_op jit(solution)/shard_map/pallas_call | solution.py:272
  16.4 3.9 %all-to-all-done.1 = bf16[16,16,512]{2,1,0:T(8,128)(2,1)S(1)} async-done(((bf16[16,16,512]{2,1,0:T(8,128)(2,1)}), bf16[16,16,512]{2,1,0:T(8,128)(2,1)S(1)}, u32[]{:S(2)}, u32[]{:S(2)}) %all-to-all-start.1) | async-done | bytes 262176 | tf_op jit(solution)/shard_map/all_to_all | solution.py:288
  20.3 12.1 %all-to-all-start = ((bf16[32,8,512]{2,1,0:T(8,128)(2,1)}), bf16[32,8,512]{2,1,0:T(8,128)(2,1)S(1)}, u32[]{:S(2)}, u32[]{:S(2)}) async-start(bf16[32,8,512]{2,1,0:T(8,128)(2,1)} %bitcast.3), calls=%async_computation | async-start | bytes 524288 | tf_op jit(solution)/shard_map/all_to_all | solution.py:288
  32.4 2.4 %shard_map.77 = (bf16[256,512]{1,0:T(8,128)(2,1)S(1)}, bf16[256,1024]{1,0:T(8,128)(2,1)S(1)}) custom-call(bf16[256,512]{1,0:T(8,128)(2,1)S(1)} %bitcast.24, bf16[256,768]{1,0:T(8,128)(2,1)S(1)} %copy-done, bf16[768,256]{1,0:T(8,128)(2,1)S(1)} %bitcast.22, bf16[256,256]{1,0:T(8,128)(2,1)S(1)} %copy-done.1, bf16[256,1024]{1,0:T(8,128)(2,1)S(1)} %get-tuple-element.21.grad_so_far), custom_call_target="tpu_custom_call" | custom-call | flops 2348810240 | bytes 1048576 | tf_op jit(solution)/shard_map/pallas_call | solution.py:272
  34.8 9.2 %all-to-all-done = bf16[32,8,512]{2,1,0:T(8,128)(2,1)S(1)} async-done(((bf16[32,8,512]{2,1,0:T(8,128)(2,1)}), bf16[32,8,512]{2,1,0:T(8,128)(2,1)S(1)}, u32[]{:S(2)}, u32[]{:S(2)}) %all-to-all-start) | async-done | bytes 262176 | tf_op jit(solution)/shard_map/all_to_all | solution.py:288
  44.0 2.2 %shard_map.78 = (bf16[256,256]{1,0:T(8,128)(2,1)S(1)}, bf16[256,256]{1,0:T(8,128)(2,1)S(1)}, bf16[256,256]{1,0:T(8,128)(2,1)S(1)}, bf16[256,256]{1,0:T(8,128)(2,...) custom-call(bf16[256,512]{1,0:T(8,128)(2,1)S(1)} %bitcast.25, bf16[256,768]{1,0:T(8,128)(2,1)S(1)} %copy-done, ...), custom_call_target="tpu_custom_call" | custom-call | flops 2348810240 | bytes 1048576 | tf_op jit(solution)/shard_map/pallas_call | solution.py:272
  46.3 5.0 %collective-permute-start = (bf16[128,1024]{1,0:T(8,128)(2,1)S(1)}, bf16[128,1024]{1,0:T(8,128)(2,1)S(1)}, u32[]{:S(2)}, u32[]{:S(2)}) collective-permute-start(bf16[128,1024]{1,0:T(8,128)(2,1)S(1)} %get-tuple-element.28), channel_id=1, source_target_pairs={{0,32},{32,0},{64,96},{96,64},{128,160},{160,128},{192,224},{224,1... | collective-permute-start | bytes 786440 | tf_op jit(solution)/shard_map/ppermute | solution.py:292
  51.3 0.6 shard_map.79.back_y
  51.9 0.6 collective-permute-done.took
  52.4 0.1 shard_map.80
  52.5 21.9 %all_to_all.55 = bf16[32,8,1024]{2,1,0:T(8,128)(2,1)S(1)} all-to-all(bf16[32,8,1024]{2,1,0:T(8,128)(2,1)S(1)} %bitcast.17), channel_id=1, replica_groups=mesh['dp'=2,'row'=8,'col'=32] {'col'}, dimensions={0} | all-to-all | bytes 1048576 | tf_op jit(solution)/shard_map/all_to_all | solution.py:288
  74.5 0.1 shard_map.81
  74.5 13.4 %all_to_all.56 = bf16[16,16,768]{2,1,0:T(8,128)(2,1)S(1)} all-to-all(bf16[16,16,768]{2,1,0:T(8,128)(2,1)S(1)} %bitcast.20), channel_id=1, replica_groups=mesh['dp'=2,'row'=8,'col'=32] {'dp','row'}, dimensions={0} | all-to-all | bytes 786432 | tf_op jit(solution)/shard_map/all_to_all | solution.py:288
  88.0 16.8 %all_to_all.57 = bf16[32,16,256]{2,1,0:T(8,128)(2,1)S(1)} all-to-all(bf16[32,16,256]{2,1,0:T(8,128)(2,1)S(1)} %bitcast.28), channel_id=1, replica_groups=mesh['dp'=2,'row'=8,'col'=32] {'col'}, dimensions={0} | all-to-all | bytes 524288 | tf_op jit(solution)/shard_map/all_to_all | solution.py:288
  104.8 5.1 %collective-permute-start.1 = (bf16[512,256]{1,0:T(8,128)(2,1)S(1)}, bf16[512,256]{1,0:T(8,128)(2,1)S(1)}, u32[]{:S(2)}, u32[]{:S(2)}) collective-permute-start(bf16[512,256]{1,0:T(8,128)(2,1)S(1)} %bitcast.26), channel_id=1, source_target_pairs={{0,32},{32,0},{64,96},{96,64},{128,160},{160,128},{192,224},{224,1... | collective-permute-start | bytes 786440 | tf_op jit(solution)/shard_map/ppermute | solution.py:292
  109.9 1.1 shard_map.82
  111.0 0.1 collective-permute-done.1.other
  111.0 1.0 shard_map.84
  (1 shorter events, 0.0 us)
Async XLA Ops:
  2.7 10.4 %copy-start = (bf16[256,768]{1,0:T(8,128)(2,1)S(1)}, bf16[256,768]{1,0:T(8,128)(2,1)}, u32[]{:S(2)}) copy-start(bf16[256,768]{1,0:T(8,128)(2,1)} %w_qkv.7) | copy-start | bytes 1179652
  2.7 17.6 %all-to-all-start.1 = ((bf16[16,16,512]{2,1,0:T(8,128)(2,1)}), bf16[16,16,512]{2,1,0:T(8,128)(2,1)S(1)}, u32[]{:S(2)}, u32[]{:S(2)}) async-start(bf16[16,16,512]{2,1,0:T(8,128)(2,1)} %bitcast.33), calls=%async_computation.1 | async-start | bytes 524288 | tf_op jit(solution)/shard_map/all_to_all | solution.py:288
  13.0 0.9 copy-start.1
  13.0 1.0 copy-start.2
  13.1 1.0 copy-start.3
  20.3 23.8 %all-to-all-start = ((bf16[32,8,512]{2,1,0:T(8,128)(2,1)}), bf16[32,8,512]{2,1,0:T(8,128)(2,1)S(1)}, u32[]{:S(2)}, u32[]{:S(2)}) async-start(bf16[32,8,512]{2,1,0:T(8,128)(2,1)} %bitcast.3), calls=%async_computation | async-start | bytes 524288 | tf_op jit(solution)/shard_map/all_to_all | solution.py:288
  46.3 6.2 %collective-permute-start = (bf16[128,1024]{1,0:T(8,128)(2,1)S(1)}, bf16[128,1024]{1,0:T(8,128)(2,1)S(1)}, u32[]{:S(2)}, u32[]{:S(2)}) collective-permute-start(bf16[128,1024]{1,0:T(8,128)(2,1)S(1)} %get-tuple-element.28), channel_id=1, source_target_pairs={{0,32},{32,0},{64,96},{96,64},{128,160},{160,128},{192,224},{224,1... | collective-permute-start | bytes 786440 | tf_op jit(solution)/shard_map/ppermute | solution.py:292
  104.8 6.3 %collective-permute-start.1 = (bf16[512,256]{1,0:T(8,128)(2,1)S(1)}, bf16[512,256]{1,0:T(8,128)(2,1)S(1)}, u32[]{:S(2)}, u32[]{:S(2)}) collective-permute-start(bf16[512,256]{1,0:T(8,128)(2,1)S(1)} %bitcast.26), channel_id=1, source_target_pairs={{0,32},{32,0},{64,96},{96,64},{128,160},{160,128},{192,224},{224,1... | collective-permute-start | bytes 786440 | tf_op jit(solution)/shard_map/ppermute | solution.py:292

commit v5 on v4

--- a/solution.py
+++ b/solution.py
@@ -35,21 +35,23 @@
     return lax.broadcasted_iota(jnp.int32, shape, axis)
 
 
-def y_source(r):
-    return ((r // LINES) % 2) * 128 + (r // 8) * LINES + r % LINES
-
-
 def x_source(r):
-    peer = r // 16
-    return (peer // 8) * 128 + (r % 8) * 16 + (peer % 8) * 2 + (r // 8) % 2
-
-
-def y_sorted(r):
-    return (r % 64) * LINES + r // 64
-
-
-def x_sorted(r):
-    return r // 128 * 128 + (r % 64) // 8 * 16 + (r // 64) % 2 * 8 + r % 8
+    peer = r // 32
+    return (peer // 4) * 128 + (r % 8) * Z + (peer % 4) * LINES + (r // 8) % LINES
+
+
+def x_sorted(t):
+    return (t % 64) // 8 * 32 + t // 64 * 8 + t % 8
+
+
+def y_row(t):
+    at = t % 128
+    return at // 2 * 8 + t // 128 * 2 + at % 2
+
+
+def y_sorted(t):
+    at = t % 64
+    return t // 128 * 256 + at // 2 * 8 + at % 2 * 2 + t // 64 % 2
 
 
 def z_line(r):
@@ -62,12 +64,6 @@
 
 def onehot(hit):
     return jnp.where(hit, 1.0, 0.0).astype(BF)
-
-
-def send(source, feat, cot, out):
-    pick = onehot(source(iota(0)) == iota(1))
-    out[:, :C] = nn(pick, feat).astype(BF)
-    out[:, C:] = nn(pick, cot).astype(BF)
 
 
 def pack_body(feat_hbm, cot_hbm, send_x, feat, cot, sorted_rows, sem):
@@ -91,19 +87,13 @@
         out.wait()
 
 
-def axis_math(source, line, feat, cot, w_qkv, w_qkv_t, w_out):
+def axis_math(line, feat, cot, w_qkv, w_qkv_t, w_out):
     scale = 1.0 / math.sqrt(DEPTH)
-    eye = onehot(iota(0) == iota(1))
-    if source is not None:
-        sort = onehot(source(iota(0)) == iota(1))
-        feat = nn(sort, feat).astype(BF)
-        cot = nn(sort, cot).astype(BF)
-    feat_t = nt(eye, feat).astype(BF)
-    cot_t = nt(eye, cot).astype(BF)
+    feat_t = nt(onehot(iota(0) == iota(1)), feat).astype(BF)
     proj = nn(feat, w_qkv[...]).astype(BF)
-    proj_t = nn(w_qkv_t[...], feat_t).astype(BF)
+    proj_t = nt(w_qkv_t[...], feat).astype(BF)
     gmix = nt(cot, w_out[...]).astype(BF)
-    gmix_t = nn(w_out[...], cot_t).astype(BF)
+    gmix_t = nt(w_out[...], cot).astype(BF)
     q, k, v = proj[:, :C], proj[:, C : 2 * C], proj[:, 2 * C :]
     q_t, k_t, v_t = proj_t[:C], proj_t[C : 2 * C], proj_t[2 * C :]
     wide = (HALF, QUAD * HALF)
@@ -172,28 +162,33 @@
     return (out_t, dq_t, dk, dv), grads
 
 
-def results(source, out_t, dq_t, dk, dv, w_qkv):
-    unsort = onehot(iota(0) == (iota(1) if source is None else source(iota(1))))
-    out = nt(unsort, out_t).astype(BF)
-    dfeat_t = (
-        nn(w_qkv[:, :C], dq_t) + nt(w_qkv[:, C : 2 * C], dk) + nt(w_qkv[:, 2 * C :], dv)
+def results(out_t, dq_t, dk, dv, w_qkv):
+    dfeat_t = nn(w_qkv[:, :C], dq_t) + nt(w_qkv[:, C : 2 * C], dk) + nt(w_qkv[:, 2 * C :], dv)
+    return out_t, dfeat_t.astype(BF)
+
+
+def z_body(feat, cot, w_qkv, w_qkv_t, w_out, back, grad, send_y):
+    wide = (2 * T, T)
+    row = y_row(iota(1, wide))
+    send_y[...] = (
+        nn(onehot(iota(0, wide) == row), feat[...]) + nn(onehot(iota(0, wide) == row + 4), cot[...])
     ).astype(BF)
-    return out, nt(unsort, dfeat_t).astype(BF)
-
-
-def z_body(feat, cot, w_qkv, w_qkv_t, w_out, back, grad, send_y):
-    send(y_source, feat[...], cot[...], send_y)
-    parts, terms = axis_math(None, z_line, feat[...], cot[...], w_qkv, w_qkv_t, w_out)
-    back[:, :C], back[:, C:] = results(None, *parts, w_qkv)
+    parts, terms = axis_math(z_line, feat[...], cot[...], w_qkv, w_qkv_t, w_out)
+    eye = onehot(iota(0) == iota(1))
+    for at, part_t in enumerate(results(*parts, w_qkv)):
+        back[:, at * C : (at + 1) * C] = nt(eye, part_t).astype(BF)
     for at, term in enumerate(terms):
         grad[:, at * C : (at + 1) * C] = term.astype(BF)
 
 
 def x_body(got, w_qkv, w_qkv_t, w_out, grad_so_far, back, grad):
-    parts, terms = axis_math(
-        x_sorted, long_line, got[:, :C], got[:, C:], w_qkv, w_qkv_t, w_out
-    )
-    back[:, :C], back[:, C:] = results(x_sorted, *parts, w_qkv)
+    sort = onehot(x_sorted(iota(0)) == iota(1))
+    feat = nn(sort, got[:, :C]).astype(BF)
+    cot = nn(sort, got[:, C:]).astype(BF)
+    parts, terms = axis_math(long_line, feat, cot, w_qkv, w_qkv_t, w_out)
+    unsort = onehot(iota(0) == x_sorted(iota(1)))
+    for at, part_t in enumerate(results(*parts, w_qkv)):
+        back[:, at * C : (at + 1) * C] = nt(unsort, part_t).astype(BF)
     for at, term in enumerate(terms):
         cols = slice(at * C, (at + 1) * C)
         grad[:, cols] = (grad_so_far[:, cols].astype(F32) + term).astype(BF)
@@ -204,9 +199,11 @@
 
 
 def y_body(got, w_qkv, w_qkv_t, w_out, grad_so_far, out_t, dq_t, dk, dv, keep, give, total):
-    parts, terms = axis_math(
-        y_sorted, long_line, got[:, :C], got[:, C:], w_qkv, w_qkv_t, w_out
-    )
+    wide = (T, 2 * T)
+    row = y_sorted(iota(0, wide))
+    feat = nn(onehot(row == iota(1, wide)), got[...]).astype(BF)
+    cot = nn(onehot(row + 4 == iota(1, wide)), got[...]).astype(BF)
+    parts, terms = axis_math(long_line, feat, cot, w_qkv, w_qkv_t, w_out)
     for ref, part in zip((out_t, dq_t, dk, dv), parts):
         ref[...] = part
     for at, term in enumerate(terms):
@@ -218,54 +215,62 @@
 
 
 def y_back_body(out_t, dq_t, dk, dv, w_qkv, back):
-    back[:, :C], back[:, C:] = results(
-        y_sorted, out_t[...], dq_t[...], dk[...], dv[...], w_qkv
-    )
+    out_t, dfeat_t = results(out_t[...], dq_t[...], dk[...], dv[...], w_qkv)
+    wide = (2 * T, T)
+    row = y_sorted(iota(1, wide))
+    back[...] = (
+        nt(onehot(iota(0, wide) == row), out_t) + nt(onehot(iota(0, wide) == row + 4), dfeat_t)
+    ).astype(BF)
 
 
 def col_pack_body(back_y, keep, took, send_col):
-    send_col[:, : 2 * C] = back_y[...]
+    send_col[:, :C] = back_y[...]
     half = (keep[...] + took[...].astype(F32)).astype(BF)
-    send_col[:128, 2 * C :] = half[:, : 2 * C]
-    send_col[128:, 2 * C :] = half[:, 2 * C :]
+    for at in range(4):
+        send_col[at * 128 : (at + 1) * 128, C:] = half[:, at * C : (at + 1) * C]
 
 
 def row_pack_body(got_col, back_x, send_row):
     send_row[:, : 2 * C] = back_x[...]
-    block = jnp.sum(got_col[:, 2 * C :].astype(F32).reshape(32, 8, 2 * C), axis=0)
-    block = jnp.concatenate([block[:, :C], block[:, C:]], axis=0)
+    block = jnp.sum(got_col[:, C:].astype(F32).reshape(64, 8, C), axis=0)
+    block = jnp.concatenate([block[:, :128], block[:, 128:]], axis=0)
     send_row[:, 2 * C :] = jnp.concatenate([block] * 16, axis=0).astype(BF)
 
 
 def last_pack_body(factor, got_row, send):
     mine = core()
-    block = jnp.zeros((16, C), F32)
-    for peer in range(8):
-        at = pl.multiple_of((2 * peer + mine) * 16, 16)
+    block = jnp.zeros((16, 128), F32)
+    for peer in range(4):
+        at = pl.multiple_of((2 * peer + mine) * 32, 32)
         block += got_row[pl.ds(at, 16), 2 * C :].astype(F32)
-    send[...] = jnp.concatenate([block * factor] * 32, axis=0).astype(BF)
-
-
-def final_body(back_z, back_y, back_x, w_out, update, grad_in):
-    put_y = onehot(iota(0) == y_source(iota(1)))
+    block = jnp.concatenate([block[:8], block[8:]], axis=1) * factor
+    send[...] = jnp.concatenate([block] * 64, axis=0).astype(BF)
+
+
+def final_body(back_z, got_col, got_row, w_out, update, grad_in):
+    wide = (T, 2 * T)
+    row = y_row(iota(0, wide))
+    back_y = got_col[:, :C]
     put_x = onehot(iota(0) == x_source(iota(1)))
-    total = (
-        back_z[...].astype(F32) + nn(put_y, back_y[:, : 2 * C]) + nn(put_x, back_x[:, : 2 * C])
+    mix = (
+        back_z[:, :C].astype(F32)
+        + nn(onehot(row == iota(1, wide)), back_y)
+        + nn(put_x, got_row[:, :C])
     ).astype(BF)
-    update[...] = nn(total[:, :C], w_out[...]).astype(BF)
-    grad_in[...] = total[:, C:]
+    update[...] = nn(mix, w_out[...]).astype(BF)
+    grad_in[...] = (
+        back_z[:, C:].astype(F32)
+        + nn(onehot(row + 4 == iota(1, wide)), back_y)
+        + nn(put_x, got_row[:, C : 2 * C])
+    ).astype(BF)
 
 
 def unpack_body(mine, other, grad_qkv, grad_out):
     for src, half in ((mine, core()), (other, 1 - core())):
         rows = pl.ds(pl.multiple_of(half * 128, 128), 128)
-        tiles = src[...].astype(F32).reshape(2, 16, 2, 8, C)
-        for at in range(4):
-            block = tiles[at // 2, :, at % 2].reshape(128, C)
-            if at < 3:
-                grad_qkv[rows, at * C : (at + 1) * C] = block
-            else:
-                grad_out[rows, :] = block
+        for at in range(3):
+            grad_qkv[rows, at * C : (at + 1) * C] = src[at * 128 : (at + 1) * 128].astype(F32)
+        grad_out[rows, :] = src[3 * 128 :].astype(F32)
 
 
 def call(body, outs, flops, *args, space=pltpu.VMEM, scratch=(), grant=40 * 2**20):
@@ -315,11 +320,11 @@
         ],
         grant=None,
     )
-    got_x = exchange(send_x, ("dp", "row"))
+    got_x = exchange(send_x, "row")
     back_z, grad, send_y = call(
-        z_body, [back_shape, grad_shape, back_shape], cube * 70, feat, cot, *weights
-    )
-    got_y = exchange(send_y, "col")
+        z_body, [back_shape, grad_shape, shape(2 * T, C, BF)], cube * 70, feat, cot, *weights
+    )
+    got_y = exchange(send_y, ("dp", "col"))
     back_x, grad = call(x_body, [back_shape, grad_shape], cube * 70, got_x, *weights, grad)
     *parts, keep, give = call(
         y_body,
@@ -331,16 +336,16 @@
         scratch=[pltpu.VMEM((C, 4 * C), F32)],
     )
     took = swap(give)
-    (back_y,) = call(y_back_body, [back_shape], cube * 6, *parts, w_qkv)
-    (send_col,) = call(col_pack_body, [shape(T, 4 * C, BF)], 2**20, back_y, keep, took)
-    got_col = exchange(send_col, "col")
-    (send_row,) = call(row_pack_body, [shape(T, 3 * C, BF)], 2**20, got_col, back_x)
-    got_row = exchange(send_row, ("dp", "row"))
+    (back_y,) = call(y_back_body, [shape(2 * T, C, BF)], cube * 8, *parts, w_qkv)
+    (send_col,) = call(col_pack_body, [shape(2 * T, 2 * C, BF)], 2**20, back_y, keep, took)
+    got_col = exchange(send_col, ("dp", "col"))
+    (send_row,) = call(row_pack_body, [shape(T, 2 * C + 128, BF)], 2**20, got_col, back_x)
+    got_row = exchange(send_row, "row")
     factor = 1.0 / math.sqrt(PATCHES * 64 * 64 * 16)
     (send_last,) = call(
         functools.partial(last_pack_body, factor), [shape(512, C, BF)], 2**20, got_row
     )
-    mine = exchange(send_last, "col")
+    mine = exchange(send_last, ("dp", "col"))
     update, grad_in = call(
         final_body, [shape(T, C, BF)] * 2, cube * 6, back_z, got_col, got_row, w_out
     )

time: 113 us -> 111 us (0.982)
  waiting for transfers between devices: 13.7 us -> 12.3 us
    all_to_all x2, waiting for transfers between devices: 13.1 us -> 11.9 us  [exchange(): return lax.all_to_all(rows, axis, split_axis=0, concat_axis=0, tiled=True)]
  transfers between devices with their start and end apart: 4 -> 4, of which waited for: 4 -> 3; matrix products, arithmetic and copies ran while one was open for 0% -> 0% of each run, Pallas kernels for 6% -> 6%
where the time goes in v5:
time: 111 us
  blocking collectives  51.1 us (46%)
  starting transfers between devices  32.7 us (29%)
  Pallas kernels  12.7 us (11%)
  waiting for transfers between devices  12.3 us (11%)
    all_to_all x3, blocking collectives, exchange(): return lax.all_to_all(rows, axis, split_axis=0, concat_axis=0, tiled=True)  51.1 us
    all_to_all x2, starting transfers between devices, exchange(): return lax.all_to_all(rows, axis, split_axis=0, concat_axis=0, tiled=True)  22.2 us
    pallas_call x10, Pallas kernels, call(): pl.pallas_call(body, out_shape=outs, in_specs=[pl.BlockSpec(memory_space=...  12.7 us
    all_to_all x2, waiting for transfers between devices, exchange(): return lax.all_to_all(rows, axis, split_axis=0, concat_axis=0, tiled=True)  11.9 us
    ppermute x2, starting transfers between devices, swap(): return lax.ppermute(rows, 'row', [(i, i ^ 1) for i in range(8)])  10.5 us
  transfers between devices with their start and end apart: 4, of which 3 were waited for; matrix products, arithmetic and copies ran while one was open for 0% of the time, Pallas kernels for 6%

profile of v5, /device:TPU:1, one launch (start us, length us, event | category | flops | bytes accessed | tf_op | source)
XLA Modules:
  0.0 110.5 jit_solution(819842144626246438)
XLA Ops:
  0.6 2.0 %shard_map.76 = bf16[256,512]{1,0:T(8,128)(2,1)} custom-call(bf16[256,256]{1,0:T(8,128)(2,1)} %bitcast.29, bf16[256,256]{1,0:T(8,128)(2,1)} %bitcast.31), custom_call_target="tpu_custom_call" | custom-call | flops 67108864 | bytes 1048576 | tf_op jit(solution)/shard_map/pallas_call | solution.py:277
  2.7 0.0 copy-start
  2.7 10.3 %all-to-all-start.1 = ((bf16[8,32,512]{2,1,0:T(8,128)(2,1)}), bf16[8,32,512]{2,1,0:T(8,128)(2,1)S(1)}, u32[]{:S(2)}, u32[]{:S(2)}) async-start(bf16[8,32,512]{2,1,0:T(8,128)(2,1)} %bitcast.33), calls=%async_computation.1 | async-start | bytes 524288 | tf_op jit(solution)/shard_map/all_to_all | solution.py:293
  13.0 0.0 copy-done
  13.0 0.0 copy-start.1
  13.0 0.0 copy-start.2
  13.0 0.0 copy-start.3
  13.0 0.2 copy.8
  13.2 0.7 copy-done.1
  13.9 0.1 copy-done.2
  14.0 0.1 copy-done.3
  14.0 2.7 %shard_map.75 = (bf16[256,512]{1,0:T(8,128)(2,1)S(1)}, bf16[256,1024]{1,0:T(8,128)(2,1)S(1)}, bf16[512,256]{1,0:T(8,128)(2,1)}) custom-call(bf16[256,256]{1,0:T(8,128)(2,1)S(1)} %bitcast.30, bf16[256,256]{1,0:T(8,128)(2,1)S(1)} %bitcast.32, bf16[256,768]{1,0:T(8,128)(2,1)S(1)} %copy-done, bf16[768,256]{1,0:T(8,128)(2,1)S(1)} %bitcast.21, ...), custom_call_target="tpu_custom_call" | custom-call | flops 2348810240 | bytes 1048576 | tf_op jit(solution)/shard_map/pallas_call | solution.py:277
  16.7 2.8 %all-to-all-done.1 = bf16[8,32,512]{2,1,0:T(8,128)(2,1)S(1)} async-done(((bf16[8,32,512]{2,1,0:T(8,128)(2,1)}), bf16[8,32,512]{2,1,0:T(8,128)(2,1)S(1)}, u32[]{:S(2)}, u32[]{:S(2)}) %all-to-all-start.1) | async-done | bytes 262176 | tf_op jit(solution)/shard_map/all_to_all | solution.py:293
  19.5 11.9 %all-to-all-start = ((bf16[64,8,256]{2,1,0:T(8,128)(2,1)}), bf16[64,8,256]{2,1,0:T(8,128)(2,1)S(1)}, u32[]{:S(2)}, u32[]{:S(2)}) async-start(bf16[64,8,256]{2,1,0:T(8,128)(2,1)} %bitcast.3), calls=%async_computation | async-start | bytes 524288 | tf_op jit(solution)/shard_map/all_to_all | solution.py:293
  31.4 2.4 %shard_map.77 = (bf16[256,512]{1,0:T(8,128)(2,1)S(1)}, bf16[256,1024]{1,0:T(8,128)(2,1)S(1)}) custom-call(bf16[256,512]{1,0:T(8,128)(2,1)S(1)} %bitcast.24, bf16[256,768]{1,0:T(8,128)(2,1)S(1)} %copy-done, bf16[768,256]{1,0:T(8,128)(2,1)S(1)} %bitcast.22, bf16[256,256]{1,0:T(8,128)(2,1)S(1)} %copy-done.1, bf16[256,1024]{1,0:T(8,128)(2,1)S(1)} %get-tuple-element.21.grad_so_far), custom_call_target="tpu_custom_call" | custom-call | flops 2348810240 | bytes 1048576 | tf_op jit(solution)/shard_map/pallas_call | solution.py:277
  33.8 9.1 %all-to-all-done = bf16[64,8,256]{2,1,0:T(8,128)(2,1)S(1)} async-done(((bf16[64,8,256]{2,1,0:T(8,128)(2,1)}), bf16[64,8,256]{2,1,0:T(8,128)(2,1)S(1)}, u32[]{:S(2)}, u32[]{:S(2)}) %all-to-all-start) | async-done | bytes 262176 | tf_op jit(solution)/shard_map/all_to_all | solution.py:293
  42.9 2.3 %shard_map.78 = (bf16[256,256]{1,0:T(8,128)(2,1)S(1)}, bf16[256,256]{1,0:T(8,128)(2,1)S(1)}, bf16[256,256]{1,0:T(8,128)(2,1)S(1)}, bf16[256,256]{1,0:T(8,128)(2,...) custom-call(bf16[512,256]{1,0:T(8,128)(2,1)S(1)} %bitcast.25, bf16[256,768]{1,0:T(8,128)(2,1)S(1)} %copy-done, ...), custom_call_target="tpu_custom_call" | custom-call | flops 2348810240 | bytes 1048576 | tf_op jit(solution)/shard_map/pallas_call | solution.py:277
  45.2 5.2 %collective-permute-start = (bf16[128,1024]{1,0:T(8,128)(2,1)S(1)}, bf16[128,1024]{1,0:T(8,128)(2,1)S(1)}, u32[]{:S(2)}, u32[]{:S(2)}) collective-permute-start(bf16[128,1024]{1,0:T(8,128)(2,1)S(1)} %get-tuple-element.28), channel_id=1, source_target_pairs={{0,32},{32,0},{64,96},{96,64},{128,160},{160,128},{192,224},{224,1... | collective-permute-start | bytes 786440 | tf_op jit(solution)/shard_map/ppermute | solution.py:297
  50.4 0.7 shard_map.79.back_y
  51.2 0.4 collective-permute-done.took
  51.6 0.1 shard_map.80
  51.6 21.4 %all_to_all.55 = bf16[64,8,512]{2,1,0:T(8,128)(2,1)S(1)} all-to-all(bf16[64,8,512]{2,1,0:T(8,128)(2,1)S(1)} %bitcast.17), channel_id=1, replica_groups=mesh['dp'=2,'row'=8,'col'=32] {'dp','col'}, dimensions={0} | all-to-all | bytes 1048576 | tf_op jit(solution)/shard_map/all_to_all | solution.py:293
  73.1 0.1 shard_map.81
  73.2 12.4 %all_to_all.56 = bf16[8,32,640]{2,1,0:T(8,128)(2,1)S(1)} all-to-all(bf16[8,32,640]{2,1,0:T(8,128)(2,1)S(1)} %bitcast.20), channel_id=1, replica_groups=mesh['dp'=2,'row'=8,'col'=32] {'row'}, dimensions={0} | all-to-all | bytes 655360 | tf_op jit(solution)/shard_map/all_to_all | solution.py:293
  85.6 17.3 %all_to_all.57 = bf16[64,8,256]{2,1,0:T(8,128)(2,1)S(1)} all-to-all(bf16[64,8,256]{2,1,0:T(8,128)(2,1)S(1)} %bitcast.28), channel_id=1, replica_groups=mesh['dp'=2,'row'=8,'col'=32] {'dp','col'}, dimensions={0} | all-to-all | bytes 524288 | tf_op jit(solution)/shard_map/all_to_all | solution.py:293
  102.9 5.3 %collective-permute-start.1 = (bf16[512,256]{1,0:T(8,128)(2,1)S(1)}, bf16[512,256]{1,0:T(8,128)(2,1)S(1)}, u32[]{:S(2)}, u32[]{:S(2)}) collective-permute-start(bf16[512,256]{1,0:T(8,128)(2,1)S(1)} %bitcast.26), channel_id=1, source_target_pairs={{0,32},{32,0},{64,96},{96,64},{128,160},{160,128},{192,224},{224,1... | collective-permute-start | bytes 786440 | tf_op jit(solution)/shard_map/ppermute | solution.py:297
  108.1 1.3 %shard_map.82 = (bf16[256,256]{1,0:T(8,128)(2,1)}, bf16[256,256]{1,0:T(8,128)(2,1)}) custom-call(bf16[256,512]{1,0:T(8,128)(2,1)S(1)} %get-tuple-element.19.back_z, bf16[512,512]{1,0:T(8,128)(2,1)S(1)} %bitcast.16, bf16[256,640]{1,0:T(8,128)(2,1)S(1)} %bitcast.19, bf16[256,256]{1,0:T(8,128)(2,1)S(1)} %copy-done.1), custom_call_target="tpu_custom_call" | custom-call | flops 201326592 | bytes 1048576 | tf_op jit(solution)/shard_map/pallas_call | solution.py:277
  109.5 0.0 collective-permute-done.1.other
  109.5 1.0 shard_map.84
  (1 shorter events, 0.0 us)
Async XLA Ops:
  2.7 10.3 %copy-start = (bf16[256,768]{1,0:T(8,128)(2,1)S(1)}, bf16[256,768]{1,0:T(8,128)(2,1)}, u32[]{:S(2)}) copy-start(bf16[256,768]{1,0:T(8,128)(2,1)} %w_qkv.7) | copy-start | bytes 1179652
  2.7 16.9 %all-to-all-start.1 = ((bf16[8,32,512]{2,1,0:T(8,128)(2,1)}), bf16[8,32,512]{2,1,0:T(8,128)(2,1)S(1)}, u32[]{:S(2)}, u32[]{:S(2)}) async-start(bf16[8,32,512]{2,1,0:T(8,128)(2,1)} %bitcast.33), calls=%async_computation.1 | async-start | bytes 524288 | tf_op jit(solution)/shard_map/all_to_all | solution.py:293
  13.0 0.9 copy-start.1
  13.0 1.0 copy-start.2
  13.0 1.0 copy-start.3
  19.5 23.4 %all-to-all-start = ((bf16[64,8,256]{2,1,0:T(8,128)(2,1)}), bf16[64,8,256]{2,1,0:T(8,128)(2,1)S(1)}, u32[]{:S(2)}, u32[]{:S(2)}) async-start(bf16[64,8,256]{2,1,0:T(8,128)(2,1)} %bitcast.3), calls=%async_computation | async-start | bytes 524288 | tf_op jit(solution)/shard_map/all_to_all | solution.py:293
  45.2 6.4 %collective-permute-start = (bf16[128,1024]{1,0:T(8,128)(2,1)S(1)}, bf16[128,1024]{1,0:T(8,128)(2,1)S(1)}, u32[]{:S(2)}, u32[]{:S(2)}) collective-permute-start(bf16[128,1024]{1,0:T(8,128)(2,1)S(1)} %get-tuple-element.28), channel_id=1, source_target_pairs={{0,32},{32,0},{64,96},{96,64},{128,160},{160,128},{192,224},{224,1... | collective-permute-start | bytes 786440 | tf_op jit(solution)/shard_map/ppermute | solution.py:297
  102.9 6.6 %collective-permute-start.1 = (bf16[512,256]{1,0:T(8,128)(2,1)S(1)}, bf16[512,256]{1,0:T(8,128)(2,1)S(1)}, u32[]{:S(2)}, u32[]{:S(2)}) collective-permute-start(bf16[512,256]{1,0:T(8,128)(2,1)S(1)} %bitcast.26), channel_id=1, source_target_pairs={{0,32},{32,0},{64,96},{96,64},{128,160},{160,128},{192,224},{224,1... | collective-permute-start | bytes 786440 | tf_op jit(solution)/shard_map/ppermute | solution.py:297

commit v6 on v5

--- a/solution.py
+++ b/solution.py
@@ -215,62 +215,60 @@
 
 
 def y_back_body(out_t, dq_t, dk, dv, w_qkv, back):
-    out_t, dfeat_t = results(out_t[...], dq_t[...], dk[...], dv[...], w_qkv)
     wide = (2 * T, T)
     row = y_sorted(iota(1, wide))
-    back[...] = (
-        nt(onehot(iota(0, wide) == row), out_t) + nt(onehot(iota(0, wide) == row + 4), dfeat_t)
-    ).astype(BF)
+    low, high = onehot(iota(0, wide) == row), onehot(iota(0, wide) == row + 4)
+    for at, part_t in enumerate(results(out_t[...], dq_t[...], dk[...], dv[...], w_qkv)):
+        back[:, at * 128 : (at + 1) * 128] = (
+            nt(low, part_t[:128]) + nt(high, part_t[128:])
+        ).astype(BF)
 
 
 def col_pack_body(back_y, keep, took, send_col):
-    send_col[:, :C] = back_y[...]
+    send_col[:, :128] = back_y[:, :128]
     half = (keep[...] + took[...].astype(F32)).astype(BF)
     for at in range(4):
-        send_col[at * 128 : (at + 1) * 128, C:] = half[:, at * C : (at + 1) * C]
+        send_col[at * 128 : (at + 1) * 128, 128:] = half[:, at * C : (at + 1) * C]
 
 
 def row_pack_body(got_col, back_x, send_row):
     send_row[:, : 2 * C] = back_x[...]
-    block = jnp.sum(got_col[:, C:].astype(F32).reshape(64, 8, C), axis=0)
+    block = jnp.sum(got_col[:, 128:].astype(F32).reshape(64, 8, C), axis=0)
     block = jnp.concatenate([block[:, :128], block[:, 128:]], axis=0)
     send_row[:, 2 * C :] = jnp.concatenate([block] * 16, axis=0).astype(BF)
 
 
-def last_pack_body(factor, got_row, send):
+def last_pack_body(factor, got_row, back_y, send):
     mine = core()
     block = jnp.zeros((16, 128), F32)
     for peer in range(4):
         at = pl.multiple_of((2 * peer + mine) * 32, 32)
         block += got_row[pl.ds(at, 16), 2 * C :].astype(F32)
     block = jnp.concatenate([block[:8], block[8:]], axis=1) * factor
-    send[...] = jnp.concatenate([block] * 64, axis=0).astype(BF)
-
-
-def final_body(back_z, got_col, got_row, w_out, update, grad_in):
+    send[:, :128] = back_y[:, 128:]
+    send[:, 128:] = jnp.concatenate([block] * 64, axis=0).astype(BF)
+
+
+def final_body(back_z, got_col, got_row, got_last, w_out, update, grad_in):
     wide = (T, 2 * T)
     row = y_row(iota(0, wide))
-    back_y = got_col[:, :C]
+    low, high = onehot(row == iota(1, wide)), onehot(row + 4 == iota(1, wide))
     put_x = onehot(iota(0) == x_source(iota(1)))
-    mix = (
-        back_z[:, :C].astype(F32)
-        + nn(onehot(row == iota(1, wide)), back_y)
-        + nn(put_x, got_row[:, :C])
-    ).astype(BF)
-    update[...] = nn(mix, w_out[...]).astype(BF)
-    grad_in[...] = (
-        back_z[:, C:].astype(F32)
-        + nn(onehot(row + 4 == iota(1, wide)), back_y)
-        + nn(put_x, got_row[:, C : 2 * C])
-    ).astype(BF)
+    sums = []
+    for at, rows in enumerate((got_col[:, :128], got_last[:, :128])):
+        cols = slice(at * C, (at + 1) * C)
+        from_y = jnp.concatenate([nn(low, rows), nn(high, rows)], axis=1)
+        sums.append((back_z[:, cols].astype(F32) + from_y + nn(put_x, got_row[:, cols])).astype(BF))
+    update[...] = nn(sums[0], w_out[...]).astype(BF)
+    grad_in[...] = sums[1]
 
 
 def unpack_body(mine, other, grad_qkv, grad_out):
     for src, half in ((mine, core()), (other, 1 - core())):
         rows = pl.ds(pl.multiple_of(half * 128, 128), 128)
         for at in range(3):
-            grad_qkv[rows, at * C : (at + 1) * C] = src[at * 128 : (at + 1) * 128].astype(F32)
-        grad_out[rows, :] = src[3 * 128 :].astype(F32)
+            grad_qkv[rows, at * C : (at + 1) * C] = src[at * 128 : (at + 1) * 128, 128:].astype(F32)
+        grad_out[rows, :] = src[3 * 128 :, 128:].astype(F32)
 
 
 def call(body, outs, flops, *args, space=pltpu.VMEM, scratch=(), grant=40 * 2**20):
@@ -337,17 +335,21 @@
     )
     took = swap(give)
     (back_y,) = call(y_back_body, [shape(2 * T, C, BF)], cube * 8, *parts, w_qkv)
-    (send_col,) = call(col_pack_body, [shape(2 * T, 2 * C, BF)], 2**20, back_y, keep, took)
+    (send_col,) = call(col_pack_body, [shape(2 * T, 3 * 128, BF)], 2**20, back_y, keep, took)
     got_col = exchange(send_col, ("dp", "col"))
     (send_row,) = call(row_pack_body, [shape(T, 2 * C + 128, BF)], 2**20, got_col, back_x)
     got_row = exchange(send_row, "row")
     factor = 1.0 / math.sqrt(PATCHES * 64 * 64 * 16)
     (send_last,) = call(
-        functools.partial(last_pack_body, factor), [shape(512, C, BF)], 2**20, got_row
+        functools.partial(last_pack_body, factor),
+        [shape(2 * T, 3 * 128, BF)],
+        2**20,
+        got_row,
+        back_y,
     )
     mine = exchange(send_last, ("dp", "col"))
     update, grad_in = call(
-        final_body, [shape(T, C, BF)] * 2, cube * 6, back_z, got_col, got_row, w_out
+        final_body, [shape(T, C, BF)] * 2, cube * 6, back_z, got_col, got_row, mine, w_out
     )
     grad_qkv, grad_out = call(
         unpack_body, [shape(C, 3 * C, F32), shape(C, C, F32)], 2**20, mine, swap(mine)

time: 111 us -> 110 us (level)
  no operation moved by 1% of the time
where the time goes in v6:
time: 110 us
  blocking collectives  50.3 us (46%)
  starting transfers between devices  32.8 us (30%)
  Pallas kernels  12.6 us (11%)
  waiting for transfers between devices  12.4 us (11%)
    all_to_all x3, blocking collectives, exchange(): return lax.all_to_all(rows, axis, split_axis=0, concat_axis=0, tiled=True)  50.3 us
    all_to_all x2, starting transfers between devices, exchange(): return lax.all_to_all(rows, axis, split_axis=0, concat_axis=0, tiled=True)  22.2 us
    pallas_call x10, Pallas kernels, call(): pl.pallas_call(body, out_shape=outs, in_specs=[pl.BlockSpec(memory_space=...  12.6 us
    all_to_all x2, waiting for transfers between devices, exchange(): return lax.all_to_all(rows, axis, split_axis=0, concat_axis=0, tiled=True)  11.9 us
    ppermute x2, starting transfers between devices, swap(): return lax.ppermute(rows, 'row', [(i, i ^ 1) for i in range(8)])  10.6 us
  transfers between devices with their start and end apart: 4, of which 3 were waited for; matrix products, arithmetic and copies ran while one was open for 0% of the time, Pallas kernels for 6%

profile of v6, /device:TPU:1, one launch (start us, length us, event | category | flops | bytes accessed | tf_op | source)
XLA Modules:
  0.0 109.8 jit_solution(17679360702297052054)
XLA Ops:
  0.6 2.0 %shard_map.76 = bf16[256,512]{1,0:T(8,128)(2,1)} custom-call(bf16[256,256]{1,0:T(8,128)(2,1)} %bitcast.30, bf16[256,256]{1,0:T(8,128)(2,1)} %bitcast.32), custom_call_target="tpu_custom_call" | custom-call | flops 67108864 | bytes 1048576 | tf_op jit(solution)/shard_map/pallas_call | solution.py:275
  2.7 0.0 copy-start
  2.7 10.3 %all-to-all-start.1 = ((bf16[8,32,512]{2,1,0:T(8,128)(2,1)}), bf16[8,32,512]{2,1,0:T(8,128)(2,1)S(1)}, u32[]{:S(2)}, u32[]{:S(2)}) async-start(bf16[8,32,512]{2,1,0:T(8,128)(2,1)} %bitcast.34), calls=%async_computation.1 | async-start | bytes 524288 | tf_op jit(solution)/shard_map/all_to_all | solution.py:291
  13.0 0.0 copy-done
  13.0 0.0 copy-start.1
  13.0 0.0 copy-start.2
  13.0 0.0 copy-start.3
  13.0 0.2 copy.8
  13.2 0.7 copy-done.1
  13.9 0.1 copy-done.2
  14.0 0.1 copy-done.3
  14.0 2.7 %shard_map.75 = (bf16[256,512]{1,0:T(8,128)(2,1)S(1)}, bf16[256,1024]{1,0:T(8,128)(2,1)S(1)}, bf16[512,256]{1,0:T(8,128)(2,1)}) custom-call(bf16[256,256]{1,0:T(8,128)(2,1)S(1)} %bitcast.31, bf16[256,256]{1,0:T(8,128)(2,1)S(1)} %bitcast.33, bf16[256,768]{1,0:T(8,128)(2,1)S(1)} %copy-done, bf16[768,256]{1,0:T(8,128)(2,1)S(1)} %bitcast.23, ...), custom_call_target="tpu_custom_call" | custom-call | flops 2348810240 | bytes 1048576 | tf_op jit(solution)/shard_map/pallas_call | solution.py:275
  16.7 2.8 %all-to-all-done.1 = bf16[8,32,512]{2,1,0:T(8,128)(2,1)S(1)} async-done(((bf16[8,32,512]{2,1,0:T(8,128)(2,1)}), bf16[8,32,512]{2,1,0:T(8,128)(2,1)S(1)}, u32[]{:S(2)}, u32[]{:S(2)}) %all-to-all-start.1) | async-done | bytes 262176 | tf_op jit(solution)/shard_map/all_to_all | solution.py:291
  19.5 11.9 %all-to-all-start = ((bf16[64,8,256]{2,1,0:T(8,128)(2,1)}), bf16[64,8,256]{2,1,0:T(8,128)(2,1)S(1)}, u32[]{:S(2)}, u32[]{:S(2)}) async-start(bf16[64,8,256]{2,1,0:T(8,128)(2,1)} %bitcast.3), calls=%async_computation | async-start | bytes 524288 | tf_op jit(solution)/shard_map/all_to_all | solution.py:291
  31.4 2.4 %shard_map.77 = (bf16[256,512]{1,0:T(8,128)(2,1)S(1)}, bf16[256,1024]{1,0:T(8,128)(2,1)S(1)}) custom-call(bf16[256,512]{1,0:T(8,128)(2,1)S(1)} %bitcast.28, bf16[256,768]{1,0:T(8,128)(2,1)S(1)} %copy-done, bf16[768,256]{1,0:T(8,128)(2,1)S(1)} %bitcast.24, bf16[256,256]{1,0:T(8,128)(2,1)S(1)} %copy-done.1, bf16[256,1024]{1,0:T(8,128)(2,1)S(1)} %get-tuple-element.21.grad_so_far), custom_call_target="tpu_custom_call" | custom-call | flops 2348810240 | bytes 1048576 | tf_op jit(solution)/shard_map/pallas_call | solution.py:275
  33.8 9.1 %all-to-all-done = bf16[64,8,256]{2,1,0:T(8,128)(2,1)S(1)} async-done(((bf16[64,8,256]{2,1,0:T(8,128)(2,1)}), bf16[64,8,256]{2,1,0:T(8,128)(2,1)S(1)}, u32[]{:S(2)}, u32[]{:S(2)}) %all-to-all-start) | async-done | bytes 262176 | tf_op jit(solution)/shard_map/all_to_all | solution.py:291
  42.9 2.3 %shard_map.78 = (bf16[256,256]{1,0:T(8,128)(2,1)S(1)}, bf16[256,256]{1,0:T(8,128)(2,1)S(1)}, bf16[256,256]{1,0:T(8,128)(2,1)S(1)}, bf16[256,256]{1,0:T(8,128)(2,...) custom-call(bf16[512,256]{1,0:T(8,128)(2,1)S(1)} %bitcast.29, bf16[256,768]{1,0:T(8,128)(2,1)S(1)} %copy-done, ...), custom_call_target="tpu_custom_call" | custom-call | flops 2348810240 | bytes 1048576 | tf_op jit(solution)/shard_map/pallas_call | solution.py:275
  45.2 5.2 %collective-permute-start = (bf16[128,1024]{1,0:T(8,128)(2,1)S(1)}, bf16[128,1024]{1,0:T(8,128)(2,1)S(1)}, u32[]{:S(2)}, u32[]{:S(2)}) collective-permute-start(bf16[128,1024]{1,0:T(8,128)(2,1)S(1)} %get-tuple-element.28), channel_id=1, source_target_pairs={{0,32},{32,0},{64,96},{96,64},{128,160},{160,128},{192,224},{224,1... | collective-permute-start | bytes 786440 | tf_op jit(solution)/shard_map/ppermute | solution.py:295
  50.4 0.7 shard_map.79.back_y
  51.1 0.5 collective-permute-done.took
  51.6 0.1 shard_map.80
  51.6 18.5 %all_to_all.55 = bf16[64,8,384]{2,1,0:T(8,128)(2,1)S(1)} all-to-all(bf16[64,8,384]{2,1,0:T(8,128)(2,1)S(1)} %bitcast.20), channel_id=1, replica_groups=mesh['dp'=2,'row'=8,'col'=32] {'dp','col'}, dimensions={0} | all-to-all | bytes 786432 | tf_op jit(solution)/shard_map/all_to_all | solution.py:291
  70.1 0.1 shard_map.81
  70.2 12.7 %all_to_all.56 = bf16[8,32,640]{2,1,0:T(8,128)(2,1)S(1)} all-to-all(bf16[8,32,640]{2,1,0:T(8,128)(2,1)S(1)} %bitcast.27), channel_id=1, replica_groups=mesh['dp'=2,'row'=8,'col'=32] {'row'}, dimensions={0} | all-to-all | bytes 655360 | tf_op jit(solution)/shard_map/all_to_all | solution.py:291
  82.9 0.1 shard_map.82
  82.9 19.2 %all_to_all.57 = bf16[64,8,384]{2,1,0:T(8,128)(2,1)S(1)} all-to-all(bf16[64,8,384]{2,1,0:T(8,128)(2,1)S(1)} %bitcast.26), channel_id=1, replica_groups=mesh['dp'=2,'row'=8,'col'=32] {'dp','col'}, dimensions={0} | all-to-all | bytes 786432 | tf_op jit(solution)/shard_map/all_to_all | solution.py:291
  102.1 5.3 %collective-permute-start.1 = (bf16[512,384]{1,0:T(8,128)(2,1)S(1)}, bf16[512,384]{1,0:T(8,128)(2,1)S(1)}, u32[]{:S(2)}, u32[]{:S(2)}) collective-permute-start(bf16[512,384]{1,0:T(8,128)(2,1)S(1)} %bitcast.17), channel_id=1, source_target_pairs={{0,32},{32,0},{64,96},{96,64},{128,160},{160,128},{192,224},{224,1... | collective-permute-start | bytes 1179656 | tf_op jit(solution)/shard_map/ppermute | solution.py:295
  107.4 1.3 %shard_map.83 = (bf16[256,256]{1,0:T(8,128)(2,1)}, bf16[256,256]{1,0:T(8,128)(2,1)}) custom-call(bf16[256,512]{1,0:T(8,128)(2,1)S(1)} %get-tuple-element.19.back_z, bf16[512,384]{1,0:T(8,128)(2,1)S(1)} %bitcast.16, bf16[256,640]{1,0:T(8,128)(2,1)S(1)} %bitcast.22, bf16[512,384]{1,0:T(8,128)(2,1)S(1)} %bitcast.18, bf16[256,256]{1,0:T(8,128)(2,1)S(1)} %copy-done.1), custom_call_target="tpu_custom_call" | custom-call | flops 201326592 | bytes 1048576 | tf_op jit(solution)/shard_map/pallas_call | solution.py:275
  108.7 0.0 collective-permute-done.1.other
  108.8 1.0 shard_map.84
Async XLA Ops:
  2.7 10.3 %copy-start = (bf16[256,768]{1,0:T(8,128)(2,1)S(1)}, bf16[256,768]{1,0:T(8,128)(2,1)}, u32[]{:S(2)}) copy-start(bf16[256,768]{1,0:T(8,128)(2,1)} %w_qkv.7) | copy-start | bytes 1179652
  2.7 16.9 %all-to-all-start.1 = ((bf16[8,32,512]{2,1,0:T(8,128)(2,1)}), bf16[8,32,512]{2,1,0:T(8,128)(2,1)S(1)}, u32[]{:S(2)}, u32[]{:S(2)}) async-start(bf16[8,32,512]{2,1,0:T(8,128)(2,1)} %bitcast.34), calls=%async_computation.1 | async-start | bytes 524288 | tf_op jit(solution)/shard_map/all_to_all | solution.py:291
  13.0 0.9 copy-start.1
  13.0 1.0 copy-start.2
  13.0 1.0 copy-start.3
  19.5 23.4 %all-to-all-start = ((bf16[64,8,256]{2,1,0:T(8,128)(2,1)}), bf16[64,8,256]{2,1,0:T(8,128)(2,1)S(1)}, u32[]{:S(2)}, u32[]{:S(2)}) async-start(bf16[64,8,256]{2,1,0:T(8,128)(2,1)} %bitcast.3), calls=%async_computation | async-start | bytes 524288 | tf_op jit(solution)/shard_map/all_to_all | solution.py:291
  45.2 6.4 %collective-permute-start = (bf16[128,1024]{1,0:T(8,128)(2,1)S(1)}, bf16[128,1024]{1,0:T(8,128)(2,1)S(1)}, u32[]{:S(2)}, u32[]{:S(2)}) collective-permute-start(bf16[128,1024]{1,0:T(8,128)(2,1)S(1)} %get-tuple-element.28), channel_id=1, source_target_pairs={{0,32},{32,0},{64,96},{96,64},{128,160},{160,128},{192,224},{224,1... | collective-permute-start | bytes 786440 | tf_op jit(solution)/shard_map/ppermute | solution.py:295
  102.1 6.7 %collective-permute-start.1 = (bf16[512,384]{1,0:T(8,128)(2,1)S(1)}, bf16[512,384]{1,0:T(8,128)(2,1)S(1)}, u32[]{:S(2)}, u32[]{:S(2)}) collective-permute-start(bf16[512,384]{1,0:T(8,128)(2,1)S(1)} %bitcast.17), channel_id=1, source_target_pairs={{0,32},{32,0},{64,96},{96,64},{128,160},{160,128},{192,224},{224,1... | collective-permute-start | bytes 1179656 | tf_op jit(solution)/shard_map/ppermute | solution.py:295

commit v7 on v6

--- a/solution.py
+++ b/solution.py
@@ -31,39 +31,43 @@
     return lax.dot_general(a, b, (((1,), (1,)), ((), ())), preferred_element_type=F32)
 
 
-def iota(axis, shape=(T, T)):
-    return lax.broadcasted_iota(jnp.int32, shape, axis)
+def down(n):
+    return lax.broadcasted_iota(jnp.int32, (n, 1), 0)
+
+
+def along(n):
+    return lax.broadcasted_iota(jnp.int32, (1, n), 1)
 
 
 def x_source(r):
-    peer = r // 32
-    return (peer // 4) * 128 + (r % 8) * Z + (peer % 4) * LINES + (r // 8) % LINES
+    peer = r >> 5
+    return ((peer >> 2) << 7) + ((r & 7) << 4) + ((peer & 3) << 2) + ((r >> 3) & 3)
 
 
 def x_sorted(t):
-    return (t % 64) // 8 * 32 + t // 64 * 8 + t % 8
+    return (((t & 63) >> 3) << 5) + ((t >> 6) << 3) + (t & 7)
 
 
 def y_row(t):
-    at = t % 128
-    return at // 2 * 8 + t // 128 * 2 + at % 2
+    at = t & 127
+    return ((at >> 1) << 3) + ((t >> 7) << 1) + (at & 1)
 
 
 def y_sorted(t):
-    at = t % 64
-    return t // 128 * 256 + at // 2 * 8 + at % 2 * 2 + t // 64 % 2
+    at = t & 63
+    return ((t >> 7) << 8) + ((at >> 1) << 3) + ((at & 1) << 1) + ((t >> 6) & 1)
 
 
 def z_line(r):
-    return r // Z
+    return r >> 4
 
 
 def long_line(r):
-    return r // 64
-
-
-def onehot(hit):
-    return jnp.where(hit, 1.0, 0.0).astype(BF)
+    return r >> 6
+
+
+def onehot(a, b):
+    return jnp.where(a == b, 1.0, 0.0).astype(BF)
 
 
 def pack_body(feat_hbm, cot_hbm, send_x, feat, cot, sorted_rows, sem):
@@ -73,7 +77,7 @@
     ]
     for copy in copies:
         copy.start()
-    pick = onehot(x_source(iota(0)) == iota(1))
+    pick = onehot(x_source(down(T)), along(T))
     outs = []
     for at, (copy, rows) in enumerate(zip(copies, (feat, cot))):
         copy.wait()
@@ -89,16 +93,15 @@
 
 def axis_math(line, feat, cot, w_qkv, w_qkv_t, w_out):
     scale = 1.0 / math.sqrt(DEPTH)
-    feat_t = nt(onehot(iota(0) == iota(1)), feat).astype(BF)
+    feat_t = nt(onehot(down(T), along(T)), feat).astype(BF)
     proj = nn(feat, w_qkv[...]).astype(BF)
     proj_t = nt(w_qkv_t[...], feat).astype(BF)
     gmix = nt(cot, w_out[...]).astype(BF)
     gmix_t = nt(w_out[...], cot).astype(BF)
     q, k, v = proj[:, :C], proj[:, C : 2 * C], proj[:, 2 * C :]
     q_t, k_t, v_t = proj_t[:C], proj_t[C : 2 * C], proj_t[2 * C :]
-    wide = (HALF, QUAD * HALF)
-    bias = jnp.where(line(iota(0, wide)) == line(iota(1, wide) % HALF), 0.0, NEG)
-    head_of_lane = iota(1, (HALF, HALF)) // DEPTH
+    bias = jnp.where(line(down(HALF)) == line(along(QUAD * HALF) & (HALF - 1)), 0.0, NEG)
+    head_of_lane = jnp.broadcast_to(along(HALF) >> 5, (HALF, HALF))
     blank = jnp.zeros((HALF, HALF), BF)
     strip = jnp.zeros((DEPTH, HALF), BF)
 
@@ -168,13 +171,12 @@
 
 
 def z_body(feat, cot, w_qkv, w_qkv_t, w_out, back, grad, send_y):
-    wide = (2 * T, T)
-    row = y_row(iota(1, wide))
+    row, at_row = y_row(along(T)), down(2 * T)
     send_y[...] = (
-        nn(onehot(iota(0, wide) == row), feat[...]) + nn(onehot(iota(0, wide) == row + 4), cot[...])
+        nn(onehot(at_row, row), feat[...]) + nn(onehot(at_row, row + 4), cot[...])
     ).astype(BF)
     parts, terms = axis_math(z_line, feat[...], cot[...], w_qkv, w_qkv_t, w_out)
-    eye = onehot(iota(0) == iota(1))
+    eye = onehot(down(T), along(T))
     for at, part_t in enumerate(results(*parts, w_qkv)):
         back[:, at * C : (at + 1) * C] = nt(eye, part_t).astype(BF)
     for at, term in enumerate(terms):
@@ -182,11 +184,11 @@
 
 
 def x_body(got, w_qkv, w_qkv_t, w_out, grad_so_far, back, grad):
-    sort = onehot(x_sorted(iota(0)) == iota(1))
+    sort = onehot(x_sorted(down(T)), along(T))
     feat = nn(sort, got[:, :C]).astype(BF)
     cot = nn(sort, got[:, C:]).astype(BF)
     parts, terms = axis_math(long_line, feat, cot, w_qkv, w_qkv_t, w_out)
-    unsort = onehot(iota(0) == x_sorted(iota(1)))
+    unsort = onehot(down(T), x_sorted(along(T)))
     for at, part_t in enumerate(results(*parts, w_qkv)):
         back[:, at * C : (at + 1) * C] = nt(unsort, part_t).astype(BF)
     for at, term in enumerate(terms):
@@ -199,10 +201,9 @@
 
 
 def y_body(got, w_qkv, w_qkv_t, w_out, grad_so_far, out_t, dq_t, dk, dv, keep, give, total):
-    wide = (T, 2 * T)
-    row = y_sorted(iota(0, wide))
-    feat = nn(onehot(row == iota(1, wide)), got[...]).astype(BF)
-    cot = nn(onehot(row + 4 == iota(1, wide)), got[...]).astype(BF)
+    row = y_sorted(down(T))
+    feat = nn(onehot(row, along(2 * T)), got[...]).astype(BF)
+    cot = nn(onehot(row + 4, along(2 * T)), got[...]).astype(BF)
     parts, terms = axis_math(long_line, feat, cot, w_qkv, w_qkv_t, w_out)
     for ref, part in zip((out_t, dq_t, dk, dv), parts):
         ref[...] = part
@@ -215,9 +216,8 @@
 
 
 def y_back_body(out_t, dq_t, dk, dv, w_qkv, back):
-    wide = (2 * T, T)
-    row = y_sorted(iota(1, wide))
-    low, high = onehot(iota(0, wide) == row), onehot(iota(0, wide) == row + 4)
+    row, at_row = y_sorted(along(T)), down(2 * T)
+    low, high = onehot(at_row, row), onehot(at_row, row + 4)
     for at, part_t in enumerate(results(out_t[...], dq_t[...], dk[...], dv[...], w_qkv)):
         back[:, at * 128 : (at + 1) * 128] = (
             nt(low, part_t[:128]) + nt(high, part_t[128:])
@@ -250,10 +250,9 @@
 
 
 def final_body(back_z, got_col, got_row, got_last, w_out, update, grad_in):
-    wide = (T, 2 * T)
-    row = y_row(iota(0, wide))
-    low, high = onehot(row == iota(1, wide)), onehot(row + 4 == iota(1, wide))
-    put_x = onehot(iota(0) == x_source(iota(1)))
+    row = y_row(down(T))
+    low, high = onehot(row, along(2 * T)), onehot(row + 4, along(2 * T))
+    put_x = onehot(down(T), x_source(along(T)))
     sums = []
     for at, rows in enumerate((got_col[:, :128], got_last[:, :128])):
         cols = slice(at * C, (at + 1) * C)

time: 110 us -> 110 us (level)
  no operation moved by 1% of the time
where the time goes in v7:
time: 110 us
  blocking collectives  50.3 us (46%)
  starting transfers between devices  32.8 us (30%)
  Pallas kernels  12.6 us (11%)
  waiting for transfers between devices  12.4 us (11%)
    all_to_all x3, blocking collectives, exchange(): return lax.all_to_all(rows, axis, split_axis=0, concat_axis=0, tiled=True)  50.3 us
    all_to_all x2, starting transfers between devices, exchange(): return lax.all_to_all(rows, axis, split_axis=0, concat_axis=0, tiled=True)  22.2 us
    pallas_call x10, Pallas kernels, call(): pl.pallas_call(body, out_shape=outs, in_specs=[pl.BlockSpec(memory_space=...  12.6 us
    all_to_all x2, waiting for transfers between devices, exchange(): return lax.all_to_all(rows, axis, split_axis=0, concat_axis=0, tiled=True)  11.9 us
    ppermute x2, starting transfers between devices, swap(): return lax.ppermute(rows, 'row', [(i, i ^ 1) for i in range(8)])  10.6 us
  transfers between devices with their start and end apart: 4, of which 3 were waited for; matrix products, arithmetic and copies ran while one was open for 0% of the time, Pallas kernels for 6%

profile of v7, /device:TPU:1, one launch (start us, length us, event | category | flops | bytes accessed | tf_op | source)
XLA Modules:
  0.0 109.8 jit_solution(4294475724241331837)
XLA Ops:
  0.6 2.0 %shard_map.76 = bf16[256,512]{1,0:T(8,128)(2,1)} custom-call(bf16[256,256]{1,0:T(8,128)(2,1)} %bitcast.30, bf16[256,256]{1,0:T(8,128)(2,1)} %bitcast.32), custom_call_target="tpu_custom_call" | custom-call | flops 67108864 | bytes 1048576 | tf_op jit(solution)/shard_map/pallas_call | solution.py:274
  2.7 0.0 copy-start
  2.7 10.3 %all-to-all-start.1 = ((bf16[8,32,512]{2,1,0:T(8,128)(2,1)}), bf16[8,32,512]{2,1,0:T(8,128)(2,1)S(1)}, u32[]{:S(2)}, u32[]{:S(2)}) async-start(bf16[8,32,512]{2,1,0:T(8,128)(2,1)} %bitcast.34), calls=%async_computation.1 | async-start | bytes 524288 | tf_op jit(solution)/shard_map/all_to_all | solution.py:290
  13.0 0.0 copy-done
  13.0 0.0 copy-start.1
  13.0 0.0 copy-start.2
  13.0 0.0 copy-start.3
  13.0 0.2 copy.8
  13.2 0.7 copy-done.1
  13.9 0.1 copy-done.2
  14.0 0.1 copy-done.3
  14.0 2.7 %shard_map.75 = (bf16[256,512]{1,0:T(8,128)(2,1)S(1)}, bf16[256,1024]{1,0:T(8,128)(2,1)S(1)}, bf16[512,256]{1,0:T(8,128)(2,1)}) custom-call(bf16[256,256]{1,0:T(8,128)(2,1)S(1)} %bitcast.31, bf16[256,256]{1,0:T(8,128)(2,1)S(1)} %bitcast.33, bf16[256,768]{1,0:T(8,128)(2,1)S(1)} %copy-done, bf16[768,256]{1,0:T(8,128)(2,1)S(1)} %bitcast.23, ...), custom_call_target="tpu_custom_call" | custom-call | flops 2348810240 | bytes 1048576 | tf_op jit(solution)/shard_map/pallas_call | solution.py:274
  16.7 2.8 %all-to-all-done.1 = bf16[8,32,512]{2,1,0:T(8,128)(2,1)S(1)} async-done(((bf16[8,32,512]{2,1,0:T(8,128)(2,1)}), bf16[8,32,512]{2,1,0:T(8,128)(2,1)S(1)}, u32[]{:S(2)}, u32[]{:S(2)}) %all-to-all-start.1) | async-done | bytes 262176 | tf_op jit(solution)/shard_map/all_to_all | solution.py:290
  19.5 11.9 %all-to-all-start = ((bf16[64,8,256]{2,1,0:T(8,128)(2,1)}), bf16[64,8,256]{2,1,0:T(8,128)(2,1)S(1)}, u32[]{:S(2)}, u32[]{:S(2)}) async-start(bf16[64,8,256]{2,1,0:T(8,128)(2,1)} %bitcast.3), calls=%async_computation | async-start | bytes 524288 | tf_op jit(solution)/shard_map/all_to_all | solution.py:290
  31.4 2.4 %shard_map.77 = (bf16[256,512]{1,0:T(8,128)(2,1)S(1)}, bf16[256,1024]{1,0:T(8,128)(2,1)S(1)}) custom-call(bf16[256,512]{1,0:T(8,128)(2,1)S(1)} %bitcast.28, bf16[256,768]{1,0:T(8,128)(2,1)S(1)} %copy-done, bf16[768,256]{1,0:T(8,128)(2,1)S(1)} %bitcast.24, bf16[256,256]{1,0:T(8,128)(2,1)S(1)} %copy-done.1, bf16[256,1024]{1,0:T(8,128)(2,1)S(1)} %get-tuple-element.21.grad_so_far), custom_call_target="tpu_custom_call" | custom-call | flops 2348810240 | bytes 1048576 | tf_op jit(solution)/shard_map/pallas_call | solution.py:274
  33.9 9.1 %all-to-all-done = bf16[64,8,256]{2,1,0:T(8,128)(2,1)S(1)} async-done(((bf16[64,8,256]{2,1,0:T(8,128)(2,1)}), bf16[64,8,256]{2,1,0:T(8,128)(2,1)S(1)}, u32[]{:S(2)}, u32[]{:S(2)}) %all-to-all-start) | async-done | bytes 262176 | tf_op jit(solution)/shard_map/all_to_all | solution.py:290
  42.9 2.3 %shard_map.78 = (bf16[256,256]{1,0:T(8,128)(2,1)S(1)}, bf16[256,256]{1,0:T(8,128)(2,1)S(1)}, bf16[256,256]{1,0:T(8,128)(2,1)S(1)}, bf16[256,256]{1,0:T(8,128)(2,...) custom-call(bf16[512,256]{1,0:T(8,128)(2,1)S(1)} %bitcast.29, bf16[256,768]{1,0:T(8,128)(2,1)S(1)} %copy-done, ...), custom_call_target="tpu_custom_call" | custom-call | flops 2348810240 | bytes 1048576 | tf_op jit(solution)/shard_map/pallas_call | solution.py:274
  45.2 5.2 %collective-permute-start = (bf16[128,1024]{1,0:T(8,128)(2,1)S(1)}, bf16[128,1024]{1,0:T(8,128)(2,1)S(1)}, u32[]{:S(2)}, u32[]{:S(2)}) collective-permute-start(bf16[128,1024]{1,0:T(8,128)(2,1)S(1)} %get-tuple-element.28), channel_id=1, source_target_pairs={{0,32},{32,0},{64,96},{96,64},{128,160},{160,128},{192,224},{224,1... | collective-permute-start | bytes 786440 | tf_op jit(solution)/shard_map/ppermute | solution.py:294
  50.4 0.7 shard_map.79.back_y
  51.1 0.5 collective-permute-done.took
  51.6 0.1 shard_map.80
  51.6 18.5 %all_to_all.55 = bf16[64,8,384]{2,1,0:T(8,128)(2,1)S(1)} all-to-all(bf16[64,8,384]{2,1,0:T(8,128)(2,1)S(1)} %bitcast.20), channel_id=1, replica_groups=mesh['dp'=2,'row'=8,'col'=32] {'dp','col'}, dimensions={0} | all-to-all | bytes 786432 | tf_op jit(solution)/shard_map/all_to_all | solution.py:290
  70.1 0.1 shard_map.81
  70.2 12.7 %all_to_all.56 = bf16[8,32,640]{2,1,0:T(8,128)(2,1)S(1)} all-to-all(bf16[8,32,640]{2,1,0:T(8,128)(2,1)S(1)} %bitcast.27), channel_id=1, replica_groups=mesh['dp'=2,'row'=8,'col'=32] {'row'}, dimensions={0} | all-to-all | bytes 655360 | tf_op jit(solution)/shard_map/all_to_all | solution.py:290
  82.9 0.1 shard_map.82
  82.9 19.2 %all_to_all.57 = bf16[64,8,384]{2,1,0:T(8,128)(2,1)S(1)} all-to-all(bf16[64,8,384]{2,1,0:T(8,128)(2,1)S(1)} %bitcast.26), channel_id=1, replica_groups=mesh['dp'=2,'row'=8,'col'=32] {'dp','col'}, dimensions={0} | all-to-all | bytes 786432 | tf_op jit(solution)/shard_map/all_to_all | solution.py:290
  102.1 5.3 %collective-permute-start.1 = (bf16[512,384]{1,0:T(8,128)(2,1)S(1)}, bf16[512,384]{1,0:T(8,128)(2,1)S(1)}, u32[]{:S(2)}, u32[]{:S(2)}) collective-permute-start(bf16[512,384]{1,0:T(8,128)(2,1)S(1)} %bitcast.17), channel_id=1, source_target_pairs={{0,32},{32,0},{64,96},{96,64},{128,160},{160,128},{192,224},{224,1... | collective-permute-start | bytes 1179656 | tf_op jit(solution)/shard_map/ppermute | solution.py:294
  107.5 1.3 %shard_map.83 = (bf16[256,256]{1,0:T(8,128)(2,1)}, bf16[256,256]{1,0:T(8,128)(2,1)}) custom-call(bf16[256,512]{1,0:T(8,128)(2,1)S(1)} %get-tuple-element.19.back_z, bf16[512,384]{1,0:T(8,128)(2,1)S(1)} %bitcast.16, bf16[256,640]{1,0:T(8,128)(2,1)S(1)} %bitcast.22, bf16[512,384]{1,0:T(8,128)(2,1)S(1)} %bitcast.18, bf16[256,256]{1,0:T(8,128)(2,1)S(1)} %copy-done.1), custom_call_target="tpu_custom_call" | custom-call | flops 201326592 | bytes 1048576 | tf_op jit(solution)/shard_map/pallas_call | solution.py:274
  108.7 0.0 collective-permute-done.1.other
  108.8 1.0 shard_map.84
Async XLA Ops:
  2.7 10.3 %copy-start = (bf16[256,768]{1,0:T(8,128)(2,1)S(1)}, bf16[256,768]{1,0:T(8,128)(2,1)}, u32[]{:S(2)}) copy-start(bf16[256,768]{1,0:T(8,128)(2,1)} %w_qkv.7) | copy-start | bytes 1179652
  2.7 16.9 %all-to-all-start.1 = ((bf16[8,32,512]{2,1,0:T(8,128)(2,1)}), bf16[8,32,512]{2,1,0:T(8,128)(2,1)S(1)}, u32[]{:S(2)}, u32[]{:S(2)}) async-start(bf16[8,32,512]{2,1,0:T(8,128)(2,1)} %bitcast.34), calls=%async_computation.1 | async-start | bytes 524288 | tf_op jit(solution)/shard_map/all_to_all | solution.py:290
  13.0 0.9 copy-start.1
  13.0 1.0 copy-start.2
  13.0 1.0 copy-start.3
  19.5 23.4 %all-to-all-start = ((bf16[64,8,256]{2,1,0:T(8,128)(2,1)}), bf16[64,8,256]{2,1,0:T(8,128)(2,1)S(1)}, u32[]{:S(2)}, u32[]{:S(2)}) async-start(bf16[64,8,256]{2,1,0:T(8,128)(2,1)} %bitcast.3), calls=%async_computation | async-start | bytes 524288 | tf_op jit(solution)/shard_map/all_to_all | solution.py:290
  45.2 6.4 %collective-permute-start = (bf16[128,1024]{1,0:T(8,128)(2,1)S(1)}, bf16[128,1024]{1,0:T(8,128)(2,1)S(1)}, u32[]{:S(2)}, u32[]{:S(2)}) collective-permute-start(bf16[128,1024]{1,0:T(8,128)(2,1)S(1)} %get-tuple-element.28), channel_id=1, source_target_pairs={{0,32},{32,0},{64,96},{96,64},{128,160},{160,128},{192,224},{224,1... | collective-permute-start | bytes 786440 | tf_op jit(solution)/shard_map/ppermute | solution.py:294
  102.1 6.7 %collective-permute-start.1 = (bf16[512,384]{1,0:T(8,128)(2,1)S(1)}, bf16[512,384]{1,0:T(8,128)(2,1)S(1)}, u32[]{:S(2)}, u32[]{:S(2)}) collective-permute-start(bf16[512,384]{1,0:T(8,128)(2,1)S(1)} %bitcast.17), channel_id=1, source_target_pairs={{0,32},{32,0},{64,96},{96,64},{128,160},{160,128},{192,224},{224,1... | collective-permute-start | bytes 1179656 | tf_op jit(solution)/shard_map/ppermute | solution.py:294

commit v8 on v7

v8 whole, which is shorter than its diff:
```python
import functools
import math

import jax
import jax.numpy as jnp
from jax import lax
from jax.experimental import pallas as pl
from jax.experimental.pallas import tpu as pltpu
from jax.sharding import PartitionSpec as P

HEADS = 8
DEPTH = 32
C = 256
T = 256
PATCHES = 2
Z = 16
HALF = 128
QUAD = 4
NEG = -1e30

BF = jnp.bfloat16
F32 = jnp.float32


def nn(a, b):
    return lax.dot_general(a, b, (((1,), (0,)), ((), ())), preferred_element_type=F32)


def nt(a, b):
    return lax.dot_general(a, b, (((1,), (1,)), ((), ())), preferred_element_type=F32)


def down(n):
    return lax.broadcasted_iota(jnp.int32, (n, 1), 0)


def along(n):
    return lax.broadcasted_iota(jnp.int32, (1, n), 1)


def core():
    return lax.rem(lax.axis_index("row"), 2)


def by_core(first, second):
    mine = core()
    return first * (1 - mine) + second * mine


def y_source(r):
    return (((r >> 2) & 1) << 7) + ((r >> 3) << 2) + (r & 3)


def x_source(r):
    return ((r >> 7) << 7) + ((r & 7) << 4) + ((r >> 3) & 15)


def place(t, part):
    line, at = t >> 6, t & 63
    y_place = (part << 8) + ((at >> 1) << 3) + ((at & 1) << 2) + line
    x_peer = ((at >> 4) << 3) + (part << 2) + line
    x_place = (((at >> 3) & 1) << 8) + (x_peer << 3) + (at & 7)
    return by_core(y_place, x_place)


def z_line(r):
    return r >> 4


def long_line(r):
    return r >> 6


def onehot(a, b):
    return jnp.where(a == b, 1.0, 0.0).astype(BF)


def pack_body(feat_hbm, cot_hbm, keep, give, feat, cot, mine, theirs, sem):
    copies = [
        pltpu.make_async_copy(feat_hbm, feat, sem.at[0]),
        pltpu.make_async_copy(cot_hbm, cot, sem.at[1]),
    ]
    for copy in copies:
        copy.start()
    r = down(T)
    pick_mine = onehot(by_core(y_source(r), x_source(r)), along(T))
    pick_theirs = onehot(by_core(x_source(r), y_source(r)), along(T))
    for copy in copies:
        copy.wait()
    for pick, rows in ((pick_theirs, theirs), (pick_mine, mine)):
        rows[:, :C] = nn(pick, feat[...]).astype(BF)
        rows[:, C:] = nn(pick, cot[...]).astype(BF)
    outs = [
        pltpu.make_async_copy(theirs, give, sem.at[2]),
        pltpu.make_async_copy(mine, keep, sem.at[3]),
    ]
    for out in outs:
        out.start()
    for out in outs:
        out.wait()


def merge_body(mine, took, send):
    send[:, : 2 * C] = mine[...]
    send[:, 2 * C :] = took[...]


def axis_math(line, feat, cot, w_qkv, w_qkv_t, w_out):
    scale = 1.0 / math.sqrt(DEPTH)
    feat_t = nt(onehot(down(T), along(T)), feat).astype(BF)
    proj = nn(feat, w_qkv[...]).astype(BF)
    proj_t = nt(w_qkv_t[...], feat).astype(BF)
    gmix = nt(cot, w_out[...]).astype(BF)
    gmix_t = nt(w_out[...], cot).astype(BF)
    q, k, v = proj[:, :C], proj[:, C : 2 * C], proj[:, 2 * C :]
    q_t, k_t, v_t = proj_t[:C], proj_t[C : 2 * C], proj_t[2 * C :]
    bias = jnp.where(line(down(HALF)) == line(along(QUAD * HALF) & (HALF - 1)), 0.0, NEG)
    head_of_lane = jnp.broadcast_to(along(HALF) >> 5, (HALF, HALF))
    blank = jnp.zeros((HALF, HALF), BF)
    strip = jnp.zeros((DEPTH, HALF), BF)

    def spread(a_t):
        return jnp.concatenate(
            [
                jnp.concatenate(
                    [a_t[i * DEPTH : (i + 1) * DEPTH] if i == j else strip for i in range(QUAD)],
                    axis=0,
                )
                for j in range(QUAD)
            ],
            axis=1,
        )

    def stack(a):
        return jnp.concatenate(
            [jnp.where(head_of_lane == j, a, blank) for j in range(QUAD)], axis=0
        )

    def per_head(a_t, m):
        return jnp.concatenate(
            [
                nn(a_t[j * DEPTH : (j + 1) * DEPTH], m[:, j * HALF : (j + 1) * HALF])
                for j in range(QUAD)
            ],
            axis=0,
        )

    blocks = [
        (slice(half * HALF, (half + 1) * HALF), slice(quad * HALF, (quad + 1) * HALF))
        for half in range(2)
        for quad in range(2)
    ]
    all_scores = [nn(k[t, c], spread(q_t[c, t])) + bias for t, c in blocks]
    all_dprobs = [nn(v[t, c], spread(gmix_t[c, t])) for t, c in blocks]
    soft = []
    for scores, dprobs in zip(all_scores, all_dprobs):
        top = jnp.max(scores, axis=0, keepdims=True)
        e = jnp.exp((scores - top) * scale)
        probs = e * (1.0 / jnp.sum(e, axis=0, keepdims=True))
        mean = jnp.sum(dprobs * probs, axis=0, keepdims=True)
        soft.append((probs.astype(BF), (probs * (dprobs - mean) * scale).astype(BF)))
    parts = []
    for (t, c), (rounded, dround) in zip(blocks, soft):
        out_t = per_head(v_t[c, t], rounded)
        dv = nn(rounded, stack(gmix[t, c]))
        dq_t = per_head(k_t[c, t], dround)
        dk = nn(dround, stack(q[t, c]))
        parts.append([m.astype(BF) for m in (out_t, dq_t, dk, dv)])

    def whole(at, transposed):
        p = [[parts[2 * half + quad][at] for quad in range(2)] for half in range(2)]
        if transposed:
            p = [[p[j][i] for j in range(2)] for i in range(2)]
        return jnp.concatenate([jnp.concatenate(r, axis=1) for r in p], axis=0)

    out_t, dq_t = whole(0, True), whole(1, True)
    dk, dv = whole(2, False), whole(3, False)
    grads = (nt(feat_t, dq_t), nn(feat_t, dk), nn(feat_t, dv), nn(out_t, cot))
    return (out_t, dq_t, dk, dv), grads


def results(out_t, dq_t, dk, dv, w_qkv):
    dfeat_t = nn(w_qkv[:, :C], dq_t) + nt(w_qkv[:, C : 2 * C], dk) + nt(w_qkv[:, 2 * C :], dv)
    return out_t, dfeat_t.astype(BF)


def z_body(feat, cot, w_qkv, w_qkv_t, w_out, back, grad):
    parts, terms = axis_math(z_line, feat[...], cot[...], w_qkv, w_qkv_t, w_out)
    eye = onehot(down(T), along(T))
    for at, part_t in enumerate(results(*parts, w_qkv)):
        back[:, at * C : (at + 1) * C] = nt(eye, part_t).astype(BF)
    for at, term in enumerate(terms):
        grad[:, at * C : (at + 1) * C] = term.astype(BF)


def lines_body(got, w_qkv, w_qkv_t, w_out, grad_z, *refs):
    keep, give, total = refs[8:]
    for part in range(2):
        t = place(down(T), part)
        first, second = onehot(t, along(T)), onehot(t, along(T) + T)
        feat = (nn(first, got[:, :C]) + nn(second, got[:, 2 * C : 3 * C])).astype(BF)
        cot = (nn(first, got[:, C : 2 * C]) + nn(second, got[:, 3 * C :])).astype(BF)
        held, terms = axis_math(long_line, feat, cot, w_qkv, w_qkv_t, w_out)
        for ref, value in zip(refs[part * 4 : part * 4 + 4], held):
            ref[...] = value
        for at, term in enumerate(terms):
            cols = slice(at * C, (at + 1) * C)
            total[:, cols] = (total[:, cols] if part else grad_z[:, cols].astype(F32)) + term
    mine = core()
    keep[...] = total[pl.ds(pl.multiple_of(mine * 128, 128), 128)]
    give[...] = total[pl.ds(pl.multiple_of((1 - mine) * 128, 128), 128)].astype(BF)


def back_body(*refs):
    w_qkv, back_out, back_feat = refs[8:]
    sums = [jnp.zeros((T, C), F32)] * 4
    for part in range(2):
        t = place(along(T), part)
        first, second = onehot(down(T), t), onehot(down(T) + T, t)
        out_t, feat_t = results(*[ref[...] for ref in refs[part * 4 : part * 4 + 4]], w_qkv)
        new = (nt(first, out_t), nt(second, out_t), nt(first, feat_t), nt(second, feat_t))
        sums = [a + b for a, b in zip(sums, new)]
    back_out[:, :C], back_out[:, C:] = sums[0].astype(BF), sums[1].astype(BF)
    back_feat[:, :C], back_feat[:, C:] = sums[2].astype(BF), sums[3].astype(BF)


def first_pack_body(back_out, keep, took, send):
    send[:, : 2 * C] = back_out[...]
    half = (keep[...] + took[...].astype(F32)).astype(BF)
    send[:128, 2 * C :] = half[:, : 2 * C]
    send[128:, 2 * C :] = half[:, 2 * C :]


def block_body(got, send):
    block = jnp.sum(got[:, 2 * C :].astype(F32).reshape(32, 8, 2 * C), axis=0)
    send[...] = jnp.concatenate([block] * 8, axis=0).astype(BF)


def last_pack_body(factor, got, back_feat, send):
    block = jnp.sum(got[...].astype(F32).reshape(8, 8, 2 * C), axis=0) * factor
    send[:, : 2 * C] = back_feat[...]
    send[:, 2 * C :] = jnp.concatenate([block] * 32, axis=0).astype(BF)


def give_body(got_first, got_last, give):
    give[:, :C] = got_first[:, C : 2 * C]
    give[:, C : 2 * C] = got_last[:, C : 2 * C]
    give[:, 2 * C :] = got_last[:, 2 * C :]


def final_body(back_z, got_first, got_last, took, w_out, update, grad_in, grad_qkv, grad_out):
    r = along(T)
    put_mine = onehot(down(T), by_core(y_source(r), x_source(r)))
    put_theirs = onehot(down(T), by_core(x_source(r), y_source(r)))
    sums = []
    for at, rows in enumerate((got_first[:, :C], got_last[:, :C])):
        cols = slice(at * C, (at + 1) * C)
        sums.append(
            (
                back_z[:, cols].astype(F32) + nn(put_mine, rows) + nn(put_theirs, took[:, cols])
            ).astype(BF)
        )
    update[...] = nn(sums[0], w_out[...]).astype(BF)
    grad_in[...] = sums[1]
    for src, half in ((got_last, core()), (took, 1 - core())):
        rows = pl.ds(pl.multiple_of(half * 128, 128), 128)
        grad_qkv[rows, : 2 * C] = src[:128, 2 * C :].astype(F32)
        grad_qkv[rows, 2 * C :] = src[128:, 2 * C : 3 * C].astype(F32)
        grad_out[rows, :] = src[128:, 3 * C :].astype(F32)


def call(body, outs, flops, *args, space=pltpu.VMEM, scratch=(), grant=40 * 2**20):
    return pl.pallas_call(
        body,
        out_shape=outs,
        in_specs=[pl.BlockSpec(memory_space=space)] * len(args),
        out_specs=[pl.BlockSpec(memory_space=space)] * len(outs),
        scratch_shapes=scratch,
        compiler_params=pltpu.CompilerParams(vmem_limit_bytes=grant),
        cost_estimate=pl.CostEstimate(flops=flops, bytes_accessed=2**20, transcendentals=2**19),
    )(*args)


def shape(rows, cols, dtype):
    return jax.ShapeDtypeStruct((rows, cols), dtype)


AXES = ("dp", "row", "col")


def device(x, mine, y, z):
    return z % 2 * 256 + (x * 2 + mine) * 32 + y * 4 + z // 2


X, Y, ZS = range(4), range(8), range(8)
LONG = [[device(x, 0, y, z) for y in Y for z in ZS[dp::2]] for x in X for dp in range(2)] + [
    [device(x, 1, y, z) for x in X for z in ZS] for y in Y
]
SHORT = [
    [device(x, 0, y, 2 * z + dp) for x in X for dp in range(2)] for y in Y for z in range(4)
] + [[device(x, 1, y, z) for y in Y] for x in X for z in ZS]


def exchange(rows, groups):
    return lax.all_to_all(
        rows, AXES, split_axis=0, concat_axis=0, axis_index_groups=groups, tiled=True
    )


def swap(rows):
    return lax.ppermute(rows, "row", [(i, i ^ 1) for i in range(8)])


def body(features, w_qkv, w_out, cotangent):
    local_shape = features.shape
    feat = features.reshape(T, C)
    cot = cotangent.reshape(T, C)
    weights = (w_qkv, w_qkv.T, w_out)
    cube = 2 * T * T * C
    pair = shape(T, 2 * C, BF)
    quad = shape(T, 4 * C, BF)
    mine, give = call(
        pack_body,
        [pair, pair],
        cube * 4,
        feat,
        cot,
        space=pltpu.HBM,
        scratch=[
            pltpu.VMEM((T, C), BF),
            pltpu.VMEM((T, C), BF),
            pltpu.VMEM((T, 2 * C), BF),
            pltpu.VMEM((T, 2 * C), BF),
            pltpu.SemaphoreType.DMA((4,)),
        ],
        grant=None,
    )
    (send,) = call(merge_body, [quad], 2**20, mine, swap(give))
    got = exchange(send, LONG)
    back_z, grad_z = call(z_body, [pair, shape(C, 4 * C, BF)], cube * 70, feat, cot, *weights)
    *held, keep, give = call(
        lines_body,
        [shape(T, C, BF)] * 8 + [shape(128, 4 * C, F32), shape(128, 4 * C, BF)],
        cube * 140,
        got,
        *weights,
        grad_z,
        scratch=[pltpu.VMEM((C, 4 * C), F32)],
    )
    took = swap(give)
    back_out, back_feat = call(back_body, [pair] * 2, cube * 20, *held, w_qkv)
    (send,) = call(first_pack_body, [quad], 2**20, back_out, keep, took)
    got_first = exchange(send, LONG)
    (send,) = call(block_body, [shape(64, 2 * C, BF)], 2**20, got_first)
    blocks = exchange(send, SHORT)
    factor = 1.0 / math.sqrt(PATCHES * 64 * 64 * 16)
    (send,) = call(functools.partial(last_pack_body, factor), [quad], 2**20, blocks, back_feat)
    got_last = exchange(send, LONG)
    (give,) = call(give_body, [quad], 2**20, got_first, got_last)
    update, grad_in, grad_qkv, grad_out = call(
        final_body,
        [shape(T, C, BF)] * 2 + [shape(C, 3 * C, F32), shape(C, C, F32)],
        cube * 6,
        back_z,
        got_first,
        got_last,
        swap(give),
        w_out,
    )
    return (update.reshape(local_shape), grad_in.reshape(local_shape), grad_qkv, grad_out)


def solution(mesh):
    placed = (P("dp", "col", "row", None, None), P(), P(), P("dp", "col", "row", None, None))
    return jax.shard_map(
        body,
        mesh=mesh,
        in_specs=placed,
        out_specs=(P("dp", "col", "row", None, None), P("dp", "col", "row", None, None), P(), P()),
        check_vma=False,
    )
```

time: 110 us -> 110 us (level)
  blocking collectives: 50.3 us -> 56.8 us
  starting transfers between devices: 32.8 us -> 26.8 us
    all_to_all x2 -> x1, starting transfers between devices: 22.2 us -> 7.64 us  [exchange(): lax.all_to_all(rows, AXES, split_axis=0, concat_axis=0, axis_index_groups...]
    ppermute x2 -> x3, starting transfers between devices: 10.6 us -> 19.2 us  [swap(): return lax.ppermute(rows, 'row', [(i, i ^ 1) for i in range(8)])]
    all_to_all x3, blocking collectives: 50.3 us -> 56.8 us  [exchange(): lax.all_to_all(rows, AXES, split_axis=0, concat_axis=0, axis_index_groups...]
    all_to_all x2 -> x1, waiting for transfers between devices: 11.9 us -> 8.54 us  [exchange(): lax.all_to_all(rows, AXES, split_axis=0, concat_axis=0, axis_index_groups...]
    ppermute x2 -> x3, waiting for transfers between devices: 0.5 us -> 3.6 us  [swap(): return lax.ppermute(rows, 'row', [(i, i ^ 1) for i in range(8)])]
  transfers between devices with their start and end apart: 4 -> 4, of which waited for: 3 -> 4; matrix products, arithmetic and copies ran while one was open for 0% -> 0% of each run, Pallas kernels for 6% -> 3%
where the time goes in v8:
time: 110 us
  blocking collectives  56.8 us (52%)
  starting transfers between devices  26.8 us (24%)
  waiting for transfers between devices  12.1 us (11%)
  Pallas kernels  11.5 us (10%)
  local copies, waits for them, and re-layouts  1.96 us (2%)
    all_to_all x3, blocking collectives, exchange(): lax.all_to_all(rows, AXES, split_axis=0, concat_axis=0, axis_index_groups...  56.8 us
    ppermute x3, starting transfers between devices, swap(): return lax.ppermute(rows, 'row', [(i, i ^ 1) for i in range(8)])  19.2 us
    pallas_call x10, Pallas kernels, call(): pl.pallas_call(body, out_shape=outs, in_specs=[pl.BlockSpec(memory_space=...  11.5 us
    all_to_all x1, waiting for transfers between devices, exchange(): lax.all_to_all(rows, AXES, split_axis=0, concat_axis=0, axis_index_groups...  8.54 us
    all_to_all x1, starting transfers between devices, exchange(): lax.all_to_all(rows, AXES, split_axis=0, concat_axis=0, axis_index_groups...  7.64 us
    ppermute x3, waiting for transfers between devices, swap(): return lax.ppermute(rows, 'row', [(i, i ^ 1) for i in range(8)])  3.6 us
  transfers between devices with their start and end apart: 4, of which 4 were waited for; matrix products, arithmetic and copies ran while one was open for 0% of the time, Pallas kernels for 3%

profile of v8, /device:TPU:1, one launch (start us, length us, event | category | flops | bytes accessed | tf_op | source)
XLA Modules:
  0.0 110.0 jit_solution(10348950036950130321)
XLA Ops:
  0.6 2.0 %shard_map.76 = (bf16[256,512]{1,0:T(8,128)(2,1)}, bf16[256,512]{1,0:T(8,128)(2,1)}) custom-call(bf16[256,256]{1,0:T(8,128)(2,1)} %bitcast.25, bf16[256,256]{1,0:T(8,128)(2,1)} %bitcast.27), custom_call_target="tpu_custom_call" | custom-call | flops 134217728 | bytes 1048576 | tf_op jit(solution)/shard_map/pallas_call | solution.py:273
  2.7 8.8 %collective-permute-start = (bf16[256,512]{1,0:T(8,128)(2,1)}, bf16[256,512]{1,0:T(8,128)(2,1)S(1)}, u32[]{:S(2)}, u32[]{:S(2)}) collective-permute-start(bf16[256,512]{1,0:T(8,128)(2,1)} %get-tuple-element.26), channel_id=1, source_target_pairs={{0,32},{32,0},{64,96},{96,64},{128,160},{160,128},{192,224},{224,1... | collective-permute-start | bytes 786440 | tf_op jit(solution)/shard_map/ppermute | solution.py:311
  11.5 1.4 %collective-permute-done.took = bf16[256,512]{1,0:T(8,128)(2,1)S(1)} collective-permute-done((bf16[256,512]{1,0:T(8,128)(2,1)}, bf16[256,512]{1,0:T(8,128)(2,1)S(1)}, u32[]{:S(2)}, u32[]{:S(2)}) %collective-permute-start) | collective-permute-done | bytes 262176 | tf_op jit(solution)/shard_map/ppermute | solution.py:311
  12.8 0.0 copy-start.1
  12.8 0.9 copy-done.1
  13.8 0.8 shard_map.77
  14.6 0.0 copy-start
  14.6 7.6 %all-to-all-start = ((bf16[32,8,1024]{2,1,0:T(8,128)(2,1)}), bf16[32,8,1024]{2,1,0:T(8,128)(2,1)S(1)}, u32[]{:S(2)}, u32[]{:S(2)}) async-start(bf16[32,8,1024]{2,1,0:T(8,128)(2,1)} %bitcast.3), calls=%async_computation | async-start | bytes 1048576 | tf_op jit(solution)/shard_map/all_to_all | solution.py:305
  22.2 0.0 copy-done
  22.3 0.0 copy-start.2
  22.3 0.0 copy-start.3
  22.3 0.0 copy-start.4
  22.3 0.2 copy.8
  22.5 0.7 copy-done.2
  23.2 0.1 copy-done.3
  23.2 0.1 copy-done.4
  23.3 2.2 %shard_map.75 = (bf16[256,512]{1,0:T(8,128)(2,1)S(1)}, bf16[256,1024]{1,0:T(8,128)(2,1)S(1)}) custom-call(bf16[256,256]{1,0:T(8,128)(2,1)S(1)} %bitcast.26, bf16[256,256]{1,0:T(8,128)(2,1)S(1)} %bitcast.28, bf16[256,768]{1,0:T(8,128)(2,1)S(1)} %copy-done, bf16[768,256]{1,0:T(8,128)(2,1)S(1)} %bitcast.21, bf16[256,256]{1,0:T(8,128)(2,1)S(1)} %copy-done.2), custom_call_target="tpu_custom_call" | custom-call | flops 2348810240 | bytes 1048576 | tf_op jit(solution)/shard_map/pallas_call | solution.py:273
  25.5 8.5 %all-to-all-done = bf16[32,8,1024]{2,1,0:T(8,128)(2,1)S(1)} async-done(((bf16[32,8,1024]{2,1,0:T(8,128)(2,1)}), bf16[32,8,1024]{2,1,0:T(8,128)(2,1)S(1)}, u32[]{:S(2)}, u32[]{:S(2)}) %all-to-all-start) | async-done | bytes 524320 | tf_op jit(solution)/shard_map/all_to_all | solution.py:305
  34.0 4.1 %shard_map.78 = (bf16[256,256]{1,0:T(8,128)(2,1)S(1)}, bf16[256,256]{1,0:T(8,128)(2,1)S(1)}, bf16[256,256]{1,0:T(8,128)(2,1)S(1)}, bf16[256,256]{1,0:T(8,128)(2,...) custom-call(bf16[256,1024]{1,0:T(8,128)(2,1)S(1)} %bitcast.19, ...), custom_call_target="tpu_custom_call" | custom-call | flops 4697620480 | bytes 1048576 | tf_op jit(solution)/shard_map/pallas_call | solution.py:273
  38.2 8.5 %collective-permute-start.1 = (bf16[128,1024]{1,0:T(8,128)(2,1)S(1)}, bf16[128,1024]{1,0:T(8,128)(2,1)S(1)}, u32[]{:S(2)}, u32[]{:S(2)}) collective-permute-start(bf16[128,1024]{1,0:T(8,128)(2,1)S(1)} %get-tuple-element.38), channel_id=1, source_target_pairs={{0,32},{32,0},{64,96},{96,64},{128,160},{160,128},{192,224},{224,1... | collective-permute-start | bytes 786440 | tf_op jit(solution)/shard_map/ppermute | solution.py:311
  46.6 0.8 shard_map.79
  47.4 0.4 collective-permute-done.1.took
  47.8 0.1 shard_map.80
  47.8 24.3 %all_to_all.44 = bf16[32,8,1024]{2,1,0:T(8,128)(2,1)S(1)} all-to-all(bf16[32,8,1024]{2,1,0:T(8,128)(2,1)S(1)} %bitcast.18), channel_id=1, replica_groups={{0,1,2,3,4,5,6,7,8,9,10,11,12,13,14,15,16,17,18,19,20,21,22,23,24,25,26..., dimensions={0} | all-to-all | bytes 1048576 | tf_op jit(solution)/shard_map/all_to_all | solution.py:305
  72.2 11.0 %all_to_all.45 = bf16[8,8,512]{2,1,0:T(8,128)(2,1)S(1)} all-to-all(bf16[8,8,512]{2,1,0:T(8,128)(2,1)S(1)} %bitcast.24), channel_id=1, replica_groups={{0,256,64,320,128,384,192,448},{1,257,65,321,129,385,193,449},{2,258,66..., dimensions={0} | all-to-all | bytes 131072 | tf_op jit(solution)/shard_map/all_to_all | solution.py:305
  83.2 21.5 %all_to_all.46 = bf16[32,8,1024]{2,1,0:T(8,128)(2,1)S(1)} all-to-all(bf16[32,8,1024]{2,1,0:T(8,128)(2,1)S(1)} %bitcast.20), channel_id=1, replica_groups={{0,1,2,3,4,5,6,7,8,9,10,11,12,13,14,15,16,17,18,19,20,21,22,23,24,25,26..., dimensions={0} | all-to-all | bytes 1048576 | tf_op jit(solution)/shard_map/all_to_all | solution.py:305
  104.8 1.9 %collective-permute-start.2 = (bf16[256,1024]{1,0:T(8,128)(2,1)S(1)}, bf16[256,1024]{1,0:T(8,128)(2,1)S(1)}, u32[]{:S(2)}, u32[]{:S(2)}) collective-permute-start(bf16[256,1024]{1,0:T(8,128)(2,1)S(1)} %shard_map.83), channel_id=1, source_target_pairs={{0,32},{32,0},{64,96},{96,64},{128,160},{160,128},{192,224},{224,1... | collective-permute-start | bytes 1572872 | tf_op jit(solution)/shard_map/ppermute | solution.py:311
  106.7 1.9 %collective-permute-done.2.took = bf16[256,1024]{1,0:T(8,128)(2,1)S(1)} collective-permute-done((bf16[256,1024]{1,0:T(8,128)(2,1)S(1)}, bf16[256,1024]{1,0:T(8,128)(2,1)S(1)}, u32[]{:S(2)}, u32[]{:S(2)}) %collective-permute-start.2) | collective-permute-done | bytes 524320 | tf_op jit(solution)/shard_map/ppermute | solution.py:311
  108.6 1.4 %shard_map.84 = (bf16[256,256]{1,0:T(8,128)(2,1)}, bf16[256,256]{1,0:T(8,128)(2,1)}, f32[256,768]{1,0:T(8,128)}, f32[256,256]{1,0:T(8,128)}) custom-call(bf16[256,512]{1,0:T(8,128)(2,1)S(1)} %get-tuple-element.24.back_z, bf16[256,1024]{1,0:T(8,128)(2,1)S(1)} %bitcast.15, bf16[256,1024]{1,0:T(8,128)(2,1)S(1)} %bitcast.17, ...), custom_call_target="tpu_custom_call" | custom-call | flops 201326592 | bytes 1048576 | tf_op jit(solution)/shard_map/pallas_call | solution.py:273
  (3 shorter events, 0.1 us)
Async XLA Ops:
  2.7 10.1 %collective-permute-start = (bf16[256,512]{1,0:T(8,128)(2,1)}, bf16[256,512]{1,0:T(8,128)(2,1)S(1)}, u32[]{:S(2)}, u32[]{:S(2)}) collective-permute-start(bf16[256,512]{1,0:T(8,128)(2,1)} %get-tuple-element.26), channel_id=1, source_target_pairs={{0,32},{32,0},{64,96},{96,64},{128,160},{160,128},{192,224},{224,1... | collective-permute-start | bytes 786440 | tf_op jit(solution)/shard_map/ppermute | solution.py:311
  12.8 0.9 copy-start.1
  14.6 7.7 %copy-start = (bf16[256,768]{1,0:T(8,128)(2,1)S(1)}, bf16[256,768]{1,0:T(8,128)(2,1)}, u32[]{:S(2)}) copy-start(bf16[256,768]{1,0:T(8,128)(2,1)} %refs_8_.1) | copy-start | bytes 1179652
  14.6 19.4 %all-to-all-start = ((bf16[32,8,1024]{2,1,0:T(8,128)(2,1)}), bf16[32,8,1024]{2,1,0:T(8,128)(2,1)S(1)}, u32[]{:S(2)}, u32[]{:S(2)}) async-start(bf16[32,8,1024]{2,1,0:T(8,128)(2,1)} %bitcast.3), calls=%async_computation | async-start | bytes 1048576 | tf_op jit(solution)/shard_map/all_to_all | solution.py:305
  22.3 0.9 copy-start.2
  22.3 1.0 copy-start.3
  22.3 1.0 copy-start.4
  38.2 9.6 %collective-permute-start.1 = (bf16[128,1024]{1,0:T(8,128)(2,1)S(1)}, bf16[128,1024]{1,0:T(8,128)(2,1)S(1)}, u32[]{:S(2)}, u32[]{:S(2)}) collective-permute-start(bf16[128,1024]{1,0:T(8,128)(2,1)S(1)} %get-tuple-element.38), channel_id=1, source_target_pairs={{0,32},{32,0},{64,96},{96,64},{128,160},{160,128},{192,224},{224,1... | collective-permute-start | bytes 786440 | tf_op jit(solution)/shard_map/ppermute | solution.py:311
  104.8 3.8 %collective-permute-start.2 = (bf16[256,1024]{1,0:T(8,128)(2,1)S(1)}, bf16[256,1024]{1,0:T(8,128)(2,1)S(1)}, u32[]{:S(2)}, u32[]{:S(2)}) collective-permute-start(bf16[256,1024]{1,0:T(8,128)(2,1)S(1)} %shard_map.83), channel_id=1, source_target_pairs={{0,32},{32,0},{64,96},{96,64},{128,160},{160,128},{192,224},{224,1... | collective-permute-start | bytes 1572872 | tf_op jit(solution)/shard_map/ppermute | solution.py:311

commit v9 on v8

--- a/solution.py
+++ b/solution.py
@@ -75,29 +75,15 @@
     return jnp.where(a == b, 1.0, 0.0).astype(BF)
 
 
-def pack_body(feat_hbm, cot_hbm, keep, give, feat, cot, mine, theirs, sem):
-    copies = [
-        pltpu.make_async_copy(feat_hbm, feat, sem.at[0]),
-        pltpu.make_async_copy(cot_hbm, cot, sem.at[1]),
-    ]
-    for copy in copies:
-        copy.start()
+def pack_body(feat, cot, mine, theirs):
     r = down(T)
-    pick_mine = onehot(by_core(y_source(r), x_source(r)), along(T))
-    pick_theirs = onehot(by_core(x_source(r), y_source(r)), along(T))
-    for copy in copies:
-        copy.wait()
-    for pick, rows in ((pick_theirs, theirs), (pick_mine, mine)):
-        rows[:, :C] = nn(pick, feat[...]).astype(BF)
-        rows[:, C:] = nn(pick, cot[...]).astype(BF)
-    outs = [
-        pltpu.make_async_copy(theirs, give, sem.at[2]),
-        pltpu.make_async_copy(mine, keep, sem.at[3]),
-    ]
-    for out in outs:
-        out.start()
-    for out in outs:
-        out.wait()
+    for out, source in (
+        (theirs, by_core(x_source(r), y_source(r))),
+        (mine, by_core(y_source(r), x_source(r))),
+    ):
+        pick = onehot(source, along(T))
+        out[:, :C] = nn(pick, feat[...]).astype(BF)
+        out[:, C:] = nn(pick, cot[...]).astype(BF)
 
 
 def merge_body(mine, took, send):
@@ -269,14 +255,14 @@
         grad_out[rows, :] = src[128:, 3 * C :].astype(F32)
 
 
-def call(body, outs, flops, *args, space=pltpu.VMEM, scratch=(), grant=40 * 2**20):
+def call(body, outs, flops, *args, scratch=()):
     return pl.pallas_call(
         body,
         out_shape=outs,
-        in_specs=[pl.BlockSpec(memory_space=space)] * len(args),
-        out_specs=[pl.BlockSpec(memory_space=space)] * len(outs),
+        in_specs=[pl.BlockSpec(memory_space=pltpu.VMEM)] * len(args),
+        out_specs=[pl.BlockSpec(memory_space=pltpu.VMEM)] * len(outs),
         scratch_shapes=scratch,
-        compiler_params=pltpu.CompilerParams(vmem_limit_bytes=grant),
+        compiler_params=pltpu.CompilerParams(vmem_limit_bytes=40 * 2**20),
         cost_estimate=pl.CostEstimate(flops=flops, bytes_accessed=2**20, transcendentals=2**19),
     )(*args)
 
@@ -319,22 +305,7 @@
     cube = 2 * T * T * C
     pair = shape(T, 2 * C, BF)
     quad = shape(T, 4 * C, BF)
-    mine, give = call(
-        pack_body,
-        [pair, pair],
-        cube * 4,
-        feat,
-        cot,
-        space=pltpu.HBM,
-        scratch=[
-            pltpu.VMEM((T, C), BF),
-            pltpu.VMEM((T, C), BF),
-            pltpu.VMEM((T, 2 * C), BF),
-            pltpu.VMEM((T, 2 * C), BF),
-            pltpu.SemaphoreType.DMA((4,)),
-        ],
-        grant=None,
-    )
+    mine, give = call(pack_body, [pair, pair], cube * 4, feat, cot)
     (send,) = call(merge_body, [quad], 2**20, mine, swap(give))
     got = exchange(send, LONG)
     back_z, grad_z = call(z_body, [pair, shape(C, 4 * C, BF)], cube * 70, feat, cot, *weights)

time: 110 us -> 109 us (level)
  Pallas kernels: 11.5 us -> 9.83 us
    pallas_call x10, Pallas kernels: 11.5 us -> 9.83 us  [call(): pl.pallas_call(body, out_shape=outs, in_specs=[pl.BlockSpec(memory_space=...]
    unnamed x11 -> x13, local copies, waits for them, and re-layouts: 1.96 us -> 2.82 us
where the time goes in v9:
time: 109 us
  blocking collectives  56.8 us (52%)
  starting transfers between devices  26.8 us (25%)
  waiting for transfers between devices  11.9 us (11%)
  Pallas kernels  9.83 us (9%)
  local copies, waits for them, and re-layouts  2.82 us (3%)
    all_to_all x3, blocking collectives, exchange(): lax.all_to_all(rows, AXES, split_axis=0, concat_axis=0, axis_index_groups...  56.8 us
    ppermute x3, starting transfers between devices, swap(): return lax.ppermute(rows, 'row', [(i, i ^ 1) for i in range(8)])  19.2 us
    pallas_call x10, Pallas kernels, call(): pl.pallas_call(body, out_shape=outs, in_specs=[pl.BlockSpec(memory_space=...  9.83 us
    all_to_all x1, waiting for transfers between devices, exchange(): lax.all_to_all(rows, AXES, split_axis=0, concat_axis=0, axis_index_groups...  8.54 us
    all_to_all x1, starting transfers between devices, exchange(): lax.all_to_all(rows, AXES, split_axis=0, concat_axis=0, axis_index_groups...  7.65 us
    ppermute x3, waiting for transfers between devices, swap(): return lax.ppermute(rows, 'row', [(i, i ^ 1) for i in range(8)])  3.39 us
    unnamed x13, local copies, waits for them, and re-layouts  2.82 us
  transfers between devices with their start and end apart: 4, of which 4 were waited for; matrix products, arithmetic and copies ran while one was open for 0% of the time, Pallas kernels for 3%

profile of v9, /device:TPU:1, one launch (start us, length us, event | category | flops | bytes accessed | tf_op | source)
XLA Modules:
  0.0 108.9 jit_solution(17835280524353784010)
XLA Ops:
  0.6 0.0 copy-start.2
  0.6 0.9 copy-done.2
  1.5 0.0 copy-start.4
  1.5 0.9 copy-done.4
  2.4 0.3 shard_map.76
  2.8 8.8 %collective-permute-start = (bf16[256,512]{1,0:T(8,128)(2,1)S(1)}, bf16[256,512]{1,0:T(8,128)(2,1)S(1)}, u32[]{:S(2)}, u32[]{:S(2)}) collective-permute-start(bf16[256,512]{1,0:T(8,128)(2,1)S(1)} %get-tuple-element.26), channel_id=1, source_target_pairs={{0,32},{32,0},{64,96},{96,64},{128,160},{160,128},{192,224},{224,1... | collective-permute-start | bytes 786440 | tf_op jit(solution)/shard_map/ppermute | solution.py:297
  11.6 1.1 %collective-permute-done.took = bf16[256,512]{1,0:T(8,128)(2,1)S(1)} collective-permute-done((bf16[256,512]{1,0:T(8,128)(2,1)S(1)}, bf16[256,512]{1,0:T(8,128)(2,1)S(1)}, u32[]{:S(2)}, u32[]{:S(2)}) %collective-permute-start) | collective-permute-done | bytes 262176 | tf_op jit(solution)/shard_map/ppermute | solution.py:297
  12.7 0.8 shard_map.77
  13.5 0.0 copy-start
  13.5 7.6 %all-to-all-start = ((bf16[32,8,1024]{2,1,0:T(8,128)(2,1)}), bf16[32,8,1024]{2,1,0:T(8,128)(2,1)S(1)}, u32[]{:S(2)}, u32[]{:S(2)}) async-start(bf16[32,8,1024]{2,1,0:T(8,128)(2,1)} %bitcast.3), calls=%async_computation | async-start | bytes 1048576 | tf_op jit(solution)/shard_map/all_to_all | solution.py:291
  21.2 0.0 copy-done
  21.2 0.0 copy-start.1
  21.2 0.0 copy-start.3
  21.2 0.0 copy-start.5
  21.2 0.2 copy.8
  21.4 0.7 copy-done.1
  22.1 0.1 copy-done.3
  22.2 0.1 copy-done.5
  22.2 2.2 %shard_map.75 = (bf16[256,512]{1,0:T(8,128)(2,1)S(1)}, bf16[256,1024]{1,0:T(8,128)(2,1)S(1)}) custom-call(bf16[256,256]{1,0:T(8,128)(2,1)S(1)} %bitcast.26, bf16[256,256]{1,0:T(8,128)(2,1)S(1)} %bitcast.28, bf16[256,768]{1,0:T(8,128)(2,1)S(1)} %copy-done, bf16[768,256]{1,0:T(8,128)(2,1)S(1)} %bitcast.21, bf16[256,256]{1,0:T(8,128)(2,1)S(1)} %copy-done.1), custom_call_target="tpu_custom_call" | custom-call | flops 2348810240 | bytes 1048576 | tf_op jit(solution)/shard_map/pallas_call | solution.py:259
  24.4 8.5 %all-to-all-done = bf16[32,8,1024]{2,1,0:T(8,128)(2,1)S(1)} async-done(((bf16[32,8,1024]{2,1,0:T(8,128)(2,1)}), bf16[32,8,1024]{2,1,0:T(8,128)(2,1)S(1)}, u32[]{:S(2)}, u32[]{:S(2)}) %all-to-all-start) | async-done | bytes 524320 | tf_op jit(solution)/shard_map/all_to_all | solution.py:291
  33.0 4.1 %shard_map.78 = (bf16[256,256]{1,0:T(8,128)(2,1)S(1)}, bf16[256,256]{1,0:T(8,128)(2,1)S(1)}, bf16[256,256]{1,0:T(8,128)(2,1)S(1)}, bf16[256,256]{1,0:T(8,128)(2,...) custom-call(bf16[256,1024]{1,0:T(8,128)(2,1)S(1)} %bitcast.19, ...), custom_call_target="tpu_custom_call" | custom-call | flops 4697620480 | bytes 1048576 | tf_op jit(solution)/shard_map/pallas_call | solution.py:259
  37.1 8.5 %collective-permute-start.1 = (bf16[128,1024]{1,0:T(8,128)(2,1)S(1)}, bf16[128,1024]{1,0:T(8,128)(2,1)S(1)}, u32[]{:S(2)}, u32[]{:S(2)}) collective-permute-start(bf16[128,1024]{1,0:T(8,128)(2,1)S(1)} %get-tuple-element.38), channel_id=1, source_target_pairs={{0,32},{32,0},{64,96},{96,64},{128,160},{160,128},{192,224},{224,1... | collective-permute-start | bytes 786440 | tf_op jit(solution)/shard_map/ppermute | solution.py:297
  45.6 0.8 shard_map.79
  46.3 0.4 collective-permute-done.1.took
  46.7 0.1 shard_map.80
  46.8 24.3 %all_to_all.44 = bf16[32,8,1024]{2,1,0:T(8,128)(2,1)S(1)} all-to-all(bf16[32,8,1024]{2,1,0:T(8,128)(2,1)S(1)} %bitcast.18), channel_id=1, replica_groups={{0,1,2,3,4,5,6,7,8,9,10,11,12,13,14,15,16,17,18,19,20,21,22,23,24,25,26..., dimensions={0} | all-to-all | bytes 1048576 | tf_op jit(solution)/shard_map/all_to_all | solution.py:291
  71.1 10.9 %all_to_all.45 = bf16[8,8,512]{2,1,0:T(8,128)(2,1)S(1)} all-to-all(bf16[8,8,512]{2,1,0:T(8,128)(2,1)S(1)} %bitcast.24), channel_id=1, replica_groups={{0,256,64,320,128,384,192,448},{1,257,65,321,129,385,193,449},{2,258,66..., dimensions={0} | all-to-all | bytes 131072 | tf_op jit(solution)/shard_map/all_to_all | solution.py:291
  82.1 21.5 %all_to_all.46 = bf16[32,8,1024]{2,1,0:T(8,128)(2,1)S(1)} all-to-all(bf16[32,8,1024]{2,1,0:T(8,128)(2,1)S(1)} %bitcast.20), channel_id=1, replica_groups={{0,1,2,3,4,5,6,7,8,9,10,11,12,13,14,15,16,17,18,19,20,21,22,23,24,25,26..., dimensions={0} | all-to-all | bytes 1048576 | tf_op jit(solution)/shard_map/all_to_all | solution.py:291
  103.7 1.9 %collective-permute-start.2 = (bf16[256,1024]{1,0:T(8,128)(2,1)S(1)}, bf16[256,1024]{1,0:T(8,128)(2,1)S(1)}, u32[]{:S(2)}, u32[]{:S(2)}) collective-permute-start(bf16[256,1024]{1,0:T(8,128)(2,1)S(1)} %shard_map.83), channel_id=1, source_target_pairs={{0,32},{32,0},{64,96},{96,64},{128,160},{160,128},{192,224},{224,1... | collective-permute-start | bytes 1572872 | tf_op jit(solution)/shard_map/ppermute | solution.py:297
  105.6 1.9 %collective-permute-done.2.took = bf16[256,1024]{1,0:T(8,128)(2,1)S(1)} collective-permute-done((bf16[256,1024]{1,0:T(8,128)(2,1)S(1)}, bf16[256,1024]{1,0:T(8,128)(2,1)S(1)}, u32[]{:S(2)}, u32[]{:S(2)}) %collective-permute-start.2) | collective-permute-done | bytes 524320 | tf_op jit(solution)/shard_map/ppermute | solution.py:297
  107.5 1.4 %shard_map.84 = (bf16[256,256]{1,0:T(8,128)(2,1)}, bf16[256,256]{1,0:T(8,128)(2,1)}, f32[256,768]{1,0:T(8,128)}, f32[256,256]{1,0:T(8,128)}) custom-call(bf16[256,512]{1,0:T(8,128)(2,1)S(1)} %get-tuple-element.24.back_z, bf16[256,1024]{1,0:T(8,128)(2,1)S(1)} %bitcast.15, bf16[256,1024]{1,0:T(8,128)(2,1)S(1)} %bitcast.17, ...), custom_call_target="tpu_custom_call" | custom-call | flops 201326592 | bytes 1048576 | tf_op jit(solution)/shard_map/pallas_call | solution.py:259
  (3 shorter events, 0.1 us)
Async XLA Ops:
  0.6 0.9 copy-start.2
  1.5 0.9 copy-start.4
  2.8 9.9 %collective-permute-start = (bf16[256,512]{1,0:T(8,128)(2,1)S(1)}, bf16[256,512]{1,0:T(8,128)(2,1)S(1)}, u32[]{:S(2)}, u32[]{:S(2)}) collective-permute-start(bf16[256,512]{1,0:T(8,128)(2,1)S(1)} %get-tuple-element.26), channel_id=1, source_target_pairs={{0,32},{32,0},{64,96},{96,64},{128,160},{160,128},{192,224},{224,1... | collective-permute-start | bytes 786440 | tf_op jit(solution)/shard_map/ppermute | solution.py:297
  13.5 7.7 %copy-start = (bf16[256,768]{1,0:T(8,128)(2,1)S(1)}, bf16[256,768]{1,0:T(8,128)(2,1)}, u32[]{:S(2)}) copy-start(bf16[256,768]{1,0:T(8,128)(2,1)} %refs_8_.1) | copy-start | bytes 1179652
  13.5 19.4 %all-to-all-start = ((bf16[32,8,1024]{2,1,0:T(8,128)(2,1)}), bf16[32,8,1024]{2,1,0:T(8,128)(2,1)S(1)}, u32[]{:S(2)}, u32[]{:S(2)}) async-start(bf16[32,8,1024]{2,1,0:T(8,128)(2,1)} %bitcast.3), calls=%async_computation | async-start | bytes 1048576 | tf_op jit(solution)/shard_map/all_to_all | solution.py:291
  21.2 0.9 copy-start.1
  21.2 1.0 copy-start.3
  21.2 1.0 copy-start.5
  37.1 9.6 %collective-permute-start.1 = (bf16[128,1024]{1,0:T(8,128)(2,1)S(1)}, bf16[128,1024]{1,0:T(8,128)(2,1)S(1)}, u32[]{:S(2)}, u32[]{:S(2)}) collective-permute-start(bf16[128,1024]{1,0:T(8,128)(2,1)S(1)} %get-tuple-element.38), channel_id=1, source_target_pairs={{0,32},{32,0},{64,96},{96,64},{128,160},{160,128},{192,224},{224,1... | collective-permute-start | bytes 786440 | tf_op jit(solution)/shard_map/ppermute | solution.py:297
  103.7 3.8 %collective-permute-start.2 = (bf16[256,1024]{1,0:T(8,128)(2,1)S(1)}, bf16[256,1024]{1,0:T(8,128)(2,1)S(1)}, u32[]{:S(2)}, u32[]{:S(2)}) collective-permute-start(bf16[256,1024]{1,0:T(8,128)(2,1)S(1)} %shard_map.83), channel_id=1, source_target_pairs={{0,32},{32,0},{64,96},{96,64},{128,160},{160,128},{192,224},{224,1... | collective-permute-start | bytes 1572872 | tf_op jit(solution)/shard_map/ppermute | solution.py:297

commit v10 on v9

--- a/solution.py
+++ b/solution.py
@@ -55,11 +55,10 @@
     return ((r >> 7) << 7) + ((r & 7) << 4) + ((r >> 3) & 15)
 
 
-def place(t, part):
+def place(t):
     line, at = t >> 6, t & 63
-    y_place = (part << 8) + ((at >> 1) << 3) + ((at & 1) << 2) + line
-    x_peer = ((at >> 4) << 3) + (part << 2) + line
-    x_place = (((at >> 3) & 1) << 8) + (x_peer << 3) + (at & 7)
+    y_place = ((line >> 2) << 8) + ((at >> 1) << 3) + ((at & 1) << 2) + (line & 3)
+    x_place = (((at >> 3) & 1) << 8) + ((at >> 4) << 6) + (line << 3) + (at & 7)
     return by_core(y_place, x_place)
 
 
@@ -131,9 +130,10 @@
             axis=0,
         )
 
+    halves = feat.shape[0] // HALF
     blocks = [
         (slice(half * HALF, (half + 1) * HALF), slice(quad * HALF, (quad + 1) * HALF))
-        for half in range(2)
+        for half in range(halves)
         for quad in range(2)
     ]
     all_scores = [nn(k[t, c], spread(q_t[c, t])) + bias for t, c in blocks]
@@ -154,9 +154,9 @@
         parts.append([m.astype(BF) for m in (out_t, dq_t, dk, dv)])
 
     def whole(at, transposed):
-        p = [[parts[2 * half + quad][at] for quad in range(2)] for half in range(2)]
+        p = [[parts[2 * half + quad][at] for quad in range(2)] for half in range(halves)]
         if transposed:
-            p = [[p[j][i] for j in range(2)] for i in range(2)]
+            p = [list(row) for row in zip(*p)]
         return jnp.concatenate([jnp.concatenate(r, axis=1) for r in p], axis=0)
 
     out_t, dq_t = whole(0, True), whole(1, True)
@@ -179,35 +179,27 @@
         grad[:, at * C : (at + 1) * C] = term.astype(BF)
 
 
-def lines_body(got, w_qkv, w_qkv_t, w_out, grad_z, *refs):
-    keep, give, total = refs[8:]
-    for part in range(2):
-        t = place(down(T), part)
-        first, second = onehot(t, along(T)), onehot(t, along(T) + T)
-        feat = (nn(first, got[:, :C]) + nn(second, got[:, 2 * C : 3 * C])).astype(BF)
-        cot = (nn(first, got[:, C : 2 * C]) + nn(second, got[:, 3 * C :])).astype(BF)
-        held, terms = axis_math(long_line, feat, cot, w_qkv, w_qkv_t, w_out)
-        for ref, value in zip(refs[part * 4 : part * 4 + 4], held):
-            ref[...] = value
-        for at, term in enumerate(terms):
-            cols = slice(at * C, (at + 1) * C)
-            total[:, cols] = (total[:, cols] if part else grad_z[:, cols].astype(F32)) + term
+def lines_body(got, w_qkv, w_qkv_t, w_out, grad_z, out_t, dq_t, dk, dv, keep, give, total):
+    sort = onehot(place(down(2 * T)), along(2 * T))
+    feat = nn(sort, jnp.concatenate([got[:, :C], got[:, 2 * C : 3 * C]], axis=0)).astype(BF)
+    cot = nn(sort, jnp.concatenate([got[:, C : 2 * C], got[:, 3 * C :]], axis=0)).astype(BF)
+    held, terms = axis_math(long_line, feat, cot, w_qkv, w_qkv_t, w_out)
+    for ref, value in zip((out_t, dq_t, dk, dv), held):
+        ref[...] = value
+    for at, term in enumerate(terms):
+        cols = slice(at * C, (at + 1) * C)
+        total[:, cols] = grad_z[:, cols].astype(F32) + term
     mine = core()
     keep[...] = total[pl.ds(pl.multiple_of(mine * 128, 128), 128)]
     give[...] = total[pl.ds(pl.multiple_of((1 - mine) * 128, 128), 128)].astype(BF)
 
 
-def back_body(*refs):
-    w_qkv, back_out, back_feat = refs[8:]
-    sums = [jnp.zeros((T, C), F32)] * 4
-    for part in range(2):
-        t = place(along(T), part)
-        first, second = onehot(down(T), t), onehot(down(T) + T, t)
-        out_t, feat_t = results(*[ref[...] for ref in refs[part * 4 : part * 4 + 4]], w_qkv)
-        new = (nt(first, out_t), nt(second, out_t), nt(first, feat_t), nt(second, feat_t))
-        sums = [a + b for a, b in zip(sums, new)]
-    back_out[:, :C], back_out[:, C:] = sums[0].astype(BF), sums[1].astype(BF)
-    back_feat[:, :C], back_feat[:, C:] = sums[2].astype(BF), sums[3].astype(BF)
+def back_body(out_t, dq_t, dk, dv, w_qkv, back_out, back_feat):
+    unsort = onehot(down(2 * T), place(along(2 * T)))
+    parts = results(out_t[...], dq_t[...], dk[...], dv[...], w_qkv)
+    for part_t, back in zip(parts, (back_out, back_feat)):
+        rows = nt(unsort, part_t).astype(BF)
+        back[:, :C], back[:, C:] = rows[:T], rows[T:]
 
 
 def first_pack_body(back_out, keep, took, send):
@@ -311,7 +303,9 @@
     back_z, grad_z = call(z_body, [pair, shape(C, 4 * C, BF)], cube * 70, feat, cot, *weights)
     *held, keep, give = call(
         lines_body,
-        [shape(T, C, BF)] * 8 + [shape(128, 4 * C, F32), shape(128, 4 * C, BF)],
+        [shape(C, 2 * T, BF)] * 2
+        + [shape(2 * T, C, BF)] * 2
+        + [shape(128, 4 * C, F32), shape(128, 4 * C, BF)],
         cube * 140,
         got,
         *weights,

time: 109 us -> 109 us (level)
  no operation moved by 1% of the time
where the time goes in v10:
time: 109 us
  blocking collectives  56.8 us (52%)
  starting transfers between devices  26.8 us (25%)
  waiting for transfers between devices  11.9 us (11%)
  Pallas kernels  9.57 us (9%)
  local copies, waits for them, and re-layouts  2.82 us (3%)
    all_to_all x3, blocking collectives, exchange(): lax.all_to_all(rows, AXES, split_axis=0, concat_axis=0, axis_index_groups...  56.8 us
    ppermute x3, starting transfers between devices, swap(): return lax.ppermute(rows, 'row', [(i, i ^ 1) for i in range(8)])  19.2 us
    pallas_call x10, Pallas kernels, call(): pl.pallas_call(body, out_shape=outs, in_specs=[pl.BlockSpec(memory_space=...  9.57 us
    all_to_all x1, waiting for transfers between devices, exchange(): lax.all_to_all(rows, AXES, split_axis=0, concat_axis=0, axis_index_groups...  8.54 us
    all_to_all x1, starting transfers between devices, exchange(): lax.all_to_all(rows, AXES, split_axis=0, concat_axis=0, axis_index_groups...  7.65 us
    ppermute x3, waiting for transfers between devices, swap(): return lax.ppermute(rows, 'row', [(i, i ^ 1) for i in range(8)])  3.36 us
    unnamed x13, local copies, waits for them, and re-layouts  2.82 us
  transfers between devices with their start and end apart: 4, of which 4 were waited for; matrix products, arithmetic and copies ran while one was open for 0% of the time, Pallas kernels for 3%

profile of v10, /device:TPU:1, one launch (start us, length us, event | category | flops | bytes accessed | tf_op | source)
XLA Modules:
  0.0 108.6 jit_solution(5217523369170985929)
XLA Ops:
  0.6 0.0 copy-start.2
  0.6 0.9 copy-done.2
  1.5 0.0 copy-start.4
  1.5 0.9 copy-done.4
  2.4 0.3 shard_map.76
  2.8 8.8 %collective-permute-start = (bf16[256,512]{1,0:T(8,128)(2,1)S(1)}, bf16[256,512]{1,0:T(8,128)(2,1)S(1)}, u32[]{:S(2)}, u32[]{:S(2)}) collective-permute-start(bf16[256,512]{1,0:T(8,128)(2,1)S(1)} %get-tuple-element.22), channel_id=1, source_target_pairs={{0,32},{32,0},{64,96},{96,64},{128,160},{160,128},{192,224},{224,1... | collective-permute-start | bytes 786440 | tf_op jit(solution)/shard_map/ppermute | solution.py:289
  11.6 1.1 %collective-permute-done.took = bf16[256,512]{1,0:T(8,128)(2,1)S(1)} collective-permute-done((bf16[256,512]{1,0:T(8,128)(2,1)S(1)}, bf16[256,512]{1,0:T(8,128)(2,1)S(1)}, u32[]{:S(2)}, u32[]{:S(2)}) %collective-permute-start) | collective-permute-done | bytes 262176 | tf_op jit(solution)/shard_map/ppermute | solution.py:289
  12.7 0.8 shard_map.77
  13.5 0.0 copy-start
  13.5 7.6 %all-to-all-start = ((bf16[32,8,1024]{2,1,0:T(8,128)(2,1)}), bf16[32,8,1024]{2,1,0:T(8,128)(2,1)S(1)}, u32[]{:S(2)}, u32[]{:S(2)}) async-start(bf16[32,8,1024]{2,1,0:T(8,128)(2,1)} %bitcast.3), calls=%async_computation | async-start | bytes 1048576 | tf_op jit(solution)/shard_map/all_to_all | solution.py:283
  21.2 0.0 copy-done
  21.2 0.0 copy-start.1
  21.2 0.0 copy-start.3
  21.2 0.0 copy-start.5
  21.2 0.2 copy.8
  21.4 0.7 copy-done.1
  22.1 0.1 copy-done.3
  22.2 0.1 copy-done.5
  22.2 2.2 %shard_map.75 = (bf16[256,512]{1,0:T(8,128)(2,1)S(1)}, bf16[256,1024]{1,0:T(8,128)(2,1)S(1)}) custom-call(bf16[256,256]{1,0:T(8,128)(2,1)S(1)} %bitcast.26, bf16[256,256]{1,0:T(8,128)(2,1)S(1)} %bitcast.28, bf16[256,768]{1,0:T(8,128)(2,1)S(1)} %copy-done, bf16[768,256]{1,0:T(8,128)(2,1)S(1)} %bitcast.21, bf16[256,256]{1,0:T(8,128)(2,1)S(1)} %copy-done.1), custom_call_target="tpu_custom_call" | custom-call | flops 2348810240 | bytes 1048576 | tf_op jit(solution)/shard_map/pallas_call | solution.py:251
  24.4 8.5 %all-to-all-done = bf16[32,8,1024]{2,1,0:T(8,128)(2,1)S(1)} async-done(((bf16[32,8,1024]{2,1,0:T(8,128)(2,1)}), bf16[32,8,1024]{2,1,0:T(8,128)(2,1)S(1)}, u32[]{:S(2)}, u32[]{:S(2)}) %all-to-all-start) | async-done | bytes 524320 | tf_op jit(solution)/shard_map/all_to_all | solution.py:283
  33.0 3.8 %shard_map.78 = (bf16[256,512]{1,0:T(8,128)(2,1)S(1)}, bf16[256,512]{1,0:T(8,128)(2,1)S(1)}, bf16[512,256]{1,0:T(8,128)(2,1)S(1)}, bf16[512,256]{1,0:T(8,128)(2,...) custom-call(bf16[256,1024]{1,0:T(8,128)(2,1)S(1)} %bitcast.19, bf16[256,768]{1,0:T(8,128)(2,1)S(1)} %copy-done, ...), custom_call_target="tpu_custom_call" | custom-call | flops 4697620480 | bytes 1048576 | tf_op jit(solution)/shard_map/pallas_call | solution.py:251
  36.8 8.5 %collective-permute-start.1 = (bf16[128,1024]{1,0:T(8,128)(2,1)S(1)}, bf16[128,1024]{1,0:T(8,128)(2,1)S(1)}, u32[]{:S(2)}, u32[]{:S(2)}) collective-permute-start(bf16[128,1024]{1,0:T(8,128)(2,1)S(1)} %get-tuple-element.30), channel_id=1, source_target_pairs={{0,32},{32,0},{64,96},{96,64},{128,160},{160,128},{192,224},{224,1... | collective-permute-start | bytes 786440 | tf_op jit(solution)/shard_map/ppermute | solution.py:289
  45.3 0.8 shard_map.79
  46.1 0.3 collective-permute-done.1.took
  46.4 0.1 shard_map.80
  46.5 24.3 %all_to_all.44 = bf16[32,8,1024]{2,1,0:T(8,128)(2,1)S(1)} all-to-all(bf16[32,8,1024]{2,1,0:T(8,128)(2,1)S(1)} %bitcast.18), channel_id=1, replica_groups={{0,1,2,3,4,5,6,7,8,9,10,11,12,13,14,15,16,17,18,19,20,21,22,23,24,25,26..., dimensions={0} | all-to-all | bytes 1048576 | tf_op jit(solution)/shard_map/all_to_all | solution.py:283
  70.8 11.0 %all_to_all.45 = bf16[8,8,512]{2,1,0:T(8,128)(2,1)S(1)} all-to-all(bf16[8,8,512]{2,1,0:T(8,128)(2,1)S(1)} %bitcast.24), channel_id=1, replica_groups={{0,256,64,320,128,384,192,448},{1,257,65,321,129,385,193,449},{2,258,66..., dimensions={0} | all-to-all | bytes 131072 | tf_op jit(solution)/shard_map/all_to_all | solution.py:283
  81.8 21.5 %all_to_all.46 = bf16[32,8,1024]{2,1,0:T(8,128)(2,1)S(1)} all-to-all(bf16[32,8,1024]{2,1,0:T(8,128)(2,1)S(1)} %bitcast.20), channel_id=1, replica_groups={{0,1,2,3,4,5,6,7,8,9,10,11,12,13,14,15,16,17,18,19,20,21,22,23,24,25,26..., dimensions={0} | all-to-all | bytes 1048576 | tf_op jit(solution)/shard_map/all_to_all | solution.py:283
  103.4 1.9 %collective-permute-start.2 = (bf16[256,1024]{1,0:T(8,128)(2,1)S(1)}, bf16[256,1024]{1,0:T(8,128)(2,1)S(1)}, u32[]{:S(2)}, u32[]{:S(2)}) collective-permute-start(bf16[256,1024]{1,0:T(8,128)(2,1)S(1)} %shard_map.83), channel_id=1, source_target_pairs={{0,32},{32,0},{64,96},{96,64},{128,160},{160,128},{192,224},{224,1... | collective-permute-start | bytes 1572872 | tf_op jit(solution)/shard_map/ppermute | solution.py:289
  105.3 1.9 %collective-permute-done.2.took = bf16[256,1024]{1,0:T(8,128)(2,1)S(1)} collective-permute-done((bf16[256,1024]{1,0:T(8,128)(2,1)S(1)}, bf16[256,1024]{1,0:T(8,128)(2,1)S(1)}, u32[]{:S(2)}, u32[]{:S(2)}) %collective-permute-start.2) | collective-permute-done | bytes 524320 | tf_op jit(solution)/shard_map/ppermute | solution.py:289
  107.2 1.4 %shard_map.84 = (bf16[256,256]{1,0:T(8,128)(2,1)}, bf16[256,256]{1,0:T(8,128)(2,1)}, f32[256,768]{1,0:T(8,128)}, f32[256,256]{1,0:T(8,128)}) custom-call(bf16[256,512]{1,0:T(8,128)(2,1)S(1)} %get-tuple-element.20.back_z, bf16[256,1024]{1,0:T(8,128)(2,1)S(1)} %bitcast.15, bf16[256,1024]{1,0:T(8,128)(2,1)S(1)} %bitcast.17, ...), custom_call_target="tpu_custom_call" | custom-call | flops 201326592 | bytes 1048576 | tf_op jit(solution)/shard_map/pallas_call | solution.py:251
  (3 shorter events, 0.1 us)
Async XLA Ops:
  0.6 0.9 copy-start.2
  1.5 0.9 copy-start.4
  2.8 9.9 %collective-permute-start = (bf16[256,512]{1,0:T(8,128)(2,1)S(1)}, bf16[256,512]{1,0:T(8,128)(2,1)S(1)}, u32[]{:S(2)}, u32[]{:S(2)}) collective-permute-start(bf16[256,512]{1,0:T(8,128)(2,1)S(1)} %get-tuple-element.22), channel_id=1, source_target_pairs={{0,32},{32,0},{64,96},{96,64},{128,160},{160,128},{192,224},{224,1... | collective-permute-start | bytes 786440 | tf_op jit(solution)/shard_map/ppermute | solution.py:289
  13.5 7.7 %copy-start = (bf16[256,768]{1,0:T(8,128)(2,1)S(1)}, bf16[256,768]{1,0:T(8,128)(2,1)}, u32[]{:S(2)}) copy-start(bf16[256,768]{1,0:T(8,128)(2,1)} %w_qkv.5) | copy-start | bytes 1179652
  13.5 19.4 %all-to-all-start = ((bf16[32,8,1024]{2,1,0:T(8,128)(2,1)}), bf16[32,8,1024]{2,1,0:T(8,128)(2,1)S(1)}, u32[]{:S(2)}, u32[]{:S(2)}) async-start(bf16[32,8,1024]{2,1,0:T(8,128)(2,1)} %bitcast.3), calls=%async_computation | async-start | bytes 1048576 | tf_op jit(solution)/shard_map/all_to_all | solution.py:283
  21.2 0.9 copy-start.1
  21.2 1.0 copy-start.3
  21.2 1.0 copy-start.5
  36.8 9.6 %collective-permute-start.1 = (bf16[128,1024]{1,0:T(8,128)(2,1)S(1)}, bf16[128,1024]{1,0:T(8,128)(2,1)S(1)}, u32[]{:S(2)}, u32[]{:S(2)}) collective-permute-start(bf16[128,1024]{1,0:T(8,128)(2,1)S(1)} %get-tuple-element.30), channel_id=1, source_target_pairs={{0,32},{32,0},{64,96},{96,64},{128,160},{160,128},{192,224},{224,1... | collective-permute-start | bytes 786440 | tf_op jit(solution)/shard_map/ppermute | solution.py:289
  103.4 3.8 %collective-permute-start.2 = (bf16[256,1024]{1,0:T(8,128)(2,1)S(1)}, bf16[256,1024]{1,0:T(8,128)(2,1)S(1)}, u32[]{:S(2)}, u32[]{:S(2)}) collective-permute-start(bf16[256,1024]{1,0:T(8,128)(2,1)S(1)} %shard_map.83), channel_id=1, source_target_pairs={{0,32},{32,0},{64,96},{96,64},{128,160},{160,128},{192,224},{224,1... | collective-permute-start | bytes 1572872 | tf_op jit(solution)/shard_map/ppermute | solution.py:289

commit v11 on v10

--- a/solution.py
+++ b/solution.py
@@ -74,15 +74,10 @@
     return jnp.where(a == b, 1.0, 0.0).astype(BF)
 
 
-def pack_body(feat, cot, mine, theirs):
-    r = down(T)
-    for out, source in (
-        (theirs, by_core(x_source(r), y_source(r))),
-        (mine, by_core(y_source(r), x_source(r))),
-    ):
-        pick = onehot(source, along(T))
-        out[:, :C] = nn(pick, feat[...]).astype(BF)
-        out[:, C:] = nn(pick, cot[...]).astype(BF)
+def pack_body(first, second, feat, cot, out):
+    pick = onehot(by_core(first(down(T)), second(down(T))), along(T))
+    out[:, :C] = nn(pick, feat[...]).astype(BF)
+    out[:, C:] = nn(pick, cot[...]).astype(BF)
 
 
 def merge_body(mine, took, send):
@@ -226,33 +221,44 @@
     give[:, 2 * C :] = got_last[:, 2 * C :]
 
 
-def final_body(back_z, got_first, got_last, took, w_out, update, grad_in, grad_qkv, grad_out):
+def final_body(
+    back_z, got_first, got_last, took, w_out, update, grad_in, grad_qkv, grad_out, qkv, out, rows, sem
+):
+    copies = []
+
+    def send_home(src, dst):
+        copies.append(pltpu.make_async_copy(src, dst, sem.at[len(copies)]))
+        copies[-1].start()
+
+    for at, (src, half) in enumerate(((got_last, core()), (took, 1 - core()))):
+        place_of = pl.ds(pl.multiple_of(half * 128, 128), 128)
+        qkv[at, :, : 2 * C] = src[:128, 2 * C :].astype(F32)
+        qkv[at, :, 2 * C :] = src[128:, 2 * C : 3 * C].astype(F32)
+        out[at] = src[128:, 3 * C :].astype(F32)
+        send_home(qkv.at[at], grad_qkv.at[place_of])
+        send_home(out.at[at], grad_out.at[place_of])
     r = along(T)
     put_mine = onehot(down(T), by_core(y_source(r), x_source(r)))
     put_theirs = onehot(down(T), by_core(x_source(r), y_source(r)))
-    sums = []
-    for at, rows in enumerate((got_first[:, :C], got_last[:, :C])):
-        cols = slice(at * C, (at + 1) * C)
-        sums.append(
-            (
-                back_z[:, cols].astype(F32) + nn(put_mine, rows) + nn(put_theirs, took[:, cols])
-            ).astype(BF)
-        )
-    update[...] = nn(sums[0], w_out[...]).astype(BF)
-    grad_in[...] = sums[1]
-    for src, half in ((got_last, core()), (took, 1 - core())):
-        rows = pl.ds(pl.multiple_of(half * 128, 128), 128)
-        grad_qkv[rows, : 2 * C] = src[:128, 2 * C :].astype(F32)
-        grad_qkv[rows, 2 * C :] = src[128:, 2 * C : 3 * C].astype(F32)
-        grad_out[rows, :] = src[128:, 3 * C :].astype(F32)
-
-
-def call(body, outs, flops, *args, scratch=()):
+    for at, (got, home) in enumerate(((got_last, grad_in), (got_first, update))):
+        cols = slice((1 - at) * C, (2 - at) * C)
+        total = (
+            back_z[:, cols].astype(F32)
+            + nn(put_mine, got[:, :C])
+            + nn(put_theirs, took[:, cols])
+        ).astype(BF)
+        rows[at] = nn(total, w_out[...]).astype(BF) if at else total
+        send_home(rows.at[at], home)
+    for copy in copies:
+        copy.wait()
+
+
+def call(body, outs, flops, *args, out_space=pltpu.VMEM, scratch=()):
     return pl.pallas_call(
         body,
         out_shape=outs,
         in_specs=[pl.BlockSpec(memory_space=pltpu.VMEM)] * len(args),
-        out_specs=[pl.BlockSpec(memory_space=pltpu.VMEM)] * len(outs),
+        out_specs=[pl.BlockSpec(memory_space=out_space)] * len(outs),
         scratch_shapes=scratch,
         compiler_params=pltpu.CompilerParams(vmem_limit_bytes=40 * 2**20),
         cost_estimate=pl.CostEstimate(flops=flops, bytes_accessed=2**20, transcendentals=2**19),
@@ -297,8 +303,12 @@
     cube = 2 * T * T * C
     pair = shape(T, 2 * C, BF)
     quad = shape(T, 4 * C, BF)
-    mine, give = call(pack_body, [pair, pair], cube * 4, feat, cot)
-    (send,) = call(merge_body, [quad], 2**20, mine, swap(give))
+    (give,) = call(
+        functools.partial(pack_body, x_source, y_source), [pair], cube * 2, feat, cot
+    )
+    took = swap(give)
+    (mine,) = call(functools.partial(pack_body, y_source, x_source), [pair], cube * 2, feat, cot)
+    (send,) = call(merge_body, [quad], 2**20, mine, took)
     got = exchange(send, LONG)
     back_z, grad_z = call(z_body, [pair, shape(C, 4 * C, BF)], cube * 70, feat, cot, *weights)
     *held, keep, give = call(
@@ -331,6 +341,13 @@
         got_last,
         swap(give),
         w_out,
+        out_space=pl.ANY,
+        scratch=[
+            pltpu.VMEM((2, 128, 3 * C), F32),
+            pltpu.VMEM((2, 128, C), F32),
+            pltpu.VMEM((2, T, C), BF),
+            pltpu.SemaphoreType.DMA((6,)),
+        ],
     )
     return (update.reshape(local_shape), grad_in.reshape(local_shape), grad_qkv, grad_out)
 

time: 109 us -> 109 us (level)
    pallas_call x10 -> x11, Pallas kernels: 9.57 us -> 9.73 us  [call(): pl.pallas_call(body, out_shape=outs, in_specs=[pl.BlockSpec(memory_space=...]
where the time goes in v11:
time: 109 us
  blocking collectives  56.8 us (52%)
  starting transfers between devices  26.8 us (25%)
  waiting for transfers between devices  11.6 us (11%)
  Pallas kernels  9.73 us (9%)
  local copies, waits for them, and re-layouts  2.82 us (3%)
    all_to_all x3, blocking collectives, exchange(): lax.all_to_all(rows, AXES, split_axis=0, concat_axis=0, axis_index_groups...  56.8 us
    ppermute x3, starting transfers between devices, swap(): return lax.ppermute(rows, 'row', [(i, i ^ 1) for i in range(8)])  19.2 us
    pallas_call x11, Pallas kernels, call(): pl.pallas_call(body, out_shape=outs, in_specs=[pl.BlockSpec(memory_space=...  9.73 us
    all_to_all x1, waiting for transfers between devices, exchange(): lax.all_to_all(rows, AXES, split_axis=0, concat_axis=0, axis_index_groups...  8.53 us
    all_to_all x1, starting transfers between devices, exchange(): lax.all_to_all(rows, AXES, split_axis=0, concat_axis=0, axis_index_groups...  7.64 us
    ppermute x3, waiting for transfers between devices, swap(): return lax.ppermute(rows, 'row', [(i, i ^ 1) for i in range(8)])  3.12 us
    unnamed x13, local copies, waits for them, and re-layouts  2.82 us
  transfers between devices with their start and end apart: 4, of which 4 were waited for; matrix products, arithmetic and copies ran while one was open for 0% of the time, Pallas kernels for 3%

profile of v11, /device:TPU:1, one launch (start us, length us, event | category | flops | bytes accessed | tf_op | source)
XLA Modules:
  0.0 108.5 jit_solution(17217962080812722649)
XLA Ops:
  0.6 0.0 copy-start.2
  0.6 0.9 copy-done.2
  1.5 0.0 copy-start.4
  1.5 0.9 copy-done.4
  2.4 0.2 shard_map.77
  2.7 8.8 %collective-permute-start = (bf16[256,512]{1,0:T(8,128)(2,1)S(1)}, bf16[256,512]{1,0:T(8,128)(2,1)S(1)}, u32[]{:S(2)}, u32[]{:S(2)}) collective-permute-start(bf16[256,512]{1,0:T(8,128)(2,1)S(1)} %shard_map.77), channel_id=1, source_target_pairs={{0,32},{32,0},{64,96},{96,64},{128,160},{160,128},{192,224},{224,1... | collective-permute-start | bytes 786440 | tf_op jit(solution)/shard_map/ppermute | solution.py:295
  11.5 0.2 shard_map.76.mine
  11.7 0.9 collective-permute-done.took
  12.6 0.8 shard_map.78
  13.4 0.0 copy-start
  13.4 7.6 %all-to-all-start = ((bf16[32,8,1024]{2,1,0:T(8,128)(2,1)}), bf16[32,8,1024]{2,1,0:T(8,128)(2,1)S(1)}, u32[]{:S(2)}, u32[]{:S(2)}) async-start(bf16[32,8,1024]{2,1,0:T(8,128)(2,1)} %bitcast.3), calls=%async_computation | async-start | bytes 1048576 | tf_op jit(solution)/shard_map/all_to_all | solution.py:289
  21.1 0.0 copy-done
  21.1 0.0 copy-start.1
  21.1 0.0 copy-start.3
  21.1 0.0 copy-start.5
  21.1 0.2 copy.8
  21.3 0.7 copy-done.1
  22.0 0.1 copy-done.3
  22.1 0.1 copy-done.5
  22.1 2.2 %shard_map.75 = (bf16[256,512]{1,0:T(8,128)(2,1)S(1)}, bf16[256,1024]{1,0:T(8,128)(2,1)S(1)}) custom-call(bf16[256,256]{1,0:T(8,128)(2,1)S(1)} %bitcast.27, bf16[256,256]{1,0:T(8,128)(2,1)S(1)} %bitcast.30, bf16[256,768]{1,0:T(8,128)(2,1)S(1)} %copy-done, bf16[768,256]{1,0:T(8,128)(2,1)S(1)} %bitcast.21, bf16[256,256]{1,0:T(8,128)(2,1)S(1)} %copy-done.1), custom_call_target="tpu_custom_call" | custom-call | flops 2348810240 | bytes 1048576 | tf_op jit(solution)/shard_map/pallas_call | solution.py:257
  24.4 8.5 %all-to-all-done = bf16[32,8,1024]{2,1,0:T(8,128)(2,1)S(1)} async-done(((bf16[32,8,1024]{2,1,0:T(8,128)(2,1)}), bf16[32,8,1024]{2,1,0:T(8,128)(2,1)S(1)}, u32[]{:S(2)}, u32[]{:S(2)}) %all-to-all-start) | async-done | bytes 524320 | tf_op jit(solution)/shard_map/all_to_all | solution.py:289
  32.9 3.8 %shard_map.79 = (bf16[256,512]{1,0:T(8,128)(2,1)S(1)}, bf16[256,512]{1,0:T(8,128)(2,1)S(1)}, bf16[512,256]{1,0:T(8,128)(2,1)S(1)}, bf16[512,256]{1,0:T(8,128)(2,...) custom-call(bf16[256,1024]{1,0:T(8,128)(2,1)S(1)} %bitcast.19, bf16[256,768]{1,0:T(8,128)(2,1)S(1)} %copy-done, ...), custom_call_target="tpu_custom_call" | custom-call | flops 4697620480 | bytes 1048576 | tf_op jit(solution)/shard_map/pallas_call | solution.py:257
  36.7 8.5 %collective-permute-start.1 = (bf16[128,1024]{1,0:T(8,128)(2,1)S(1)}, bf16[128,1024]{1,0:T(8,128)(2,1)S(1)}, u32[]{:S(2)}, u32[]{:S(2)}) collective-permute-start(bf16[128,1024]{1,0:T(8,128)(2,1)S(1)} %get-tuple-element.26), channel_id=1, source_target_pairs={{0,32},{32,0},{64,96},{96,64},{128,160},{160,128},{192,224},{224,1... | collective-permute-start | bytes 786440 | tf_op jit(solution)/shard_map/ppermute | solution.py:295
  45.2 0.8 shard_map.80
  46.0 0.3 collective-permute-done.1.took
  46.3 0.1 shard_map.81
  46.4 24.3 %all_to_all.44 = bf16[32,8,1024]{2,1,0:T(8,128)(2,1)S(1)} all-to-all(bf16[32,8,1024]{2,1,0:T(8,128)(2,1)S(1)} %bitcast.18), channel_id=1, replica_groups={{0,1,2,3,4,5,6,7,8,9,10,11,12,13,14,15,16,17,18,19,20,21,22,23,24,25,26..., dimensions={0} | all-to-all | bytes 1048576 | tf_op jit(solution)/shard_map/all_to_all | solution.py:289
  70.8 11.0 %all_to_all.45 = bf16[8,8,512]{2,1,0:T(8,128)(2,1)S(1)} all-to-all(bf16[8,8,512]{2,1,0:T(8,128)(2,1)S(1)} %bitcast.24), channel_id=1, replica_groups={{0,256,64,320,128,384,192,448},{1,257,65,321,129,385,193,449},{2,258,66..., dimensions={0} | all-to-all | bytes 131072 | tf_op jit(solution)/shard_map/all_to_all | solution.py:289
  81.8 21.5 %all_to_all.46 = bf16[32,8,1024]{2,1,0:T(8,128)(2,1)S(1)} all-to-all(bf16[32,8,1024]{2,1,0:T(8,128)(2,1)S(1)} %bitcast.20), channel_id=1, replica_groups={{0,1,2,3,4,5,6,7,8,9,10,11,12,13,14,15,16,17,18,19,20,21,22,23,24,25,26..., dimensions={0} | all-to-all | bytes 1048576 | tf_op jit(solution)/shard_map/all_to_all | solution.py:289
  103.3 1.9 %collective-permute-start.2 = (bf16[256,1024]{1,0:T(8,128)(2,1)S(1)}, bf16[256,1024]{1,0:T(8,128)(2,1)S(1)}, u32[]{:S(2)}, u32[]{:S(2)}) collective-permute-start(bf16[256,1024]{1,0:T(8,128)(2,1)S(1)} %shard_map.84), channel_id=1, source_target_pairs={{0,32},{32,0},{64,96},{96,64},{128,160},{160,128},{192,224},{224,1... | collective-permute-start | bytes 1572872 | tf_op jit(solution)/shard_map/ppermute | solution.py:295
  105.2 1.9 %collective-permute-done.2.took = bf16[256,1024]{1,0:T(8,128)(2,1)S(1)} collective-permute-done((bf16[256,1024]{1,0:T(8,128)(2,1)S(1)}, bf16[256,1024]{1,0:T(8,128)(2,1)S(1)}, u32[]{:S(2)}, u32[]{:S(2)}) %collective-permute-start.2) | collective-permute-done | bytes 524320 | tf_op jit(solution)/shard_map/ppermute | solution.py:295
  107.1 1.4 %shard_map.85 = (bf16[256,256]{1,0:T(8,128)(2,1)}, bf16[256,256]{1,0:T(8,128)(2,1)}, f32[256,768]{1,0:T(8,128)}, f32[256,256]{1,0:T(8,128)}) custom-call(bf16[256,512]{1,0:T(8,128)(2,1)S(1)} %get-tuple-element.18.back_z, bf16[256,1024]{1,0:T(8,128)(2,1)S(1)} %bitcast.15, bf16[256,1024]{1,0:T(8,128)(2,1)S(1)} %bitcast.17, ...), custom_call_target="tpu_custom_call" | custom-call | flops 201326592 | bytes 1048576 | tf_op jit(solution)/shard_map/pallas_call | solution.py:257
  (3 shorter events, 0.1 us)
Async XLA Ops:
  0.6 0.9 copy-start.2
  1.5 0.9 copy-start.4
  2.7 9.9 %collective-permute-start = (bf16[256,512]{1,0:T(8,128)(2,1)S(1)}, bf16[256,512]{1,0:T(8,128)(2,1)S(1)}, u32[]{:S(2)}, u32[]{:S(2)}) collective-permute-start(bf16[256,512]{1,0:T(8,128)(2,1)S(1)} %shard_map.77), channel_id=1, source_target_pairs={{0,32},{32,0},{64,96},{96,64},{128,160},{160,128},{192,224},{224,1... | collective-permute-start | bytes 786440 | tf_op jit(solution)/shard_map/ppermute | solution.py:295
  13.4 7.7 %copy-start = (bf16[256,768]{1,0:T(8,128)(2,1)S(1)}, bf16[256,768]{1,0:T(8,128)(2,1)}, u32[]{:S(2)}) copy-start(bf16[256,768]{1,0:T(8,128)(2,1)} %w_qkv.5) | copy-start | bytes 1179652
  13.4 19.4 %all-to-all-start = ((bf16[32,8,1024]{2,1,0:T(8,128)(2,1)}), bf16[32,8,1024]{2,1,0:T(8,128)(2,1)S(1)}, u32[]{:S(2)}, u32[]{:S(2)}) async-start(bf16[32,8,1024]{2,1,0:T(8,128)(2,1)} %bitcast.3), calls=%async_computation | async-start | bytes 1048576 | tf_op jit(solution)/shard_map/all_to_all | solution.py:289
  21.1 0.9 copy-start.1
  21.1 1.0 copy-start.3
  21.1 1.0 copy-start.5
  36.7 9.6 %collective-permute-start.1 = (bf16[128,1024]{1,0:T(8,128)(2,1)S(1)}, bf16[128,1024]{1,0:T(8,128)(2,1)S(1)}, u32[]{:S(2)}, u32[]{:S(2)}) collective-permute-start(bf16[128,1024]{1,0:T(8,128)(2,1)S(1)} %get-tuple-element.26), channel_id=1, source_target_pairs={{0,32},{32,0},{64,96},{96,64},{128,160},{160,128},{192,224},{224,1... | collective-permute-start | bytes 786440 | tf_op jit(solution)/shard_map/ppermute | solution.py:295
  103.3 3.8 %collective-permute-start.2 = (bf16[256,1024]{1,0:T(8,128)(2,1)S(1)}, bf16[256,1024]{1,0:T(8,128)(2,1)S(1)}, u32[]{:S(2)}, u32[]{:S(2)}) collective-permute-start(bf16[256,1024]{1,0:T(8,128)(2,1)S(1)} %shard_map.84), channel_id=1, source_target_pairs={{0,32},{32,0},{64,96},{96,64},{128,160},{160,128},{192,224},{224,1... | collective-permute-start | bytes 1572872 | tf_op jit(solution)/shard_map/ppermute | solution.py:295

commit v12 on v10

--- a/solution.py
+++ b/solution.py
@@ -58,7 +58,7 @@
 def place(t):
     line, at = t >> 6, t & 63
     y_place = ((line >> 2) << 8) + ((at >> 1) << 3) + ((at & 1) << 2) + (line & 3)
-    x_place = (((at >> 3) & 1) << 8) + ((at >> 4) << 6) + (line << 3) + (at & 7)
+    x_place = (((at >> 3) & 1) << 8) + (line << 5) + ((at >> 4) << 3) + (at & 7)
     return by_core(y_place, x_place)
 
 
@@ -74,15 +74,10 @@
     return jnp.where(a == b, 1.0, 0.0).astype(BF)
 
 
-def pack_body(feat, cot, mine, theirs):
-    r = down(T)
-    for out, source in (
-        (theirs, by_core(x_source(r), y_source(r))),
-        (mine, by_core(y_source(r), x_source(r))),
-    ):
-        pick = onehot(source, along(T))
-        out[:, :C] = nn(pick, feat[...]).astype(BF)
-        out[:, C:] = nn(pick, cot[...]).astype(BF)
+def pack_body(first, second, feat, cot, out):
+    pick = onehot(by_core(first(down(T)), second(down(T))), along(T))
+    out[:, :C] = nn(pick, feat[...]).astype(BF)
+    out[:, C:] = nn(pick, cot[...]).astype(BF)
 
 
 def merge_body(mine, took, send):
@@ -271,8 +266,8 @@
 
 
 X, Y, ZS = range(4), range(8), range(8)
-LONG = [[device(x, 0, y, z) for y in Y for z in ZS[dp::2]] for x in X for dp in range(2)] + [
-    [device(x, 1, y, z) for x in X for z in ZS] for y in Y
+LONG = [[device(x, 0, y, z) for z in ZS[dp::2] for y in Y] for x in X for dp in range(2)] + [
+    [device(x, 1, y, z) for z in ZS for x in X] for y in Y
 ]
 SHORT = [
     [device(x, 0, y, 2 * z + dp) for x in X for dp in range(2)] for y in Y for z in range(4)
@@ -297,8 +292,12 @@
     cube = 2 * T * T * C
     pair = shape(T, 2 * C, BF)
     quad = shape(T, 4 * C, BF)
-    mine, give = call(pack_body, [pair, pair], cube * 4, feat, cot)
-    (send,) = call(merge_body, [quad], 2**20, mine, swap(give))
+    (give,) = call(
+        functools.partial(pack_body, x_source, y_source), [pair], cube * 2, feat, cot
+    )
+    took = swap(give)
+    (mine,) = call(functools.partial(pack_body, y_source, x_source), [pair], cube * 2, feat, cot)
+    (send,) = call(merge_body, [quad], 2**20, mine, took)
     got = exchange(send, LONG)
     back_z, grad_z = call(z_body, [pair, shape(C, 4 * C, BF)], cube * 70, feat, cot, *weights)
     *held, keep, give = call(

time: 109 us -> 110 us (level)
  waiting for transfers between devices: 11.9 us -> 15.2 us
  starting transfers between devices: 26.8 us -> 23.6 us
    all_to_all x1, waiting for transfers between devices: 8.54 us -> 12.1 us  [exchange(): lax.all_to_all(rows, AXES, split_axis=0, concat_axis=0, axis_index_groups...]
    ppermute x3, starting transfers between devices: 19.2 us -> 15.9 us  [swap(): return lax.ppermute(rows, 'row', [(i, i ^ 1) for i in range(8)])]
    pallas_call x10 -> x11, Pallas kernels: 9.57 us -> 9.73 us  [call(): pl.pallas_call(body, out_shape=outs, in_specs=[pl.BlockSpec(memory_space=...]
where the time goes in v12:
time: 110 us; the launch traced here: 109 us
  blocking collectives  57.4 us (52%)
  starting transfers between devices  23.6 us (21%)
  waiting for transfers between devices  15.2 us (14%)
  Pallas kernels  9.73 us (9%)
  local copies, waits for them, and re-layouts  2.82 us (3%)
    all_to_all x3, blocking collectives, exchange(): lax.all_to_all(rows, AXES, split_axis=0, concat_axis=0, axis_index_groups...  57.4 us
    ppermute x3, starting transfers between devices, swap(): return lax.ppermute(rows, 'row', [(i, i ^ 1) for i in range(8)])  15.9 us
    all_to_all x1, waiting for transfers between devices, exchange(): lax.all_to_all(rows, AXES, split_axis=0, concat_axis=0, axis_index_groups...  12.1 us
    pallas_call x11, Pallas kernels, call(): pl.pallas_call(body, out_shape=outs, in_specs=[pl.BlockSpec(memory_space=...  9.73 us
    all_to_all x1, starting transfers between devices, exchange(): lax.all_to_all(rows, AXES, split_axis=0, concat_axis=0, axis_index_groups...  7.64 us
    ppermute x3, waiting for transfers between devices, swap(): return lax.ppermute(rows, 'row', [(i, i ^ 1) for i in range(8)])  3.12 us
    unnamed x13, local copies, waits for them, and re-layouts  2.82 us
  transfers between devices with their start and end apart: 4, of which 4 were waited for; matrix products, arithmetic and copies ran while one was open for 0% of the time, Pallas kernels for 3%

profile of v12, /device:TPU:1, one launch (start us, length us, event | category | flops | bytes accessed | tf_op | source)
XLA Modules:
  0.0 109.4 jit_solution(1158071596022830823)
XLA Ops:
  0.6 0.0 copy-start.2
  0.6 0.9 copy-done.2
  1.5 0.0 copy-start.4
  1.5 0.9 copy-done.4
  2.4 0.2 shard_map.77
  2.7 8.8 %collective-permute-start = (bf16[256,512]{1,0:T(8,128)(2,1)S(1)}, bf16[256,512]{1,0:T(8,128)(2,1)S(1)}, u32[]{:S(2)}, u32[]{:S(2)}) collective-permute-start(bf16[256,512]{1,0:T(8,128)(2,1)S(1)} %shard_map.77), channel_id=1, source_target_pairs={{0,32},{32,0},{64,96},{96,64},{128,160},{160,128},{192,224},{224,1... | collective-permute-start | bytes 786440 | tf_op jit(solution)/shard_map/ppermute | solution.py:284
  11.5 0.2 shard_map.76.mine
  11.7 0.9 collective-permute-done.took
  12.6 0.8 shard_map.78
  13.4 0.0 copy-start
  13.4 7.6 %all-to-all-start = ((bf16[32,8,1024]{2,1,0:T(8,128)(2,1)}), bf16[32,8,1024]{2,1,0:T(8,128)(2,1)S(1)}, u32[]{:S(2)}, u32[]{:S(2)}) async-start(bf16[32,8,1024]{2,1,0:T(8,128)(2,1)} %bitcast.3), calls=%async_computation | async-start | bytes 1048576 | tf_op jit(solution)/shard_map/all_to_all | solution.py:278
  21.1 0.0 copy-done
  21.1 0.0 copy-start.1
  21.1 0.0 copy-start.3
  21.1 0.0 copy-start.5
  21.1 0.2 copy.8
  21.3 0.7 copy-done.1
  22.0 0.1 copy-done.3
  22.1 0.1 copy-done.5
  22.1 2.2 %shard_map.75 = (bf16[256,512]{1,0:T(8,128)(2,1)S(1)}, bf16[256,1024]{1,0:T(8,128)(2,1)S(1)}) custom-call(bf16[256,256]{1,0:T(8,128)(2,1)S(1)} %bitcast.27, bf16[256,256]{1,0:T(8,128)(2,1)S(1)} %bitcast.30, bf16[256,768]{1,0:T(8,128)(2,1)S(1)} %copy-done, bf16[768,256]{1,0:T(8,128)(2,1)S(1)} %bitcast.21, bf16[256,256]{1,0:T(8,128)(2,1)S(1)} %copy-done.1), custom_call_target="tpu_custom_call" | custom-call | flops 2348810240 | bytes 1048576 | tf_op jit(solution)/shard_map/pallas_call | solution.py:246
  24.4 12.1 %all-to-all-done = bf16[32,8,1024]{2,1,0:T(8,128)(2,1)S(1)} async-done(((bf16[32,8,1024]{2,1,0:T(8,128)(2,1)}), bf16[32,8,1024]{2,1,0:T(8,128)(2,1)S(1)}, u32[]{:S(2)}, u32[]{:S(2)}) %all-to-all-start) | async-done | bytes 524320 | tf_op jit(solution)/shard_map/all_to_all | solution.py:278
  36.4 3.8 %shard_map.79 = (bf16[256,512]{1,0:T(8,128)(2,1)S(1)}, bf16[256,512]{1,0:T(8,128)(2,1)S(1)}, bf16[512,256]{1,0:T(8,128)(2,1)S(1)}, bf16[512,256]{1,0:T(8,128)(2,...) custom-call(bf16[256,1024]{1,0:T(8,128)(2,1)S(1)} %bitcast.19, bf16[256,768]{1,0:T(8,128)(2,1)S(1)} %copy-done, ...), custom_call_target="tpu_custom_call" | custom-call | flops 4697620480 | bytes 1048576 | tf_op jit(solution)/shard_map/pallas_call | solution.py:246
  40.3 5.2 %collective-permute-start.1 = (bf16[128,1024]{1,0:T(8,128)(2,1)S(1)}, bf16[128,1024]{1,0:T(8,128)(2,1)S(1)}, u32[]{:S(2)}, u32[]{:S(2)}) collective-permute-start(bf16[128,1024]{1,0:T(8,128)(2,1)S(1)} %get-tuple-element.26), channel_id=1, source_target_pairs={{0,32},{32,0},{64,96},{96,64},{128,160},{160,128},{192,224},{224,1... | collective-permute-start | bytes 786440 | tf_op jit(solution)/shard_map/ppermute | solution.py:284
  45.5 0.8 shard_map.80
  46.3 0.3 collective-permute-done.1.took
  46.6 0.1 shard_map.81
  46.7 23.7 %all_to_all.44 = bf16[32,8,1024]{2,1,0:T(8,128)(2,1)S(1)} all-to-all(bf16[32,8,1024]{2,1,0:T(8,128)(2,1)S(1)} %bitcast.18), channel_id=1, replica_groups={{0,4,8,12,16,20,24,28,1,5,9,13,17,21,25,29,2,6,10,14,18,22,26,30,3,7,11..., dimensions={0} | all-to-all | bytes 1048576 | tf_op jit(solution)/shard_map/all_to_all | solution.py:278
  70.4 12.2 %all_to_all.45 = bf16[8,8,512]{2,1,0:T(8,128)(2,1)S(1)} all-to-all(bf16[8,8,512]{2,1,0:T(8,128)(2,1)S(1)} %bitcast.24), channel_id=1, replica_groups={{0,256,64,320,128,384,192,448},{1,257,65,321,129,385,193,449},{2,258,66..., dimensions={0} | all-to-all | bytes 131072 | tf_op jit(solution)/shard_map/all_to_all | solution.py:278
  82.7 21.5 %all_to_all.46 = bf16[32,8,1024]{2,1,0:T(8,128)(2,1)S(1)} all-to-all(bf16[32,8,1024]{2,1,0:T(8,128)(2,1)S(1)} %bitcast.20), channel_id=1, replica_groups={{0,4,8,12,16,20,24,28,1,5,9,13,17,21,25,29,2,6,10,14,18,22,26,30,3,7,11..., dimensions={0} | all-to-all | bytes 1048576 | tf_op jit(solution)/shard_map/all_to_all | solution.py:278
  104.2 1.9 %collective-permute-start.2 = (bf16[256,1024]{1,0:T(8,128)(2,1)S(1)}, bf16[256,1024]{1,0:T(8,128)(2,1)S(1)}, u32[]{:S(2)}, u32[]{:S(2)}) collective-permute-start(bf16[256,1024]{1,0:T(8,128)(2,1)S(1)} %shard_map.84), channel_id=1, source_target_pairs={{0,32},{32,0},{64,96},{96,64},{128,160},{160,128},{192,224},{224,1... | collective-permute-start | bytes 1572872 | tf_op jit(solution)/shard_map/ppermute | solution.py:284
  106.1 1.9 %collective-permute-done.2.took = bf16[256,1024]{1,0:T(8,128)(2,1)S(1)} collective-permute-done((bf16[256,1024]{1,0:T(8,128)(2,1)S(1)}, bf16[256,1024]{1,0:T(8,128)(2,1)S(1)}, u32[]{:S(2)}, u32[]{:S(2)}) %collective-permute-start.2) | collective-permute-done | bytes 524320 | tf_op jit(solution)/shard_map/ppermute | solution.py:284
  108.0 1.4 %shard_map.85 = (bf16[256,256]{1,0:T(8,128)(2,1)}, bf16[256,256]{1,0:T(8,128)(2,1)}, f32[256,768]{1,0:T(8,128)}, f32[256,256]{1,0:T(8,128)}) custom-call(bf16[256,512]{1,0:T(8,128)(2,1)S(1)} %get-tuple-element.18.back_z, bf16[256,1024]{1,0:T(8,128)(2,1)S(1)} %bitcast.15, bf16[256,1024]{1,0:T(8,128)(2,1)S(1)} %bitcast.17, ...), custom_call_target="tpu_custom_call" | custom-call | flops 201326592 | bytes 1048576 | tf_op jit(solution)/shard_map/pallas_call | solution.py:246
  (3 shorter events, 0.1 us)
Async XLA Ops:
  0.6 0.9 copy-start.2
  1.5 0.9 copy-start.4
  2.7 9.9 %collective-permute-start = (bf16[256,512]{1,0:T(8,128)(2,1)S(1)}, bf16[256,512]{1,0:T(8,128)(2,1)S(1)}, u32[]{:S(2)}, u32[]{:S(2)}) collective-permute-start(bf16[256,512]{1,0:T(8,128)(2,1)S(1)} %shard_map.77), channel_id=1, source_target_pairs={{0,32},{32,0},{64,96},{96,64},{128,160},{160,128},{192,224},{224,1... | collective-permute-start | bytes 786440 | tf_op jit(solution)/shard_map/ppermute | solution.py:284
  13.4 7.7 %copy-start = (bf16[256,768]{1,0:T(8,128)(2,1)S(1)}, bf16[256,768]{1,0:T(8,128)(2,1)}, u32[]{:S(2)}) copy-start(bf16[256,768]{1,0:T(8,128)(2,1)} %w_qkv.5) | copy-start | bytes 1179652
  13.4 23.0 %all-to-all-start = ((bf16[32,8,1024]{2,1,0:T(8,128)(2,1)}), bf16[32,8,1024]{2,1,0:T(8,128)(2,1)S(1)}, u32[]{:S(2)}, u32[]{:S(2)}) async-start(bf16[32,8,1024]{2,1,0:T(8,128)(2,1)} %bitcast.3), calls=%async_computation | async-start | bytes 1048576 | tf_op jit(solution)/shard_map/all_to_all | solution.py:278
  21.1 0.9 copy-start.1
  21.1 1.0 copy-start.3
  21.1 1.0 copy-start.5
  40.3 6.4 %collective-permute-start.1 = (bf16[128,1024]{1,0:T(8,128)(2,1)S(1)}, bf16[128,1024]{1,0:T(8,128)(2,1)S(1)}, u32[]{:S(2)}, u32[]{:S(2)}) collective-permute-start(bf16[128,1024]{1,0:T(8,128)(2,1)S(1)} %get-tuple-element.26), channel_id=1, source_target_pairs={{0,32},{32,0},{64,96},{96,64},{128,160},{160,128},{192,224},{224,1... | collective-permute-start | bytes 786440 | tf_op jit(solution)/shard_map/ppermute | solution.py:284
  104.2 3.8 %collective-permute-start.2 = (bf16[256,1024]{1,0:T(8,128)(2,1)S(1)}, bf16[256,1024]{1,0:T(8,128)(2,1)S(1)}, u32[]{:S(2)}, u32[]{:S(2)}) collective-permute-start(bf16[256,1024]{1,0:T(8,128)(2,1)S(1)} %shard_map.84), channel_id=1, source_target_pairs={{0,32},{32,0},{64,96},{96,64},{128,160},{160,128},{192,224},{224,1... | collective-permute-start | bytes 1572872 | tf_op jit(solution)/shard_map/ppermute | solution.py:284

commit v13 on v12

--- a/solution.py
+++ b/solution.py
@@ -58,7 +58,7 @@
 def place(t):
     line, at = t >> 6, t & 63
     y_place = ((line >> 2) << 8) + ((at >> 1) << 3) + ((at & 1) << 2) + (line & 3)
-    x_place = (((at >> 3) & 1) << 8) + (line << 5) + ((at >> 4) << 3) + (at & 7)
+    x_place = (((at >> 3) & 1) << 8) + ((at >> 4) << 6) + (line << 3) + (at & 7)
     return by_core(y_place, x_place)
 
 
@@ -156,8 +156,11 @@
 
     out_t, dq_t = whole(0, True), whole(1, True)
     dk, dv = whole(2, False), whole(3, False)
-    grads = (nt(feat_t, dq_t), nn(feat_t, dk), nn(feat_t, dv), nn(out_t, cot))
-    return (out_t, dq_t, dk, dv), grads
+    return out_t, dq_t, dk, dv, feat_t
+
+
+def gradients(feat_t, out_t, dq_t, dk, dv, cot):
+    return nt(feat_t, dq_t), nn(feat_t, dk), nn(feat_t, dv), nn(out_t, cot)
 
 
 def results(out_t, dq_t, dk, dv, w_qkv):
@@ -166,35 +169,41 @@
 
 
 def z_body(feat, cot, w_qkv, w_qkv_t, w_out, back, grad):
-    parts, terms = axis_math(z_line, feat[...], cot[...], w_qkv, w_qkv_t, w_out)
+    *parts, feat_t = axis_math(z_line, feat[...], cot[...], w_qkv, w_qkv_t, w_out)
     eye = onehot(down(T), along(T))
     for at, part_t in enumerate(results(*parts, w_qkv)):
         back[:, at * C : (at + 1) * C] = nt(eye, part_t).astype(BF)
+    for at, term in enumerate(gradients(feat_t, *parts, cot[...])):
+        grad[:, at * C : (at + 1) * C] = term.astype(BF)
+
+
+def half_gradient(half, grad_z, feat_t, out_t, dq_t, dk, dv, cot, grad):
+    rows = pl.ds(pl.multiple_of(half * 128, 128), 128)
+    terms = gradients(feat_t[rows, :], out_t[rows, :], dq_t[...], dk[...], dv[...], cot[...])
     for at, term in enumerate(terms):
-        grad[:, at * C : (at + 1) * C] = term.astype(BF)
-
-
-def lines_body(got, w_qkv, w_qkv_t, w_out, grad_z, out_t, dq_t, dk, dv, keep, give, total):
+        cols = slice(at * C, (at + 1) * C)
+        grad[:, cols] = (grad_z[rows, cols].astype(F32) + term).astype(grad.dtype)
+
+
+def lines_body(
+    got, w_qkv, w_qkv_t, w_out, grad_z, feat_t, out_t, dq_t, dk, dv, cot, give
+):
     sort = onehot(place(down(2 * T)), along(2 * T))
     feat = nn(sort, jnp.concatenate([got[:, :C], got[:, 2 * C : 3 * C]], axis=0)).astype(BF)
-    cot = nn(sort, jnp.concatenate([got[:, C : 2 * C], got[:, 3 * C :]], axis=0)).astype(BF)
-    held, terms = axis_math(long_line, feat, cot, w_qkv, w_qkv_t, w_out)
-    for ref, value in zip((out_t, dq_t, dk, dv), held):
+    cot[...] = nn(sort, jnp.concatenate([got[:, C : 2 * C], got[:, 3 * C :]], axis=0)).astype(BF)
+    held = axis_math(long_line, feat, cot[...], w_qkv, w_qkv_t, w_out)
+    for ref, value in zip((out_t, dq_t, dk, dv, feat_t), held):
         ref[...] = value
-    for at, term in enumerate(terms):
-        cols = slice(at * C, (at + 1) * C)
-        total[:, cols] = grad_z[:, cols].astype(F32) + term
-    mine = core()
-    keep[...] = total[pl.ds(pl.multiple_of(mine * 128, 128), 128)]
-    give[...] = total[pl.ds(pl.multiple_of((1 - mine) * 128, 128), 128)].astype(BF)
-
-
-def back_body(out_t, dq_t, dk, dv, w_qkv, back_out, back_feat):
+    half_gradient(1 - core(), grad_z, feat_t, out_t, dq_t, dk, dv, cot, give)
+
+
+def back_body(grad_z, feat_t, out_t, dq_t, dk, dv, cot, w_qkv, back_out, back_feat, keep):
     unsort = onehot(down(2 * T), place(along(2 * T)))
     parts = results(out_t[...], dq_t[...], dk[...], dv[...], w_qkv)
     for part_t, back in zip(parts, (back_out, back_feat)):
         rows = nt(unsort, part_t).astype(BF)
         back[:, :C], back[:, C:] = rows[:T], rows[T:]
+    half_gradient(core(), grad_z, feat_t, out_t, dq_t, dk, dv, cot, keep)
 
 
 def first_pack_body(back_out, keep, took, send):
@@ -266,8 +275,8 @@
 
 
 X, Y, ZS = range(4), range(8), range(8)
-LONG = [[device(x, 0, y, z) for z in ZS[dp::2] for y in Y] for x in X for dp in range(2)] + [
-    [device(x, 1, y, z) for z in ZS for x in X] for y in Y
+LONG = [[device(x, 0, y, z) for y in Y for z in ZS[dp::2]] for x in X for dp in range(2)] + [
+    [device(x, 1, y, z) for x in X for z in ZS] for y in Y
 ]
 SHORT = [
     [device(x, 0, y, 2 * z + dp) for x in X for dp in range(2)] for y in Y for z in range(4)
@@ -300,19 +309,18 @@
     (send,) = call(merge_body, [quad], 2**20, mine, took)
     got = exchange(send, LONG)
     back_z, grad_z = call(z_body, [pair, shape(C, 4 * C, BF)], cube * 70, feat, cot, *weights)
-    *held, keep, give = call(
+    *held, give = call(
         lines_body,
-        [shape(C, 2 * T, BF)] * 2
-        + [shape(2 * T, C, BF)] * 2
-        + [shape(128, 4 * C, F32), shape(128, 4 * C, BF)],
+        [shape(C, 2 * T, BF)] * 3 + [shape(2 * T, C, BF)] * 3 + [shape(128, 4 * C, BF)],
         cube * 140,
         got,
         *weights,
         grad_z,
-        scratch=[pltpu.VMEM((C, 4 * C), F32)],
     )
     took = swap(give)
-    back_out, back_feat = call(back_body, [pair] * 2, cube * 20, *held, w_qkv)
+    back_out, back_feat, keep = call(
+        back_body, [pair, pair, shape(128, 4 * C, F32)], cube * 20, grad_z, *held, w_qkv
+    )
     (send,) = call(first_pack_body, [quad], 2**20, back_out, keep, took)
     got_first = exchange(send, LONG)
     (send,) = call(block_body, [shape(64, 2 * C, BF)], 2**20, got_first)

time: 110 us -> 109 us (level)
  waiting for transfers between devices: 15.2 us -> 11.5 us
  starting transfers between devices: 23.6 us -> 26.8 us
    all_to_all x1, waiting for transfers between devices: 12.1 us -> 8.54 us  [exchange(): lax.all_to_all(rows, AXES, split_axis=0, concat_axis=0, axis_index_groups...]
    ppermute x3, starting transfers between devices: 15.9 us -> 19.2 us  [swap(): return lax.ppermute(rows, 'row', [(i, i ^ 1) for i in range(8)])]
where the time goes in v13:
time: 109 us; the launch traced here: 108 us
  blocking collectives  56.8 us (52%)
  starting transfers between devices  26.8 us (25%)
  waiting for transfers between devices  11.5 us (11%)
  Pallas kernels  9.86 us (9%)
  local copies, waits for them, and re-layouts  2.82 us (3%)
    all_to_all x3, blocking collectives, exchange(): lax.all_to_all(rows, AXES, split_axis=0, concat_axis=0, axis_index_groups...  56.8 us
    ppermute x3, starting transfers between devices, swap(): return lax.ppermute(rows, 'row', [(i, i ^ 1) for i in range(8)])  19.2 us
    pallas_call x11, Pallas kernels, call(): pl.pallas_call(body, out_shape=outs, in_specs=[pl.BlockSpec(memory_space=...  9.86 us
    all_to_all x1, waiting for transfers between devices, exchange(): lax.all_to_all(rows, AXES, split_axis=0, concat_axis=0, axis_index_groups...  8.54 us
    all_to_all x1, starting transfers between devices, exchange(): lax.all_to_all(rows, AXES, split_axis=0, concat_axis=0, axis_index_groups...  7.64 us
    ppermute x3, waiting for transfers between devices, swap(): return lax.ppermute(rows, 'row', [(i, i ^ 1) for i in range(8)])  2.96 us
    unnamed x13, local copies, waits for them, and re-layouts  2.82 us
  transfers between devices with their start and end apart: 4, of which 4 were waited for; matrix products, arithmetic and copies ran while one was open for 0% of the time, Pallas kernels for 3%

profile of v13, /device:TPU:1, one launch (start us, length us, event | category | flops | bytes accessed | tf_op | source)
XLA Modules:
  0.0 108.5 jit_solution(12163055846529448024)
XLA Ops:
  0.6 0.0 copy-start.2
  0.6 0.9 copy-done.2
  1.5 0.0 copy-start.4
  1.5 0.9 copy-done.4
  2.4 0.2 shard_map.77
  2.7 8.8 %collective-permute-start = (bf16[256,512]{1,0:T(8,128)(2,1)S(1)}, bf16[256,512]{1,0:T(8,128)(2,1)S(1)}, u32[]{:S(2)}, u32[]{:S(2)}) collective-permute-start(bf16[256,512]{1,0:T(8,128)(2,1)S(1)} %shard_map.77), channel_id=1, source_target_pairs={{0,32},{32,0},{64,96},{96,64},{128,160},{160,128},{192,224},{224,1... | collective-permute-start | bytes 786440 | tf_op jit(solution)/shard_map/ppermute | solution.py:293
  11.5 0.2 shard_map.76.mine
  11.7 0.9 collective-permute-done.took
  12.6 0.8 shard_map.78
  13.4 0.0 copy-start
  13.4 7.6 %all-to-all-start = ((bf16[32,8,1024]{2,1,0:T(8,128)(2,1)}), bf16[32,8,1024]{2,1,0:T(8,128)(2,1)S(1)}, u32[]{:S(2)}, u32[]{:S(2)}) async-start(bf16[32,8,1024]{2,1,0:T(8,128)(2,1)} %bitcast.3), calls=%async_computation | async-start | bytes 1048576 | tf_op jit(solution)/shard_map/all_to_all | solution.py:287
  21.1 0.0 copy-done
  21.1 0.0 copy-start.1
  21.1 0.0 copy-start.3
  21.1 0.0 copy-start.5
  21.1 0.2 copy.8
  21.3 0.7 copy-done.1
  22.0 0.1 copy-done.3
  22.1 0.1 copy-done.5
  22.1 2.2 %shard_map.75 = (bf16[256,512]{1,0:T(8,128)(2,1)S(1)}, bf16[256,1024]{1,0:T(8,128)(2,1)S(1)}) custom-call(bf16[256,256]{1,0:T(8,128)(2,1)S(1)} %bitcast.27, bf16[256,256]{1,0:T(8,128)(2,1)S(1)} %bitcast.30, bf16[256,768]{1,0:T(8,128)(2,1)S(1)} %copy-done, bf16[768,256]{1,0:T(8,128)(2,1)S(1)} %bitcast.21, bf16[256,256]{1,0:T(8,128)(2,1)S(1)} %copy-done.1), custom_call_target="tpu_custom_call" | custom-call | flops 2348810240 | bytes 1048576 | tf_op jit(solution)/shard_map/pallas_call | solution.py:255
  24.3 8.5 %all-to-all-done = bf16[32,8,1024]{2,1,0:T(8,128)(2,1)S(1)} async-done(((bf16[32,8,1024]{2,1,0:T(8,128)(2,1)}), bf16[32,8,1024]{2,1,0:T(8,128)(2,1)S(1)}, u32[]{:S(2)}, u32[]{:S(2)}) %all-to-all-start) | async-done | bytes 524320 | tf_op jit(solution)/shard_map/all_to_all | solution.py:287
  32.9 3.8 %shard_map.79 = (bf16[256,512]{1,0:T(8,128)(2,1)S(1)}, bf16[256,512]{1,0:T(8,128)(2,1)S(1)}, bf16[256,512]{1,0:T(8,128)(2,1)S(1)}, bf16[512,256]{1,0:T(8,128)(2,...) custom-call(bf16[256,1024]{1,0:T(8,128)(2,1)S(1)} %bitcast.19, ...), custom_call_target="tpu_custom_call" | custom-call | flops 4697620480 | bytes 1048576 | tf_op jit(solution)/shard_map/pallas_call | solution.py:255
  36.7 8.5 %collective-permute-start.1 = (bf16[128,1024]{1,0:T(8,128)(2,1)S(1)}, bf16[128,1024]{1,0:T(8,128)(2,1)S(1)}, u32[]{:S(2)}, u32[]{:S(2)}) collective-permute-start(bf16[128,1024]{1,0:T(8,128)(2,1)S(1)} %get-tuple-element.30), channel_id=1, source_target_pairs={{0,32},{32,0},{64,96},{96,64},{128,160},{160,128},{192,224},{224,1... | collective-permute-start | bytes 786440 | tf_op jit(solution)/shard_map/ppermute | solution.py:293
  45.2 1.0 shard_map.80
  46.1 0.2 collective-permute-done.1.took
  46.3 0.1 shard_map.81
  46.4 24.3 %all_to_all.44 = bf16[32,8,1024]{2,1,0:T(8,128)(2,1)S(1)} all-to-all(bf16[32,8,1024]{2,1,0:T(8,128)(2,1)S(1)} %bitcast.18), channel_id=1, replica_groups={{0,1,2,3,4,5,6,7,8,9,10,11,12,13,14,15,16,17,18,19,20,21,22,23,24,25,26..., dimensions={0} | all-to-all | bytes 1048576 | tf_op jit(solution)/shard_map/all_to_all | solution.py:287
  70.7 10.9 %all_to_all.45 = bf16[8,8,512]{2,1,0:T(8,128)(2,1)S(1)} all-to-all(bf16[8,8,512]{2,1,0:T(8,128)(2,1)S(1)} %bitcast.24), channel_id=1, replica_groups={{0,256,64,320,128,384,192,448},{1,257,65,321,129,385,193,449},{2,258,66..., dimensions={0} | all-to-all | bytes 131072 | tf_op jit(solution)/shard_map/all_to_all | solution.py:287
  81.7 21.5 %all_to_all.46 = bf16[32,8,1024]{2,1,0:T(8,128)(2,1)S(1)} all-to-all(bf16[32,8,1024]{2,1,0:T(8,128)(2,1)S(1)} %bitcast.20), channel_id=1, replica_groups={{0,1,2,3,4,5,6,7,8,9,10,11,12,13,14,15,16,17,18,19,20,21,22,23,24,25,26..., dimensions={0} | all-to-all | bytes 1048576 | tf_op jit(solution)/shard_map/all_to_all | solution.py:287
  103.3 1.9 %collective-permute-start.2 = (bf16[256,1024]{1,0:T(8,128)(2,1)S(1)}, bf16[256,1024]{1,0:T(8,128)(2,1)S(1)}, u32[]{:S(2)}, u32[]{:S(2)}) collective-permute-start(bf16[256,1024]{1,0:T(8,128)(2,1)S(1)} %shard_map.84), channel_id=1, source_target_pairs={{0,32},{32,0},{64,96},{96,64},{128,160},{160,128},{192,224},{224,1... | collective-permute-start | bytes 1572872 | tf_op jit(solution)/shard_map/ppermute | solution.py:293
  105.2 1.9 %collective-permute-done.2.took = bf16[256,1024]{1,0:T(8,128)(2,1)S(1)} collective-permute-done((bf16[256,1024]{1,0:T(8,128)(2,1)S(1)}, bf16[256,1024]{1,0:T(8,128)(2,1)S(1)}, u32[]{:S(2)}, u32[]{:S(2)}) %collective-permute-start.2) | collective-permute-done | bytes 524320 | tf_op jit(solution)/shard_map/ppermute | solution.py:293
  107.1 1.4 %shard_map.85 = (bf16[256,256]{1,0:T(8,128)(2,1)}, bf16[256,256]{1,0:T(8,128)(2,1)}, f32[256,768]{1,0:T(8,128)}, f32[256,256]{1,0:T(8,128)}) custom-call(bf16[256,512]{1,0:T(8,128)(2,1)S(1)} %get-tuple-element.20.back_z, bf16[256,1024]{1,0:T(8,128)(2,1)S(1)} %bitcast.15, bf16[256,1024]{1,0:T(8,128)(2,1)S(1)} %bitcast.17, ...), custom_call_target="tpu_custom_call" | custom-call | flops 201326592 | bytes 1048576 | tf_op jit(solution)/shard_map/pallas_call | solution.py:255
  (3 shorter events, 0.1 us)
Async XLA Ops:
  0.6 0.9 copy-start.2
  1.5 0.9 copy-start.4
  2.7 9.9 %collective-permute-start = (bf16[256,512]{1,0:T(8,128)(2,1)S(1)}, bf16[256,512]{1,0:T(8,128)(2,1)S(1)}, u32[]{:S(2)}, u32[]{:S(2)}) collective-permute-start(bf16[256,512]{1,0:T(8,128)(2,1)S(1)} %shard_map.77), channel_id=1, source_target_pairs={{0,32},{32,0},{64,96},{96,64},{128,160},{160,128},{192,224},{224,1... | collective-permute-start | bytes 786440 | tf_op jit(solution)/shard_map/ppermute | solution.py:293
  13.4 7.7 %copy-start = (bf16[256,768]{1,0:T(8,128)(2,1)S(1)}, bf16[256,768]{1,0:T(8,128)(2,1)}, u32[]{:S(2)}) copy-start(bf16[256,768]{1,0:T(8,128)(2,1)} %w_qkv.5) | copy-start | bytes 1179652
  13.4 19.4 %all-to-all-start = ((bf16[32,8,1024]{2,1,0:T(8,128)(2,1)}), bf16[32,8,1024]{2,1,0:T(8,128)(2,1)S(1)}, u32[]{:S(2)}, u32[]{:S(2)}) async-start(bf16[32,8,1024]{2,1,0:T(8,128)(2,1)} %bitcast.3), calls=%async_computation | async-start | bytes 1048576 | tf_op jit(solution)/shard_map/all_to_all | solution.py:287
  21.1 0.9 copy-start.1
  21.1 1.0 copy-start.3
  21.1 1.0 copy-start.5
  36.7 9.6 %collective-permute-start.1 = (bf16[128,1024]{1,0:T(8,128)(2,1)S(1)}, bf16[128,1024]{1,0:T(8,128)(2,1)S(1)}, u32[]{:S(2)}, u32[]{:S(2)}) collective-permute-start(bf16[128,1024]{1,0:T(8,128)(2,1)S(1)} %get-tuple-element.30), channel_id=1, source_target_pairs={{0,32},{32,0},{64,96},{96,64},{128,160},{160,128},{192,224},{224,1... | collective-permute-start | bytes 786440 | tf_op jit(solution)/shard_map/ppermute | solution.py:293
  103.3 3.8 %collective-permute-start.2 = (bf16[256,1024]{1,0:T(8,128)(2,1)S(1)}, bf16[256,1024]{1,0:T(8,128)(2,1)S(1)}, u32[]{:S(2)}, u32[]{:S(2)}) collective-permute-start(bf16[256,1024]{1,0:T(8,128)(2,1)S(1)} %shard_map.84), channel_id=1, source_target_pairs={{0,32},{32,0},{64,96},{96,64},{128,160},{160,128},{192,224},{224,1... | collective-permute-start | bytes 1572872 | tf_op jit(solution)/shard_map/ppermute | solution.py:293

commit v14 on v12

--- a/solution.py
+++ b/solution.py
@@ -58,7 +58,7 @@
 def place(t):
     line, at = t >> 6, t & 63
     y_place = ((line >> 2) << 8) + ((at >> 1) << 3) + ((at & 1) << 2) + (line & 3)
-    x_place = (((at >> 3) & 1) << 8) + (line << 5) + ((at >> 4) << 3) + (at & 7)
+    x_place = (((at >> 3) & 1) << 8) + ((at >> 4) << 6) + (line << 3) + (at & 7)
     return by_core(y_place, x_place)
 
 
@@ -85,13 +85,13 @@
     send[:, 2 * C :] = took[...]
 
 
-def axis_math(line, feat, cot, w_qkv, w_qkv_t, w_out):
+def axis_math(line, feat, cot, w_qkv, w_out):
     scale = 1.0 / math.sqrt(DEPTH)
-    feat_t = nt(onehot(down(T), along(T)), feat).astype(BF)
+    feat_t = feat.T
     proj = nn(feat, w_qkv[...]).astype(BF)
-    proj_t = nt(w_qkv_t[...], feat).astype(BF)
+    proj_t = proj.T
     gmix = nt(cot, w_out[...]).astype(BF)
-    gmix_t = nt(w_out[...], cot).astype(BF)
+    gmix_t = gmix.T
     q, k, v = proj[:, :C], proj[:, C : 2 * C], proj[:, 2 * C :]
     q_t, k_t, v_t = proj_t[:C], proj_t[C : 2 * C], proj_t[2 * C :]
     bias = jnp.where(line(down(HALF)) == line(along(QUAD * HALF) & (HALF - 1)), 0.0, NEG)
@@ -131,22 +131,35 @@
         for half in range(halves)
         for quad in range(2)
     ]
-    all_scores = [nn(k[t, c], spread(q_t[c, t])) + bias for t, c in blocks]
-    all_dprobs = [nn(v[t, c], spread(gmix_t[c, t])) for t, c in blocks]
-    soft = []
-    for scores, dprobs in zip(all_scores, all_dprobs):
+    def softmax(scores, dprobs):
         top = jnp.max(scores, axis=0, keepdims=True)
         e = jnp.exp((scores - top) * scale)
         probs = e * (1.0 / jnp.sum(e, axis=0, keepdims=True))
         mean = jnp.sum(dprobs * probs, axis=0, keepdims=True)
-        soft.append((probs.astype(BF), (probs * (dprobs - mean) * scale).astype(BF)))
-    parts = []
-    for (t, c), (rounded, dround) in zip(blocks, soft):
+        return probs.astype(BF), (probs * (dprobs - mean) * scale).astype(BF)
+
+    def score(block):
+        t, c = block
+        scores = nn(k[t, c], spread(q_t[c, t])) + bias
+        return scores, nn(v[t, c], spread(gmix_t[c, t]))
+
+    def products(block, rounded, dround):
+        t, c = block
         out_t = per_head(v_t[c, t], rounded)
         dv = nn(rounded, stack(gmix[t, c]))
         dq_t = per_head(k_t[c, t], dround)
         dk = nn(dround, stack(q[t, c]))
-        parts.append([m.astype(BF) for m in (out_t, dq_t, dk, dv)])
+        return [m.astype(BF) for m in (out_t, dq_t, dk, dv)]
+
+    parts = []
+    scored, soft = [score(blocks[0])], []
+    for at in range(len(blocks) + 1):
+        if at + 1 < len(blocks):
+            scored.append(score(blocks[at + 1]))
+        if at < len(blocks):
+            soft.append(softmax(*scored[at]))
+        if at:
+            parts.append(products(blocks[at - 1], *soft[at - 1]))
 
     def whole(at, transposed):
         p = [[parts[2 * half + quad][at] for quad in range(2)] for half in range(halves)]
@@ -165,8 +178,8 @@
     return out_t, dfeat_t.astype(BF)
 
 
-def z_body(feat, cot, w_qkv, w_qkv_t, w_out, back, grad):
-    parts, terms = axis_math(z_line, feat[...], cot[...], w_qkv, w_qkv_t, w_out)
+def z_body(feat, cot, w_qkv, w_out, back, grad):
+    parts, terms = axis_math(z_line, feat[...], cot[...], w_qkv, w_out)
     eye = onehot(down(T), along(T))
     for at, part_t in enumerate(results(*parts, w_qkv)):
         back[:, at * C : (at + 1) * C] = nt(eye, part_t).astype(BF)
@@ -174,11 +187,11 @@
         grad[:, at * C : (at + 1) * C] = term.astype(BF)
 
 
-def lines_body(got, w_qkv, w_qkv_t, w_out, grad_z, out_t, dq_t, dk, dv, keep, give, total):
+def lines_body(got, w_qkv, w_out, grad_z, out_t, dq_t, dk, dv, keep, give, total):
     sort = onehot(place(down(2 * T)), along(2 * T))
     feat = nn(sort, jnp.concatenate([got[:, :C], got[:, 2 * C : 3 * C]], axis=0)).astype(BF)
     cot = nn(sort, jnp.concatenate([got[:, C : 2 * C], got[:, 3 * C :]], axis=0)).astype(BF)
-    held, terms = axis_math(long_line, feat, cot, w_qkv, w_qkv_t, w_out)
+    held, terms = axis_math(long_line, feat, cot, w_qkv, w_out)
     for ref, value in zip((out_t, dq_t, dk, dv), held):
         ref[...] = value
     for at, term in enumerate(terms):
@@ -266,8 +279,8 @@
 
 
 X, Y, ZS = range(4), range(8), range(8)
-LONG = [[device(x, 0, y, z) for z in ZS[dp::2] for y in Y] for x in X for dp in range(2)] + [
-    [device(x, 1, y, z) for z in ZS for x in X] for y in Y
+LONG = [[device(x, 0, y, z) for y in Y for z in ZS[dp::2]] for x in X for dp in range(2)] + [
+    [device(x, 1, y, z) for x in X for z in ZS] for y in Y
 ]
 SHORT = [
     [device(x, 0, y, 2 * z + dp) for x in X for dp in range(2)] for y in Y for z in range(4)
@@ -288,7 +301,7 @@
     local_shape = features.shape
     feat = features.reshape(T, C)
     cot = cotangent.reshape(T, C)
-    weights = (w_qkv, w_qkv.T, w_out)
+    weights = (w_qkv, w_out)
     cube = 2 * T * T * C
     pair = shape(T, 2 * C, BF)
     quad = shape(T, 4 * C, BF)

time: 110 us -> 108 us (0.982)
  starting transfers between devices: 23.6 us -> 26.8 us
  waiting for transfers between devices: 15.2 us -> 12.7 us
    ppermute x3, starting transfers between devices: 15.9 us -> 19.2 us  [swap(): return lax.ppermute(rows, 'row', [(i, i ^ 1) for i in range(8)])]
    all_to_all x1, waiting for transfers between devices: 12.1 us -> 9.59 us  [exchange(): lax.all_to_all(rows, AXES, split_axis=0, concat_axis=0, axis_index_groups...]
    unnamed x13 -> x12, local copies, waits for them, and re-layouts: 2.82 us -> 1.82 us
where the time goes in v14:
time: 108 us
  blocking collectives  56.8 us (53%)
  starting transfers between devices  26.8 us (25%)
  waiting for transfers between devices  12.7 us (12%)
  Pallas kernels  9.1 us (8%)
  local copies, waits for them, and re-layouts  1.82 us (2%)
    all_to_all x3, blocking collectives, exchange(): lax.all_to_all(rows, AXES, split_axis=0, concat_axis=0, axis_index_groups...  56.8 us
    ppermute x3, starting transfers between devices, swap(): return lax.ppermute(rows, 'row', [(i, i ^ 1) for i in range(8)])  19.2 us
    all_to_all x1, waiting for transfers between devices, exchange(): lax.all_to_all(rows, AXES, split_axis=0, concat_axis=0, axis_index_groups...  9.59 us
    pallas_call x11, Pallas kernels, call(): pl.pallas_call(body, out_shape=outs, in_specs=[pl.BlockSpec(memory_space=...  9.1 us
    all_to_all x1, starting transfers between devices, exchange(): lax.all_to_all(rows, AXES, split_axis=0, concat_axis=0, axis_index_groups...  7.66 us
    ppermute x3, waiting for transfers between devices, swap(): return lax.ppermute(rows, 'row', [(i, i ^ 1) for i in range(8)])  3.12 us
  transfers between devices with their start and end apart: 4, of which 4 were waited for; matrix products, arithmetic and copies ran while one was open for 0% of the time, Pallas kernels for 3%

profile of v14, /device:TPU:1, one launch (start us, length us, event | category | flops | bytes accessed | tf_op | source)
XLA Modules:
  0.0 108.0 jit_solution(13508894231955884995)
XLA Ops:
  0.6 0.0 copy-start.2
  0.6 0.9 copy-done.2
  1.5 0.0 copy-start.4
  1.5 0.9 copy-done.4
  2.4 0.2 shard_map.77
  2.7 8.8 %collective-permute-start = (bf16[256,512]{1,0:T(8,128)(2,1)S(1)}, bf16[256,512]{1,0:T(8,128)(2,1)S(1)}, u32[]{:S(2)}, u32[]{:S(2)}) collective-permute-start(bf16[256,512]{1,0:T(8,128)(2,1)S(1)} %shard_map.77), channel_id=1, source_target_pairs={{0,32},{32,0},{64,96},{96,64},{128,160},{160,128},{192,224},{224,1... | collective-permute-start | bytes 786440 | tf_op jit(solution)/shard_map/ppermute | solution.py:297
  11.5 0.2 shard_map.76.mine
  11.7 0.9 collective-permute-done.took
  12.6 0.8 shard_map.78
  13.4 0.0 copy-start
  13.4 0.0 copy-start.1
  13.5 0.0 copy-start.3
  13.5 0.0 copy-start.5
  13.5 7.7 %all-to-all-start = ((bf16[32,8,1024]{2,1,0:T(8,128)(2,1)}), bf16[32,8,1024]{2,1,0:T(8,128)(2,1)S(1)}, u32[]{:S(2)}, u32[]{:S(2)}) async-start(bf16[32,8,1024]{2,1,0:T(8,128)(2,1)} %bitcast.2), calls=%async_computation | async-start | bytes 1048576 | tf_op jit(solution)/shard_map/all_to_all | solution.py:291
  21.1 0.0 copy-done
  21.1 0.0 copy-done.1
  21.1 0.0 copy-done.3
  21.2 0.0 copy-done.5
  21.2 2.1 %shard_map.75 = (bf16[256,512]{1,0:T(8,128)(2,1)S(1)}, bf16[256,1024]{1,0:T(8,128)(2,1)S(1)}) custom-call(bf16[256,256]{1,0:T(8,128)(2,1)S(1)} %bitcast.24, bf16[256,256]{1,0:T(8,128)(2,1)S(1)} %bitcast.27, bf16[256,768]{1,0:T(8,128)(2,1)S(1)} %copy-done.1, bf16[256,256]{1,0:T(8,128)(2,1)S(1)} %copy-done), custom_call_target="tpu_custom_call" | custom-call | flops 2348810240 | bytes 1048576 | tf_op jit(solution)/shard_map/pallas_call | solution.py:259
  23.3 9.6 %all-to-all-done = bf16[32,8,1024]{2,1,0:T(8,128)(2,1)S(1)} async-done(((bf16[32,8,1024]{2,1,0:T(8,128)(2,1)}), bf16[32,8,1024]{2,1,0:T(8,128)(2,1)S(1)}, u32[]{:S(2)}, u32[]{:S(2)}) %all-to-all-start) | async-done | bytes 524320 | tf_op jit(solution)/shard_map/all_to_all | solution.py:291
  32.9 3.2 %shard_map.79 = (bf16[256,512]{1,0:T(8,128)(2,1)S(1)}, bf16[256,512]{1,0:T(8,128)(2,1)S(1)}, bf16[512,256]{1,0:T(8,128)(2,1)S(1)}, bf16[512,256]{1,0:T(8,128)(2,...) custom-call(bf16[256,1024]{1,0:T(8,128)(2,1)S(1)} %bitcast.18, bf16[256,768]{1,0:T(8,128)(2,1)S(1)} %copy-done.1, ...), custom_call_target="tpu_custom_call" | custom-call | flops 4697620480 | bytes 1048576 | tf_op jit(solution)/shard_map/pallas_call | solution.py:259
  36.2 8.5 %collective-permute-start.1 = (bf16[128,1024]{1,0:T(8,128)(2,1)S(1)}, bf16[128,1024]{1,0:T(8,128)(2,1)S(1)}, u32[]{:S(2)}, u32[]{:S(2)}) collective-permute-start(bf16[128,1024]{1,0:T(8,128)(2,1)S(1)} %get-tuple-element.26), channel_id=1, source_target_pairs={{0,32},{32,0},{64,96},{96,64},{128,160},{160,128},{192,224},{224,1... | collective-permute-start | bytes 786440 | tf_op jit(solution)/shard_map/ppermute | solution.py:297
  44.6 0.8 shard_map.80
  45.5 0.3 collective-permute-done.1.took
  45.8 0.1 shard_map.81
  45.9 24.3 %all_to_all.44 = bf16[32,8,1024]{2,1,0:T(8,128)(2,1)S(1)} all-to-all(bf16[32,8,1024]{2,1,0:T(8,128)(2,1)S(1)} %bitcast.17), channel_id=1, replica_groups={{0,1,2,3,4,5,6,7,8,9,10,11,12,13,14,15,16,17,18,19,20,21,22,23,24,25,26..., dimensions={0} | all-to-all | bytes 1048576 | tf_op jit(solution)/shard_map/all_to_all | solution.py:291
  70.2 11.0 %all_to_all.45 = bf16[8,8,512]{2,1,0:T(8,128)(2,1)S(1)} all-to-all(bf16[8,8,512]{2,1,0:T(8,128)(2,1)S(1)} %bitcast.21), channel_id=1, replica_groups={{0,256,64,320,128,384,192,448},{1,257,65,321,129,385,193,449},{2,258,66..., dimensions={0} | all-to-all | bytes 131072 | tf_op jit(solution)/shard_map/all_to_all | solution.py:291
  81.2 21.5 %all_to_all.46 = bf16[32,8,1024]{2,1,0:T(8,128)(2,1)S(1)} all-to-all(bf16[32,8,1024]{2,1,0:T(8,128)(2,1)S(1)} %bitcast.19), channel_id=1, replica_groups={{0,1,2,3,4,5,6,7,8,9,10,11,12,13,14,15,16,17,18,19,20,21,22,23,24,25,26..., dimensions={0} | all-to-all | bytes 1048576 | tf_op jit(solution)/shard_map/all_to_all | solution.py:291
  102.8 1.9 %collective-permute-start.2 = (bf16[256,1024]{1,0:T(8,128)(2,1)S(1)}, bf16[256,1024]{1,0:T(8,128)(2,1)S(1)}, u32[]{:S(2)}, u32[]{:S(2)}) collective-permute-start(bf16[256,1024]{1,0:T(8,128)(2,1)S(1)} %shard_map.84), channel_id=1, source_target_pairs={{0,32},{32,0},{64,96},{96,64},{128,160},{160,128},{192,224},{224,1... | collective-permute-start | bytes 1572872 | tf_op jit(solution)/shard_map/ppermute | solution.py:297
  104.7 1.9 %collective-permute-done.2.took = bf16[256,1024]{1,0:T(8,128)(2,1)S(1)} collective-permute-done((bf16[256,1024]{1,0:T(8,128)(2,1)S(1)}, bf16[256,1024]{1,0:T(8,128)(2,1)S(1)}, u32[]{:S(2)}, u32[]{:S(2)}) %collective-permute-start.2) | collective-permute-done | bytes 524320 | tf_op jit(solution)/shard_map/ppermute | solution.py:297
  106.6 1.4 %shard_map.85 = (bf16[256,256]{1,0:T(8,128)(2,1)}, bf16[256,256]{1,0:T(8,128)(2,1)}, f32[256,768]{1,0:T(8,128)}, f32[256,256]{1,0:T(8,128)}) custom-call(bf16[256,512]{1,0:T(8,128)(2,1)S(1)} %get-tuple-element.18.back_z, bf16[256,1024]{1,0:T(8,128)(2,1)S(1)} %bitcast.14, bf16[256,1024]{1,0:T(8,128)(2,1)S(1)} %bitcast.16, ...), custom_call_target="tpu_custom_call" | custom-call | flops 201326592 | bytes 1048576 | tf_op jit(solution)/shard_map/pallas_call | solution.py:259
  (3 shorter events, 0.1 us)
Async XLA Ops:
  0.6 0.9 copy-start.2
  1.5 0.9 copy-start.4
  2.7 9.9 %collective-permute-start = (bf16[256,512]{1,0:T(8,128)(2,1)S(1)}, bf16[256,512]{1,0:T(8,128)(2,1)S(1)}, u32[]{:S(2)}, u32[]{:S(2)}) collective-permute-start(bf16[256,512]{1,0:T(8,128)(2,1)S(1)} %shard_map.77), channel_id=1, source_target_pairs={{0,32},{32,0},{64,96},{96,64},{128,160},{160,128},{192,224},{224,1... | collective-permute-start | bytes 786440 | tf_op jit(solution)/shard_map/ppermute | solution.py:297
  13.4 7.7 %copy-start = (bf16[256,256]{1,0:T(8,128)(2,1)S(1)}, bf16[256,256]{1,0:T(8,128)(2,1)}, u32[]{:S(2)}) copy-start(bf16[256,256]{1,0:T(8,128)(2,1)} %w_out.5) | copy-start | bytes 393220
  13.4 7.7 %copy-start.1 = (bf16[256,768]{1,0:T(8,128)(2,1)S(1)}, bf16[256,768]{1,0:T(8,128)(2,1)}, u32[]{:S(2)}) copy-start(bf16[256,768]{1,0:T(8,128)(2,1)} %w_qkv.5) | copy-start | bytes 1179652
  13.5 7.7 %copy-start.3 = (bf16[1,2,8,16,256]{4,3,2,1,0:T(8,128)(2,1)S(1)}, bf16[1,2,8,16,256]{4,3,2,1,0:T(8,128)(2,1)}, u32[]{:S(2)}) copy-start(bf16[1,2,8,16,256]{4,3,2,1,0:T(8,128)(2,1)} %param.4) | copy-start | bytes 393220
  13.5 7.7 %copy-start.5 = (bf16[1,2,8,16,256]{4,3,2,1,0:T(8,128)(2,1)S(1)}, bf16[1,2,8,16,256]{4,3,2,1,0:T(8,128)(2,1)}, u32[]{:S(2)}) copy-start(bf16[1,2,8,16,256]{4,3,2,1,0:T(8,128)(2,1)} %param.7) | copy-start | bytes 393220
  13.5 19.4 %all-to-all-start = ((bf16[32,8,1024]{2,1,0:T(8,128)(2,1)}), bf16[32,8,1024]{2,1,0:T(8,128)(2,1)S(1)}, u32[]{:S(2)}, u32[]{:S(2)}) async-start(bf16[32,8,1024]{2,1,0:T(8,128)(2,1)} %bitcast.2), calls=%async_computation | async-start | bytes 1048576 | tf_op jit(solution)/shard_map/all_to_all | solution.py:291
  36.2 9.6 %collective-permute-start.1 = (bf16[128,1024]{1,0:T(8,128)(2,1)S(1)}, bf16[128,1024]{1,0:T(8,128)(2,1)S(1)}, u32[]{:S(2)}, u32[]{:S(2)}) collective-permute-start(bf16[128,1024]{1,0:T(8,128)(2,1)S(1)} %get-tuple-element.26), channel_id=1, source_target_pairs={{0,32},{32,0},{64,96},{96,64},{128,160},{160,128},{192,224},{224,1... | collective-permute-start | bytes 786440 | tf_op jit(solution)/shard_map/ppermute | solution.py:297
  102.8 3.8 %collective-permute-start.2 = (bf16[256,1024]{1,0:T(8,128)(2,1)S(1)}, bf16[256,1024]{1,0:T(8,128)(2,1)S(1)}, u32[]{:S(2)}, u32[]{:S(2)}) collective-permute-start(bf16[256,1024]{1,0:T(8,128)(2,1)S(1)} %shard_map.84), channel_id=1, source_target_pairs={{0,32},{32,0},{64,96},{96,64},{128,160},{160,128},{192,224},{224,1... | collective-permute-start | bytes 1572872 | tf_op jit(solution)/shard_map/ppermute | solution.py:297

commit v15 on v14

--- a/solution.py
+++ b/solution.py
@@ -234,20 +234,18 @@
     give[:, 2 * C :] = got_last[:, 2 * C :]
 
 
-def final_body(back_z, got_first, got_last, took, w_out, update, grad_in, grad_qkv, grad_out):
-    r = along(T)
-    put_mine = onehot(down(T), by_core(y_source(r), x_source(r)))
-    put_theirs = onehot(down(T), by_core(x_source(r), y_source(r)))
-    sums = []
-    for at, rows in enumerate((got_first[:, :C], got_last[:, :C])):
+def own_sum_body(back_z, got_first, got_last, part):
+    put = onehot(down(T), by_core(y_source(along(T)), x_source(along(T))))
+    for at, got in enumerate((got_first, got_last)):
         cols = slice(at * C, (at + 1) * C)
-        sums.append(
-            (
-                back_z[:, cols].astype(F32) + nn(put_mine, rows) + nn(put_theirs, took[:, cols])
-            ).astype(BF)
-        )
-    update[...] = nn(sums[0], w_out[...]).astype(BF)
-    grad_in[...] = sums[1]
+        part[:, cols] = back_z[:, cols].astype(F32) + nn(put, got[:, :C])
+
+
+def final_body(part, got_last, took, w_out, update, grad_in, grad_qkv, grad_out):
+    put = onehot(down(T), by_core(x_source(along(T)), y_source(along(T))))
+    sums = (part[...] + nn(put, took[:, : 2 * C])).astype(BF)
+    update[...] = nn(sums[:, :C], w_out[...]).astype(BF)
+    grad_in[...] = sums[:, C:]
     for src, half in ((got_last, core()), (took, 1 - core())):
         rows = pl.ds(pl.multiple_of(half * 128, 128), 128)
         grad_qkv[rows, : 2 * C] = src[:128, 2 * C :].astype(F32)
@@ -334,14 +332,17 @@
     (send,) = call(functools.partial(last_pack_body, factor), [quad], 2**20, blocks, back_feat)
     got_last = exchange(send, LONG)
     (give,) = call(give_body, [quad], 2**20, got_first, got_last)
+    took = swap(give)
+    (part,) = call(
+        own_sum_body, [shape(T, 2 * C, F32)], cube * 2, back_z, got_first, got_last
+    )
     update, grad_in, grad_qkv, grad_out = call(
         final_body,
         [shape(T, C, BF)] * 2 + [shape(C, 3 * C, F32), shape(C, C, F32)],
         cube * 6,
-        back_z,
-        got_first,
+        part,
         got_last,
-        swap(give),
+        took,
         w_out,
     )
     return (update.reshape(local_shape), grad_in.reshape(local_shape), grad_qkv, grad_out)

time: 108 us -> 108 us (level)
    pallas_call x11 -> x12, Pallas kernels: 9.1 us -> 9.24 us  [call(): pl.pallas_call(body, out_shape=outs, in_specs=[pl.BlockSpec(memory_space=...]
where the time goes in v15:
time: 108 us
  blocking collectives  56.8 us (53%)
  starting transfers between devices  26.8 us (25%)
  waiting for transfers between devices  12.5 us (12%)
  Pallas kernels  9.24 us (9%)
  local copies, waits for them, and re-layouts  1.82 us (2%)
    all_to_all x3, blocking collectives, exchange(): lax.all_to_all(rows, AXES, split_axis=0, concat_axis=0, axis_index_groups...  56.8 us
    ppermute x3, starting transfers between devices, swap(): return lax.ppermute(rows, 'row', [(i, i ^ 1) for i in range(8)])  19.2 us
    all_to_all x1, waiting for transfers between devices, exchange(): lax.all_to_all(rows, AXES, split_axis=0, concat_axis=0, axis_index_groups...  9.59 us
    pallas_call x12, Pallas kernels, call(): pl.pallas_call(body, out_shape=outs, in_specs=[pl.BlockSpec(memory_space=...  9.24 us
    all_to_all x1, starting transfers between devices, exchange(): lax.all_to_all(rows, AXES, split_axis=0, concat_axis=0, axis_index_groups...  7.66 us
    ppermute x3, waiting for transfers between devices, swap(): return lax.ppermute(rows, 'row', [(i, i ^ 1) for i in range(8)])  2.87 us
  transfers between devices with their start and end apart: 4, of which 4 were waited for; matrix products, arithmetic and copies ran while one was open for 0% of the time, Pallas kernels for 3%

profile of v15, /device:TPU:1, one launch (start us, length us, event | category | flops | bytes accessed | tf_op | source)
XLA Modules:
  0.0 107.9 jit_solution(830941363558559507)
XLA Ops:
  0.6 0.0 copy-start.2
  0.6 0.9 copy-done.2
  1.5 0.0 copy-start.4
  1.5 0.9 copy-done.4
  2.4 0.2 shard_map.77
  2.7 8.8 %collective-permute-start = (bf16[256,512]{1,0:T(8,128)(2,1)S(1)}, bf16[256,512]{1,0:T(8,128)(2,1)S(1)}, u32[]{:S(2)}, u32[]{:S(2)}) collective-permute-start(bf16[256,512]{1,0:T(8,128)(2,1)S(1)} %shard_map.77), channel_id=1, source_target_pairs={{0,32},{32,0},{64,96},{96,64},{128,160},{160,128},{192,224},{224,1... | collective-permute-start | bytes 786440 | tf_op jit(solution)/shard_map/ppermute | solution.py:295
  11.5 0.2 shard_map.76.mine
  11.7 0.9 collective-permute-done.took
  12.6 0.8 shard_map.78
  13.4 0.0 copy-start
  13.4 0.0 copy-start.1
  13.5 0.0 copy-start.3
  13.5 0.0 copy-start.5
  13.5 7.7 %all-to-all-start = ((bf16[32,8,1024]{2,1,0:T(8,128)(2,1)}), bf16[32,8,1024]{2,1,0:T(8,128)(2,1)S(1)}, u32[]{:S(2)}, u32[]{:S(2)}) async-start(bf16[32,8,1024]{2,1,0:T(8,128)(2,1)} %bitcast.2), calls=%async_computation | async-start | bytes 1048576 | tf_op jit(solution)/shard_map/all_to_all | solution.py:289
  21.1 0.0 copy-done
  21.1 0.0 copy-done.1
  21.1 0.0 copy-done.3
  21.2 0.0 copy-done.5
  21.2 2.1 %shard_map.75 = (bf16[256,512]{1,0:T(8,128)(2,1)S(1)}, bf16[256,1024]{1,0:T(8,128)(2,1)S(1)}) custom-call(bf16[256,256]{1,0:T(8,128)(2,1)S(1)} %bitcast.25, bf16[256,256]{1,0:T(8,128)(2,1)S(1)} %bitcast.28, bf16[256,768]{1,0:T(8,128)(2,1)S(1)} %copy-done.1, bf16[256,256]{1,0:T(8,128)(2,1)S(1)} %copy-done), custom_call_target="tpu_custom_call" | custom-call | flops 2348810240 | bytes 1048576 | tf_op jit(solution)/shard_map/pallas_call | solution.py:257
  23.3 9.6 %all-to-all-done = bf16[32,8,1024]{2,1,0:T(8,128)(2,1)S(1)} async-done(((bf16[32,8,1024]{2,1,0:T(8,128)(2,1)}), bf16[32,8,1024]{2,1,0:T(8,128)(2,1)S(1)}, u32[]{:S(2)}, u32[]{:S(2)}) %all-to-all-start) | async-done | bytes 524320 | tf_op jit(solution)/shard_map/all_to_all | solution.py:289
  32.9 3.2 %shard_map.79 = (bf16[256,512]{1,0:T(8,128)(2,1)S(1)}, bf16[256,512]{1,0:T(8,128)(2,1)S(1)}, bf16[512,256]{1,0:T(8,128)(2,1)S(1)}, bf16[512,256]{1,0:T(8,128)(2,...) custom-call(bf16[256,1024]{1,0:T(8,128)(2,1)S(1)} %bitcast.19, bf16[256,768]{1,0:T(8,128)(2,1)S(1)} %copy-done.1, ...), custom_call_target="tpu_custom_call" | custom-call | flops 4697620480 | bytes 1048576 | tf_op jit(solution)/shard_map/pallas_call | solution.py:257
  36.2 8.5 %collective-permute-start.1 = (bf16[128,1024]{1,0:T(8,128)(2,1)S(1)}, bf16[128,1024]{1,0:T(8,128)(2,1)S(1)}, u32[]{:S(2)}, u32[]{:S(2)}) collective-permute-start(bf16[128,1024]{1,0:T(8,128)(2,1)S(1)} %get-tuple-element.26), channel_id=1, source_target_pairs={{0,32},{32,0},{64,96},{96,64},{128,160},{160,128},{192,224},{224,1... | collective-permute-start | bytes 786440 | tf_op jit(solution)/shard_map/ppermute | solution.py:295
  44.6 0.8 shard_map.80
  45.5 0.3 collective-permute-done.1.took
  45.8 0.1 shard_map.81
  45.9 24.3 %all_to_all.44 = bf16[32,8,1024]{2,1,0:T(8,128)(2,1)S(1)} all-to-all(bf16[32,8,1024]{2,1,0:T(8,128)(2,1)S(1)} %bitcast.18), channel_id=1, replica_groups={{0,1,2,3,4,5,6,7,8,9,10,11,12,13,14,15,16,17,18,19,20,21,22,23,24,25,26..., dimensions={0} | all-to-all | bytes 1048576 | tf_op jit(solution)/shard_map/all_to_all | solution.py:289
  70.2 11.0 %all_to_all.45 = bf16[8,8,512]{2,1,0:T(8,128)(2,1)S(1)} all-to-all(bf16[8,8,512]{2,1,0:T(8,128)(2,1)S(1)} %bitcast.22), channel_id=1, replica_groups={{0,256,64,320,128,384,192,448},{1,257,65,321,129,385,193,449},{2,258,66..., dimensions={0} | all-to-all | bytes 131072 | tf_op jit(solution)/shard_map/all_to_all | solution.py:289
  81.2 21.5 %all_to_all.46 = bf16[32,8,1024]{2,1,0:T(8,128)(2,1)S(1)} all-to-all(bf16[32,8,1024]{2,1,0:T(8,128)(2,1)S(1)} %bitcast.20), channel_id=1, replica_groups={{0,1,2,3,4,5,6,7,8,9,10,11,12,13,14,15,16,17,18,19,20,21,22,23,24,25,26..., dimensions={0} | all-to-all | bytes 1048576 | tf_op jit(solution)/shard_map/all_to_all | solution.py:289
  102.8 1.9 %collective-permute-start.2 = (bf16[256,1024]{1,0:T(8,128)(2,1)S(1)}, bf16[256,1024]{1,0:T(8,128)(2,1)S(1)}, u32[]{:S(2)}, u32[]{:S(2)}) collective-permute-start(bf16[256,1024]{1,0:T(8,128)(2,1)S(1)} %shard_map.85), channel_id=1, source_target_pairs={{0,32},{32,0},{64,96},{96,64},{128,160},{160,128},{192,224},{224,1... | collective-permute-start | bytes 1572872 | tf_op jit(solution)/shard_map/ppermute | solution.py:295
  104.7 0.2 shard_map.84.part
  104.9 1.6 %collective-permute-done.2.took = bf16[256,1024]{1,0:T(8,128)(2,1)S(1)} collective-permute-done((bf16[256,1024]{1,0:T(8,128)(2,1)S(1)}, bf16[256,1024]{1,0:T(8,128)(2,1)S(1)}, u32[]{:S(2)}, u32[]{:S(2)}) %collective-permute-start.2) | collective-permute-done | bytes 524320 | tf_op jit(solution)/shard_map/ppermute | solution.py:295
  106.6 1.3 %shard_map.86 = (bf16[256,256]{1,0:T(8,128)(2,1)}, bf16[256,256]{1,0:T(8,128)(2,1)}, f32[256,768]{1,0:T(8,128)}, f32[256,256]{1,0:T(8,128)}) custom-call(f32[256,512]{1,0:T(8,128)S(1)} %shard_map.84.part, bf16[256,1024]{1,0:T(8,128)(2,1)S(1)} %bitcast.14, bf16[256,1024]{1,0:T(8,128)(2,1)S(1)} %collective-permute-done.2.took, bf16[256,256]{1,0:T(8,128)(2,1)S(1)} %copy-done), custom_call_target="tpu_custom_call" | custom-call | flops 201326592 | bytes 1048576 | tf_op jit(solution)/shard_map/pallas_call | solution.py:257
  (3 shorter events, 0.1 us)
Async XLA Ops:
  0.6 0.9 copy-start.2
  1.5 0.9 copy-start.4
  2.7 9.9 %collective-permute-start = (bf16[256,512]{1,0:T(8,128)(2,1)S(1)}, bf16[256,512]{1,0:T(8,128)(2,1)S(1)}, u32[]{:S(2)}, u32[]{:S(2)}) collective-permute-start(bf16[256,512]{1,0:T(8,128)(2,1)S(1)} %shard_map.77), channel_id=1, source_target_pairs={{0,32},{32,0},{64,96},{96,64},{128,160},{160,128},{192,224},{224,1... | collective-permute-start | bytes 786440 | tf_op jit(solution)/shard_map/ppermute | solution.py:295
  13.4 7.7 %copy-start = (bf16[256,256]{1,0:T(8,128)(2,1)S(1)}, bf16[256,256]{1,0:T(8,128)(2,1)}, u32[]{:S(2)}) copy-start(bf16[256,256]{1,0:T(8,128)(2,1)} %w_out.5) | copy-start | bytes 393220
  13.4 7.7 %copy-start.1 = (bf16[256,768]{1,0:T(8,128)(2,1)S(1)}, bf16[256,768]{1,0:T(8,128)(2,1)}, u32[]{:S(2)}) copy-start(bf16[256,768]{1,0:T(8,128)(2,1)} %w_qkv.5) | copy-start | bytes 1179652
  13.5 7.7 %copy-start.3 = (bf16[1,2,8,16,256]{4,3,2,1,0:T(8,128)(2,1)S(1)}, bf16[1,2,8,16,256]{4,3,2,1,0:T(8,128)(2,1)}, u32[]{:S(2)}) copy-start(bf16[1,2,8,16,256]{4,3,2,1,0:T(8,128)(2,1)} %param.4) | copy-start | bytes 393220
  13.5 7.7 %copy-start.5 = (bf16[1,2,8,16,256]{4,3,2,1,0:T(8,128)(2,1)S(1)}, bf16[1,2,8,16,256]{4,3,2,1,0:T(8,128)(2,1)}, u32[]{:S(2)}) copy-start(bf16[1,2,8,16,256]{4,3,2,1,0:T(8,128)(2,1)} %param.7) | copy-start | bytes 393220
  13.5 19.4 %all-to-all-start = ((bf16[32,8,1024]{2,1,0:T(8,128)(2,1)}), bf16[32,8,1024]{2,1,0:T(8,128)(2,1)S(1)}, u32[]{:S(2)}, u32[]{:S(2)}) async-start(bf16[32,8,1024]{2,1,0:T(8,128)(2,1)} %bitcast.2), calls=%async_computation | async-start | bytes 1048576 | tf_op jit(solution)/shard_map/all_to_all | solution.py:289
  36.2 9.6 %collective-permute-start.1 = (bf16[128,1024]{1,0:T(8,128)(2,1)S(1)}, bf16[128,1024]{1,0:T(8,128)(2,1)S(1)}, u32[]{:S(2)}, u32[]{:S(2)}) collective-permute-start(bf16[128,1024]{1,0:T(8,128)(2,1)S(1)} %get-tuple-element.26), channel_id=1, source_target_pairs={{0,32},{32,0},{64,96},{96,64},{128,160},{160,128},{192,224},{224,1... | collective-permute-start | bytes 786440 | tf_op jit(solution)/shard_map/ppermute | solution.py:295
  102.8 3.8 %collective-permute-start.2 = (bf16[256,1024]{1,0:T(8,128)(2,1)S(1)}, bf16[256,1024]{1,0:T(8,128)(2,1)S(1)}, u32[]{:S(2)}, u32[]{:S(2)}) collective-permute-start(bf16[256,1024]{1,0:T(8,128)(2,1)S(1)} %shard_map.85), channel_id=1, source_target_pairs={{0,32},{32,0},{64,96},{96,64},{128,160},{160,128},{192,224},{224,1... | collective-permute-start | bytes 1572872 | tf_op jit(solution)/shard_map/ppermute | solution.py:295
